TPU v7x, 256 devices: a whole 4x4x8 slice. The times are simulated.
256 devices in a mesh: px: 4 (over x), py: 2 (over y_hi), fr: 32 (over z, y_lo, core).
Axes of the slice: x: 4, y: 4 (y_hi: 2, y_lo: 2; y = y_hi * 2 + y_lo), z: 8, core: 2. Of those that a mesh axis runs over, the one named last changes fastest.
Arguments:
- water_voxel: int32 [128, 8, 4, 128], P('fr', 'px', 'py'), may hold values from 0 to 23039, as said below
- water_offset: float32 [128, 8, 4, 3, 128], P('fr', 'px', 'py'), may hold values from -0.25 to 0.25
- water_angles: float32 [128, 8, 4, 3, 128], P('fr', 'px', 'py'), may hold values from -3.140625 to 3.140625
- water_count: int32 [128, 8, 4], P('fr', 'px', 'py'), may hold values from 16 to 128, as said below
- solute_frac: float32 [8, 4, 3, 128], P('px', 'py'), may hold values from 0 to 1
- solute_type: int32 [8, 4, 128], P('px', 'py'), may hold values from 0 to 31
- type_sigma: float32 [32], replicated, may hold values from 2.4 to 3.9
- type_well: float32 [32], replicated, may hold values from 0.02 to 0.3
- type_charge: float32 [32], replicated, may hold values from -1 to 1
Outputs:
- gist_grid: float32 [13, 8, 4, 23040], P(None, 'px', 'py', 'fr')
Inputs may be any that keep to these rules, and one draw needn't show every extreme that they name: `water_count`: at most 128 waters in a cell; some cell holds 128 in every frame; the slots below the count hold waters. `water_voxel`: in each frame and cell, each of the 32 aligned ranges of 720 voxels holds exactly 4 of the slots; some slot lies at voxel 0 and some at voxel 23040 - 1.
All inputs are finite; a program needn't handle non-finite values.
Results may differ from a plain program's by a relative error of at most 0.0003.
Values sent between devices are 32-bit elements; how exact they have to be, the bound alone decides.
No kernel may reach another device: no remote copies, remote signals or barrier semaphores. Data moves between devices by JAX's collectives and lax.ppermute only.
A program may use at most 64 MiB of HBM per device.

v0:
```python
import jax
import jax.numpy as jnp
from jax import lax
from jax.sharding import PartitionSpec as P

CELL_XY = 24
SLAB = 40


spacing = 0.5
soft_sq = 9.0
sigma_water = 3.1507
eps_water = 0.1521
k_dipole = 79.4
k_charge = 162.3
rho_bulk = 0.0334
pair_index = ((0, 0), (0, 1), (0, 2), (0, 3), (1, 1), (1, 2), (1, 3), (2, 2), (2, 3), (3, 3))


def with_halo(block, sides, width):
    for axis, dim in sides:
        count = lax.axis_size(axis)
        forward = [(i, i + 1) for i in range(count - 1)]
        backward = [(target, source) for source, target in forward]
        low = lax.ppermute(
            lax.slice_in_dim(block, block.shape[dim] - width, None, axis=dim), axis, forward
        )
        high = lax.ppermute(lax.slice_in_dim(block, 0, width, axis=dim), axis, backward)
        block = jnp.concatenate([low, block, high], axis=dim)
    return block


def water_parts(voxel_id, offset, angles, counts):
    plane_size = CELL_XY * SLAB
    cell_x = voxel_id // plane_size
    cell_y = voxel_id // SLAB % CELL_XY
    cell_z = voxel_id % SLAB
    lattice = jnp.stack([cell_x, cell_y, cell_z], axis=-2).astype(offset.dtype)
    position = spacing * (lattice + 0.5) + offset
    half_b = 0.5 * angles[..., 1, :]
    plus_half = 0.5 * (angles[..., 0, :] + angles[..., 2, :])
    minus_half = 0.5 * (angles[..., 0, :] - angles[..., 2, :])
    quat_w = jnp.cos(half_b) * jnp.cos(plus_half)
    quat_x = -jnp.sin(half_b) * jnp.sin(minus_half)
    quat_y = jnp.sin(half_b) * jnp.cos(minus_half)
    quat_z = jnp.cos(half_b) * jnp.sin(plus_half)
    dipole = jnp.stack(
        [
            2.0 * (quat_x * quat_z + quat_w * quat_y),
            2.0 * (quat_y * quat_z - quat_w * quat_x),
            1.0 - 2.0 * (quat_x * quat_x + quat_y * quat_y),
        ],
        axis=-2,
    )
    slot_count = voxel_id.shape[-1]
    filled = (jnp.arange(slot_count, dtype=jnp.int32) < counts[..., None]).astype(offset.dtype)
    features = jnp.concatenate([position, dipole, filled[..., None, :]], axis=-2)
    quaternion = jnp.stack([quat_w, quat_x, quat_y, quat_z], axis=-2)
    return (features, quaternion)


def solute_features(solute_frac, sigma_atom, root_atom, charge_atom):
    cell_box = jnp.array(
        [spacing * CELL_XY, spacing * CELL_XY, spacing * SLAB], dtype=solute_frac.dtype
    )[:, None]
    place = solute_frac * cell_box
    return jnp.concatenate(
        [place, jnp.stack([sigma_atom, root_atom, charge_atom], axis=-2)], axis=-2
    )


def energies(own, water_pad, solute_pad):
    cells_x, cells_y, slot_count = (own.shape[0], own.shape[1], own.shape[3])
    cutoff = spacing * CELL_XY
    position = own[:, :, 0:3]
    filled = own[:, :, 6]
    dipole_own = own[:, :, 3:6, :, None]
    not_self = 1.0 - jnp.eye(slot_count, dtype=own.dtype)
    water_water = jnp.zeros((cells_x, cells_y, slot_count), own.dtype)
    solute_water = jnp.zeros((cells_x, cells_y, slot_count), own.dtype)
    for step_x in (-1, 0, 1):
        for step_y in (-1, 0, 1):
            shift_vec = jnp.array([step_x * cutoff, step_y * cutoff, 0.0], dtype=own.dtype)[
                :, None, None
            ]
            others = water_pad[1 + step_x : 1 + step_x + cells_x, 1 + step_y : 1 + step_y + cells_y]
            separation = others[:, :, 0:3, None, :] + shift_vec - position[:, :, :, :, None]
            dist_sq = jnp.sum(separation * separation, axis=2)
            inverse = 1.0 / (dist_sq + soft_sq)
            switch = jnp.square(jnp.maximum(0.0, 1.0 - dist_sq / (cutoff * cutoff)))
            ratio_cube = (sigma_water * sigma_water * inverse) ** 3
            lj_term = 4.0 * eps_water * (ratio_cube * ratio_cube - ratio_cube)
            dipole_other = others[:, :, 3:6, None, :]
            aligned = jnp.sum(dipole_own * dipole_other, axis=2)
            along_own = jnp.sum(dipole_own * separation, axis=2)
            along_other = jnp.sum(dipole_other * separation, axis=2)
            dipolar = (
                k_dipole
                * (aligned - 3.0 * along_own * along_other * inverse)
                * inverse
                * jnp.sqrt(inverse)
            )
            pair_energy = (
                (lj_term + dipolar) * switch * filled[:, :, :, None] * others[:, :, 6, None, :]
            )
            if step_x == 0 and step_y == 0:
                pair_energy = pair_energy * not_self
            water_water = water_water + 0.5 * jnp.sum(pair_energy, axis=3)
            solute_atoms = solute_pad[
                1 + step_x : 1 + step_x + cells_x, 1 + step_y : 1 + step_y + cells_y
            ]
            away = position[:, :, :, :, None] - solute_atoms[:, :, 0:3, None, :] - shift_vec
            dist_solute = jnp.sum(away * away, axis=2)
            inverse_solute = 1.0 / (dist_solute + soft_sq)
            switch_solute = jnp.square(jnp.maximum(0.0, 1.0 - dist_solute / (cutoff * cutoff)))
            sigma_mix = 0.5 * (sigma_water + solute_atoms[:, :, 3, None, :])
            ratio_solute = (sigma_mix * sigma_mix * inverse_solute) ** 3
            lj_solute = (
                4.0
                * jnp.sqrt(eps_water)
                * solute_atoms[:, :, 4, None, :]
                * (ratio_solute * ratio_solute - ratio_solute)
            )
            charge_term = (
                -k_charge
                * solute_atoms[:, :, 5, None, :]
                * jnp.sum(dipole_own * away, axis=2)
                * inverse_solute
                * jnp.sqrt(inverse_solute)
            )
            solute_water = (
                solute_water + jnp.sum((lj_solute + charge_term) * switch_solute, axis=3) * filled
            )
    return (water_water, solute_water)


def records(features, quaternion, water_water, solute_water):
    filled = features[..., 6, :]
    moments = [
        quaternion[..., first_comp, :] * quaternion[..., second_comp, :] * filled
        for first_comp, second_comp in pair_index
    ]
    return jnp.stack([filled, solute_water, water_water] + moments, axis=-2)


def finish(totals, frame_total):
    counted = totals[0]
    density = counted / (frame_total * rho_bulk * spacing**3)
    scaled = totals[1:] / jnp.maximum(counted, 1.0)
    return jnp.concatenate([density[None], scaled], axis=0)


def frame_record(features, padded, quaternion, voxel_id, solute_pad):
    water_water, solute_water = energies(features, padded, solute_pad)
    record = records(features, quaternion, water_water, solute_water)
    return jnp.concatenate([record, voxel_id[:, :, None, :].astype(record.dtype)], axis=2)


def bin_range(running, pieces_in, row_count, cells_x, cells_y):
    cell_total = cells_x * cells_y
    local = pieces_in[:, :, :, 13, :].astype(jnp.int32)
    inside = (local >= 0) & (local < row_count)
    row_index = jnp.where(inside, local, row_count)[:, :, :, None, :]
    values = pieces_in[:, :, :, 0:13, :]
    cell_number = jnp.arange(cell_total, dtype=jnp.int32).reshape(1, cells_x, cells_y, 1, 1)
    column = jnp.arange(13, dtype=jnp.int32).reshape(1, 1, 1, 13, 1) * cell_total + cell_number
    row_full = jnp.broadcast_to(row_index, values.shape).reshape(-1)
    column_full = jnp.broadcast_to(column, values.shape).reshape(-1)
    return running.at[row_full, column_full].add(values.reshape(-1), mode="drop")


def shards(
    water_voxel,
    water_offset,
    water_angles,
    water_count,
    solute_frac,
    solute_type,
    type_sigma,
    type_well,
    type_charge,
):
    type_total = type_sigma.shape[0]
    type_table = jnp.stack([type_sigma, jnp.sqrt(type_well), type_charge], axis=0)
    one_hot = (solute_type[..., None] == jnp.arange(type_total, dtype=jnp.int32)).astype(
        jnp.float32
    )
    looked = jnp.einsum("xyat,pt->pxya", one_hot, type_table, precision=lax.Precision.HIGHEST)
    solute = solute_features(solute_frac, looked[0], looked[1], looked[2])
    solute_pad = with_halo(solute, (("px", 0), ("py", 1)), 1)
    frames_dev, cells_x, cells_y, slot_count = water_voxel.shape
    features, quaternion = water_parts(water_voxel, water_offset, water_angles, water_count)

    def framed(inputs):
        padded = with_halo(inputs[1], (("px", 0), ("py", 1)), 1)
        return frame_record(inputs[0], padded, inputs[2], inputs[3], solute_pad)

    stacked = lax.map(framed, (features, features, quaternion, water_voxel))
    cell_vox = CELL_XY * CELL_XY * SLAB
    own_rows = cell_vox // lax.axis_size("fr")
    empty_rows = jnp.zeros((own_rows * lax.axis_size("fr"), 13 * cells_x * cells_y), jnp.float32)
    totals = lax.psum_scatter(
        bin_range(empty_rows, stacked, own_rows * lax.axis_size("fr"), cells_x, cells_y),
        "fr",
        scatter_dimension=0,
        tiled=True,
    )
    share_total = totals.shape[0]
    voxel_grid = jnp.transpose(totals.reshape(share_total, 13, cells_x, cells_y), (1, 2, 3, 0))
    return finish(voxel_grid, frames_dev * lax.axis_size("fr"))


def solution(mesh):
    placed = (
        P("fr", "px", "py", None),
        P("fr", "px", "py", None, None),
        P("fr", "px", "py", None, None),
        P("fr", "px", "py"),
        P("px", "py", None, None),
        P("px", "py", None),
        P(),
        P(),
        P(),
    )
    return jax.shard_map(
        shards, mesh=mesh, in_specs=placed, out_specs=P(None, "px", "py", "fr"), check_vma=False
    )
```

profile of v0, /device:TPU:1, one launch (start us, length us, event | category | flops | bytes accessed | tf_op | source)
XLA Modules:
  0.0 476.9 jit_solution(16517538467684141002)
XLA Ops:
  8.9 3.9 collective-permute-start.4
  12.8 1.3 collective-permute-start.5
  17.7 4.8 %collective-permute-start.6 = (f32[4,1,6,128]{3,2,1,0:T(8,128)S(1)}, f32[4,1,6,128]{3,2,1,0:T(8,128)S(1)}, u32[]{:S(2)}, u32[]{:S(2)}) collective-permute-start(f32[4,1,6,128]{3,2,1,0:T(8,128)S(1)} %get-tuple-element.396), channel_id=1, source_target_pairs={{0,32},{1,33},{2,34},{3,35},{4,36},{5,37},{6,38},{7,39},{8,40},{9,... | collective-permute-start | bytes 36872 | tf_op jit(solution)/shard_map/ppermute | solution.py:25
  22.6 1.3 collective-permute-start.7
  24.1 4.4 collective-permute-done.7
  28.6 127.3 %while.11 = (s32[]{:T(128)}, f32[4,2,2,14,128]{4,2,1,3,0:T(2,128)S(1)}, f32[4,2,2,7,128]{4,2,3,1,0:T(2,128)S(1)}, f32[4,4,6,128]{3,1,0,2:T(4,128)S(1)}, f32[4,2,...) while((s32[]{:T(128)}, ...), condition=%wide.region_73.74_spmd.clone, body=%wide.region_0.73_spmd.sunk.clone.sunk | while | flops 47825920 | bytes 30223068 | solution.py:198
  29.9 4.6 collective-permute-start.1
  35.4 1.7 collective-permute-start.2
  39.2 3.9 collective-permute-done.3
  45.4 3.2 fusion.168
  50.7 5.5 %fusion.173 = (f32[2,2,128,128]{3,2,1,0:T(8,128)S(1)}, f32[2,2,128,128]{3,2,1,0:T(8,128)S(1)}, f32[2,2,128,128]{3,2,1,0:T(8,128)S(1)}, f32[2,2,128,128]{3,2,1,0:...) fusion(f32[2,2,3,128]{3,2,1,0:T(4,128)S(1)} %copy.256, ...), kind=kLoop, calls=%fused_computation.37.clone.1 | loop fusion | flops 13631488 | bytes 9285644 | tf_op jit(solution)/shard_map/while/body/eval_jaxpr/reduce_sum | solution.py:96
  62.1 4.2 collective-permute-start.1
  67.1 1.7 collective-permute-start.2
  68.8 1.3 collective-permute-start.3
  70.9 3.9 collective-permute-done.3
  77.1 3.2 fusion.168
  82.4 5.5 %fusion.173 = (f32[2,2,128,128]{3,2,1,0:T(8,128)S(1)}, f32[2,2,128,128]{3,2,1,0:T(8,128)S(1)}, f32[2,2,128,128]{3,2,1,0:T(8,128)S(1)}, f32[2,2,128,128]{3,2,1,0:...) fusion(f32[2,2,3,128]{3,2,1,0:T(4,128)S(1)} %copy.256, ...), kind=kLoop, calls=%fused_computation.37.clone.1 | loop fusion | flops 13631488 | bytes 9285644 | tf_op jit(solution)/shard_map/while/body/eval_jaxpr/reduce_sum | solution.py:96
  92.5 1.3 collective-permute-start
  93.8 4.2 collective-permute-start.1
  98.9 1.7 collective-permute-start.2
  102.6 3.9 collective-permute-done.3
  108.9 3.2 fusion.168
  114.1 5.5 %fusion.173 = (f32[2,2,128,128]{3,2,1,0:T(8,128)S(1)}, f32[2,2,128,128]{3,2,1,0:T(8,128)S(1)}, f32[2,2,128,128]{3,2,1,0:T(8,128)S(1)}, f32[2,2,128,128]{3,2,1,0:...) fusion(f32[2,2,3,128]{3,2,1,0:T(4,128)S(1)} %copy.256, ...), kind=kLoop, calls=%fused_computation.37.clone.1 | loop fusion | flops 13631488 | bytes 9285644 | tf_op jit(solution)/shard_map/while/body/eval_jaxpr/reduce_sum | solution.py:96
  125.5 4.2 collective-permute-start.1
  130.6 1.7 collective-permute-start.2
  134.4 3.9 collective-permute-done.3
  140.6 3.2 fusion.168
  145.9 5.5 %fusion.173 = (f32[2,2,128,128]{3,2,1,0:T(8,128)S(1)}, f32[2,2,128,128]{3,2,1,0:T(8,128)S(1)}, f32[2,2,128,128]{3,2,1,0:T(8,128)S(1)}, f32[2,2,128,128]{3,2,1,0:...) fusion(f32[2,2,3,128]{3,2,1,0:T(4,128)S(1)} %copy.256, ...), kind=kLoop, calls=%fused_computation.37.clone.1 | loop fusion | flops 13631488 | bytes 9285644 | tf_op jit(solution)/shard_map/while/body/eval_jaxpr/reduce_sum | solution.py:96
  157.3 141.6 %scatter_custom_fusion = f32[1198080]{0:T(1024)} fusion(s32[26624]{0:T(1024)S(1)} %broadcast_select_fusion, f32[26624]{0:T(1024)S(1)} %reshape.316, f32[]{:T(128)} %constant.145.clone), kind=kCustom, calls=%fused_computation.304 | custom fusion | flops 26624 | bytes 4792324
  298.9 6.0 %reshape.304 = f32[52,23040]{1,0:T(8,128)} reshape(f32[1198080]{0:T(1024)} %scatter_custom_fusion) | data formatting | bytes 9584640
  304.9 9.1 %copy.158 = f32[23040,52]{1,0:T(8,128)} copy(f32[23040,52]{0,1:T(8,128)} %bitcast.161) | data formatting | bytes 9584640
  314.0 153.9 %reduce-scatter.4.cloned.1.call-done = f32[720,52]{1,0:T(8,128)} async-done(((f32[23040,52]{1,0:T(8,128)}), f32[720,52]{1,0:T(8,128)}) %reduce-scatter.4.cloned.1.call-update) | async-done | bytes 149776
  (359 shorter events, 58.3 us)
Async XLA Ops:
  6.5 461.4 %reduce-scatter.4.cloned.1.call-start = ((), (), s32[]{:S(2)}) async-start(), calls=%async_computation.1 | async-start | bytes 12165120
  8.9 8.8 %collective-permute-start.4 = (f32[1,2,6,128]{3,2,1,0:T(8,128)S(1)}, f32[1,2,6,128]{3,2,1,0:T(8,128)S(1)}, u32[]{:S(2)}, u32[]{:S(2)}) collective-permute-start(f32[1,2,6,128]{3,2,1,0:T(8,128)S(1)} %get-tuple-element.401), channel_id=1, source_target_pairs={{0,64},{64,128},{128,192},{1,65},{65,129},{129,193},{2,66},{66,130... | collective-permute-start | bytes 18440 | tf_op jit(solution)/shard_map/ppermute | solution.py:25
  12.8 4.9 %collective-permute-start.5 = (f32[1,2,6,128]{3,2,1,0:T(8,128)S(1)}, f32[1,2,6,128]{3,2,1,0:T(8,128)S(1)}, u32[]{:S(2)}, u32[]{:S(2)}) collective-permute-start(f32[1,2,6,128]{3,2,1,0:T(8,128)S(1)} %get-tuple-element.402), channel_id=1, source_target_pairs={{64,0},{128,64},{192,128},{65,1},{129,65},{193,129},{66,2},{130,66... | collective-permute-start | bytes 18440 | tf_op jit(solution)/shard_map/ppermute | solution.py:28
  17.7 6.4 %collective-permute-start.6 = (f32[4,1,6,128]{3,2,1,0:T(8,128)S(1)}, f32[4,1,6,128]{3,2,1,0:T(8,128)S(1)}, u32[]{:S(2)}, u32[]{:S(2)}) collective-permute-start(f32[4,1,6,128]{3,2,1,0:T(8,128)S(1)} %get-tuple-element.396), channel_id=1, source_target_pairs={{0,32},{1,33},{2,34},{3,35},{4,36},{5,37},{6,38},{7,39},{8,40},{9,... | collective-permute-start | bytes 36872 | tf_op jit(solution)/shard_map/ppermute | solution.py:25
  22.6 6.0 %collective-permute-start.7 = (f32[4,1,6,128]{3,2,1,0:T(8,128)S(1)}, f32[4,1,6,128]{3,2,1,0:T(8,128)S(1)}, u32[]{:S(2)}, u32[]{:S(2)}) collective-permute-start(f32[4,1,6,128]{3,2,1,0:T(8,128)S(1)} %get-tuple-element.397), channel_id=1, source_target_pairs={{32,0},{33,1},{34,2},{35,3},{36,4},{37,5},{38,6},{39,7},{40,8},{41... | collective-permute-start | bytes 36872 | tf_op jit(solution)/shard_map/ppermute | solution.py:28
  28.6 127.8 %copy-start.2 = (s32[2]{0:T(128)S(1)}, s32[2]{0:T(128)}, u32[]{:S(2)}) copy-start(s32[2]{0:T(128)} %constant.159) | copy-start | bytes 28
  28.6 128.3 %copy-start.1 = (s32[2]{0:T(128)S(1)}, s32[2]{0:T(128)}, u32[]{:S(2)}) copy-start(s32[2]{0:T(128)} %constant.156) | copy-start | bytes 28
  28.6 6.2 %collective-permute-start = (f32[1,2,7,128]{3,1,0,2:T(2,128)S(1)}, f32[1,2,7,128]{3,1,0,2:T(2,128)S(1)}, u32[]{:S(2)}, u32[]{:S(2)}) collective-permute-start(f32[1,2,7,128]{3,1,0,2:T(2,128)S(1)} %get-tuple-element.610), channel_id=1, source_target_pairs={{64,0},{128,64},{192,128},{65,1},{129,65},{193,129},{66,2},{130,66... | collective-permute-start | bytes 21512 | tf_op jit(solution)/shard_map/while/body/eval_jaxpr/ppermute | solution.py:28
  29.9 5.4 %collective-permute-start.1 = (f32[1,2,7,128]{3,1,2,0:T(2,128)S(1)}, f32[1,2,7,128]{3,1,2,0:T(2,128)S(1)}, u32[]{:S(2)}, u32[]{:S(2)}) collective-permute-start(f32[1,2,7,128]{3,1,2,0:T(2,128)S(1)} %get-tuple-element.611), channel_id=1, source_target_pairs={{0,64},{64,128},{128,192},{1,65},{65,129},{129,193},{2,66},{66,130... | collective-permute-start | bytes 21512 | tf_op jit(solution)/shard_map/while/body/eval_jaxpr/ppermute | solution.py:25
  35.4 15.3 %copy-start = (f32[3]{0:T(128)S(1)}, f32[3]{0:T(128)}, u32[]{:S(2)}) copy-start(f32[3]{0:T(128)} %get-tuple-element.828) | copy-start | bytes 40 | tf_op jit(solution)/shard_map/while
  35.4 3.7 collective-permute-start.2
  37.1 6.0 %collective-permute-start.3 = (f32[4,1,7,128]{3,1,0,2:T(1,128)S(1)}, f32[4,1,7,128]{3,1,0,2:T(1,128)S(1)}, u32[]{:S(2)}, u32[]{:S(2)}) collective-permute-start(f32[4,1,7,128]{3,1,0,2:T(1,128)S(1)} %get-tuple-element.614), channel_id=1, source_target_pairs={{32,0},{33,1},{34,2},{35,3},{36,4},{37,5},{38,6},{39,7},{40,8},{41... | collective-permute-start | bytes 43016 | tf_op jit(solution)/shard_map/while/body/eval_jaxpr/ppermute | solution.py:28
  60.8 5.8 %collective-permute-start = (f32[1,2,7,128]{3,1,0,2:T(2,128)S(1)}, f32[1,2,7,128]{3,1,0,2:T(2,128)S(1)}, u32[]{:S(2)}, u32[]{:S(2)}) collective-permute-start(f32[1,2,7,128]{3,1,0,2:T(2,128)S(1)} %get-tuple-element.610), channel_id=1, source_target_pairs={{64,0},{128,64},{192,128},{65,1},{129,65},{193,129},{66,2},{130,66... | collective-permute-start | bytes 21512 | tf_op jit(solution)/shard_map/while/body/eval_jaxpr/ppermute | solution.py:28
  62.1 5.0 %collective-permute-start.1 = (f32[1,2,7,128]{3,1,2,0:T(2,128)S(1)}, f32[1,2,7,128]{3,1,2,0:T(2,128)S(1)}, u32[]{:S(2)}, u32[]{:S(2)}) collective-permute-start(f32[1,2,7,128]{3,1,2,0:T(2,128)S(1)} %get-tuple-element.611), channel_id=1, source_target_pairs={{0,64},{64,128},{128,192},{1,65},{65,129},{129,193},{2,66},{66,130... | collective-permute-start | bytes 21512 | tf_op jit(solution)/shard_map/while/body/eval_jaxpr/ppermute | solution.py:25
  67.1 15.3 %copy-start = (f32[3]{0:T(128)S(1)}, f32[3]{0:T(128)}, u32[]{:S(2)}) copy-start(f32[3]{0:T(128)} %get-tuple-element.828) | copy-start | bytes 40 | tf_op jit(solution)/shard_map/while
  67.1 3.7 collective-permute-start.2
  68.8 6.0 %collective-permute-start.3 = (f32[4,1,7,128]{3,1,0,2:T(1,128)S(1)}, f32[4,1,7,128]{3,1,0,2:T(1,128)S(1)}, u32[]{:S(2)}, u32[]{:S(2)}) collective-permute-start(f32[4,1,7,128]{3,1,0,2:T(1,128)S(1)} %get-tuple-element.614), channel_id=1, source_target_pairs={{32,0},{33,1},{34,2},{35,3},{36,4},{37,5},{38,6},{39,7},{40,8},{41... | collective-permute-start | bytes 43016 | tf_op jit(solution)/shard_map/while/body/eval_jaxpr/ppermute | solution.py:28
  92.5 5.8 %collective-permute-start = (f32[1,2,7,128]{3,1,0,2:T(2,128)S(1)}, f32[1,2,7,128]{3,1,0,2:T(2,128)S(1)}, u32[]{:S(2)}, u32[]{:S(2)}) collective-permute-start(f32[1,2,7,128]{3,1,0,2:T(2,128)S(1)} %get-tuple-element.610), channel_id=1, source_target_pairs={{64,0},{128,64},{192,128},{65,1},{129,65},{193,129},{66,2},{130,66... | collective-permute-start | bytes 21512 | tf_op jit(solution)/shard_map/while/body/eval_jaxpr/ppermute | solution.py:28
  93.8 5.0 %collective-permute-start.1 = (f32[1,2,7,128]{3,1,2,0:T(2,128)S(1)}, f32[1,2,7,128]{3,1,2,0:T(2,128)S(1)}, u32[]{:S(2)}, u32[]{:S(2)}) collective-permute-start(f32[1,2,7,128]{3,1,2,0:T(2,128)S(1)} %get-tuple-element.611), channel_id=1, source_target_pairs={{0,64},{64,128},{128,192},{1,65},{65,129},{129,193},{2,66},{66,130... | collective-permute-start | bytes 21512 | tf_op jit(solution)/shard_map/while/body/eval_jaxpr/ppermute | solution.py:25
  98.8 15.3 %copy-start = (f32[3]{0:T(128)S(1)}, f32[3]{0:T(128)}, u32[]{:S(2)}) copy-start(f32[3]{0:T(128)} %get-tuple-element.828) | copy-start | bytes 40 | tf_op jit(solution)/shard_map/while
  98.9 3.7 collective-permute-start.2
  100.5 6.0 %collective-permute-start.3 = (f32[4,1,7,128]{3,1,0,2:T(1,128)S(1)}, f32[4,1,7,128]{3,1,0,2:T(1,128)S(1)}, u32[]{:S(2)}, u32[]{:S(2)}) collective-permute-start(f32[4,1,7,128]{3,1,0,2:T(1,128)S(1)} %get-tuple-element.614), channel_id=1, source_target_pairs={{32,0},{33,1},{34,2},{35,3},{36,4},{37,5},{38,6},{39,7},{40,8},{41... | collective-permute-start | bytes 43016 | tf_op jit(solution)/shard_map/while/body/eval_jaxpr/ppermute | solution.py:28
  124.2 5.8 %collective-permute-start = (f32[1,2,7,128]{3,1,0,2:T(2,128)S(1)}, f32[1,2,7,128]{3,1,0,2:T(2,128)S(1)}, u32[]{:S(2)}, u32[]{:S(2)}) collective-permute-start(f32[1,2,7,128]{3,1,0,2:T(2,128)S(1)} %get-tuple-element.610), channel_id=1, source_target_pairs={{64,0},{128,64},{192,128},{65,1},{129,65},{193,129},{66,2},{130,66... | collective-permute-start | bytes 21512 | tf_op jit(solution)/shard_map/while/body/eval_jaxpr/ppermute | solution.py:28
  125.5 5.0 %collective-permute-start.1 = (f32[1,2,7,128]{3,1,2,0:T(2,128)S(1)}, f32[1,2,7,128]{3,1,2,0:T(2,128)S(1)}, u32[]{:S(2)}, u32[]{:S(2)}) collective-permute-start(f32[1,2,7,128]{3,1,2,0:T(2,128)S(1)} %get-tuple-element.611), channel_id=1, source_target_pairs={{0,64},{64,128},{128,192},{1,65},{65,129},{129,193},{2,66},{66,130... | collective-permute-start | bytes 21512 | tf_op jit(solution)/shard_map/while/body/eval_jaxpr/ppermute | solution.py:25
  130.6 15.3 %copy-start = (f32[3]{0:T(128)S(1)}, f32[3]{0:T(128)}, u32[]{:S(2)}) copy-start(f32[3]{0:T(128)} %get-tuple-element.828) | copy-start | bytes 40 | tf_op jit(solution)/shard_map/while
  130.6 3.7 collective-permute-start.2
  132.3 6.0 %collective-permute-start.3 = (f32[4,1,7,128]{3,1,0,2:T(1,128)S(1)}, f32[4,1,7,128]{3,1,0,2:T(1,128)S(1)}, u32[]{:S(2)}, u32[]{:S(2)}) collective-permute-start(f32[4,1,7,128]{3,1,0,2:T(1,128)S(1)} %get-tuple-element.614), channel_id=1, source_target_pairs={{32,0},{33,1},{34,2},{35,3},{36,4},{37,5},{38,6},{39,7},{40,8},{41... | collective-permute-start | bytes 43016 | tf_op jit(solution)/shard_map/while/body/eval_jaxpr/ppermute | solution.py:28
Sparse Core Ops, SparseCore 0:
  314.2 153.7 reduce-scatter.3
where the time goes:
time: 480 us; the launch traced here: 477 us
  other arithmetic  220 us (46%)
  waiting for transfers between devices  176 us (37%)
  starting transfers between devices  45.6 us (10%)
  local copies, waits for them, and re-layouts  19.7 us (4%)
  between operations  13.7 us (3%)
    unnamed x2, waiting for transfers between devices  154 us
    unnamed x5, other arithmetic  143 us
    reduce_sum x8, other arithmetic, energies(): along_other = jnp.sum(dipole_other * separation, axis=2)  34.9 us
    ppermute x10, starting transfers between devices, with_halo(): lax.ppermute(lax.slice_in_dim(block, block.shape[dim] - width, None, axis...  32.7 us
    ppermute x10, waiting for transfers between devices, with_halo(): lax.ppermute(lax.slice_in_dim(block, 0, width, axis=dim), axis, backward)  19.9 us
    unnamed x13, local copies, waits for them, and re-layouts  17.1 us
    ppermute x10, starting transfers between devices, with_halo(): lax.ppermute(lax.slice_in_dim(block, 0, width, axis=dim), axis, backward)  12.9 us
    reduce_sum x12, other arithmetic, energies(): water_water = water_water + 0.5 * jnp.sum(pair_energy, axis=3)  11.9 us
  transfers between devices with their start and end apart: 21, of which 10 were waited for; matrix products, arithmetic and copies ran while one was open for 2% of the time, Pallas kernels for 0%

commit v1 on v0

v1 whole, which is shorter than its diff:
```python
import functools

import jax
import jax.numpy as jnp
from jax import lax
from jax.experimental import pallas as pl
from jax.experimental.pallas import tpu as pltpu
from jax.sharding import PartitionSpec as P

CELL_XY = 24
SLAB = 40
F32 = jnp.float32
BF16 = jnp.bfloat16

spacing = 0.5
soft_sq = 9.0
sigma_water = 3.1507
eps_water = 0.1521
k_dipole = 79.4
k_charge = 162.3
rho_bulk = 0.0334
pair_index = ((0, 0), (0, 1), (0, 2), (0, 3), (1, 1), (1, 2), (1, 3), (2, 2), (2, 3), (3, 3))

CUTOFF = spacing * CELL_XY
UNIT = 1.0 / sigma_water
P_SOFT = soft_sq * UNIT * UNIT
P_CUT = CUTOFF * CUTOFF * UNIT * UNIT
P_END = P_SOFT + P_CUT
KD = k_dipole / (4.0 * eps_water * sigma_water**3)
KQ = k_charge * UNIT * UNIT
SCALE_WW = 0.5 * 4.0 * eps_water / (P_CUT * P_CUT)
SCALE_SW = 1.0 / (P_CUT * P_CUT)
FAR = 1.0e4
ROWS = 64


def split3(value):
    first = value.astype(BF16).astype(F32)
    rest = value - first
    second = rest.astype(BF16).astype(F32)
    return first, second, (rest - second).astype(BF16).astype(F32)


def rows_of(parts, fill=0.0):
    lanes = parts[0].shape[1]
    missing = 8 - len(parts)
    if missing:
        parts = list(parts) + [jnp.full((missing, lanes), fill, F32)]
    return jnp.concatenate(parts, axis=0)


def sincos(angle):
    turns = jnp.floor(angle * 0.6366197723675814 + 0.5)
    rest = angle - turns * 1.5703125 - turns * 4.838267948966e-4
    square = rest * rest
    sine = rest + rest * square * (
        -1.6666654611e-1 + square * (8.3321608736e-3 - square * 1.9515295891e-4)
    )
    cosine = (
        1.0
        - 0.5 * square
        + square
        * square
        * (4.166664568298827e-2 + square * (-1.388731625493765e-3 + square * 2.443315711809948e-5))
    )
    quarter = turns.astype(jnp.int32) & 3
    odd = (quarter & 1) == 1
    sin_out = jnp.where(odd, cosine, sine)
    cos_out = jnp.where(odd, sine, cosine)
    sin_out = jnp.where(quarter >= 2, -sin_out, sin_out)
    cos_out = jnp.where((quarter == 1) | (quarter == 2), -cos_out, cos_out)
    return sin_out, cos_out


def prepare_kernel(
    place_ref, count_ref, sigma_ref, well_ref, charge_ref,
    voxel_ref, offset_ref, angle_ref, frac_ref, type_ref,
    feat_ref, side_ref, comp_ref,
    raw_ref, key_ref, sorted_ref,
):
    frames = voxel_ref.shape[0]
    lane = lax.broadcasted_iota(jnp.int32, (1, 128), 1)
    for i in range(2):
        for j in range(2):
            for f in range(frames):
                fc = (i * 2 + j) * frames + f
                voxel = voxel_ref[f, i, j : j + 1, :]
                raw_ref[fc, 0:1, :] = voxel.astype(F32)
                raw_ref[fc, 1:4, :] = offset_ref[f, i, j]
                raw_ref[fc, 4:7, :] = angle_ref[f, i, j]
                raw_ref[fc, 7:8, :] = jnp.where(lane < count_ref[f, i, j], 1.0, 0.0).astype(F32)
                key_ref[fc : fc + 1, :] = (voxel * 128 + lane).astype(F32)
    total = 4 * frames
    keys = key_ref[...]
    keys_t = keys.T
    rank_iota = lax.broadcasted_iota(jnp.int32, (128, 128), 0).astype(F32)
    for fc in range(total):
        before = jnp.where(keys_t[:, fc : fc + 1] < keys[fc : fc + 1, :], 1.0, 0.0)
        rank = jnp.sum(before, axis=0, keepdims=True)
        chosen = jnp.where(rank_iota == rank, 1.0, 0.0).astype(BF16)
        parts = jnp.concatenate(split3(raw_ref[fc]), axis=0).astype(BF16)
        moved = lax.dot_general(
            parts, chosen, (((1,), (1,)), ((), ())), preferred_element_type=F32
        )
        sorted_ref[:, fc, :] = moved[0:8] + moved[8:16] + moved[16:24]

    voxel = sorted_ref[0]
    cell_x = jnp.floor((voxel + 0.5) * (1.0 / (CELL_XY * SLAB)))
    in_plane = voxel - cell_x * (CELL_XY * SLAB)
    cell_y = jnp.floor((in_plane + 0.5) * (1.0 / SLAB))
    cell_z = in_plane - cell_y * SLAB
    row = lax.broadcasted_iota(jnp.int32, (total, 128), 0)
    own_x = (row // (2 * frames)).astype(F32)
    own_y = ((row // frames) % 2).astype(F32)
    x = (spacing * (cell_x + 0.5) + sorted_ref[1] + CUTOFF * (own_x - 1.0)) * UNIT
    y = (spacing * (cell_y + 0.5) + sorted_ref[2] + CUTOFF * (own_y - 1.0)) * UNIT
    z = (spacing * (cell_z + 0.5) + sorted_ref[3] - 0.5 * spacing * SLAB) * UNIT
    sin_b, cos_b = sincos(0.5 * sorted_ref[5])
    sin_p, cos_p = sincos(0.5 * (sorted_ref[4] + sorted_ref[6]))
    sin_m, cos_m = sincos(0.5 * (sorted_ref[4] - sorted_ref[6]))
    quat_w = cos_b * cos_p
    quat_x = -sin_b * sin_m
    quat_y = sin_b * cos_m
    quat_z = cos_b * sin_p
    features = (
        x, y, z,
        2.0 * (quat_x * quat_z + quat_w * quat_y),
        2.0 * (quat_y * quat_z - quat_w * quat_x),
        1.0 - 2.0 * (quat_x * quat_x + quat_y * quat_y),
        sorted_ref[7],
    )
    for number, value in enumerate(features):
        for cell in range(4):
            feat_ref[cell, 0:frames, number, :] = value[cell * frames : (cell + 1) * frames]
    share = CELL_XY * CELL_XY * SLAB // 32
    band = (lax.broadcasted_iota(jnp.int32, (total, 128), 1) // 4 * share).astype(F32)
    for number, value in enumerate((quat_w, quat_x, quat_y, quat_z, sorted_ref[7], voxel - band)):
        comp_ref[number] = value

    for i in range(2):
        for j in range(2):
            kind = type_ref[i, j : j + 1, :]
            sigma = jnp.zeros((1, 128), F32)
            well = jnp.zeros((1, 128), F32)
            charge = jnp.zeros((1, 128), F32)
            for t in range(sigma_ref.shape[0]):
                same = kind == t
                sigma = jnp.where(same, sigma_ref[t], sigma)
                well = jnp.where(same, well_ref[t], well)
                charge = jnp.where(same, charge_ref[t], charge)
            ratio = 0.5 * (1.0 + sigma * UNIT)
            cube = ratio * ratio * ratio
            sixth = cube * cube
            lower = (4.0 * eps_water**0.5) * jnp.sqrt(well) * sixth
            frac = frac_ref[i, j]
            atom_x = (frac[0:1] * CUTOFF + CUTOFF * (i - 1.0)) * UNIT
            atom_y = (frac[1:2] * CUTOFF + CUTOFF * (j - 1.0)) * UNIT
            atom_z = (frac[2:3] * (spacing * SLAB) - 0.5 * spacing * SLAB) * UNIT
            feat_ref[i * 2 + j, frames] = rows_of(
                [atom_x, atom_y, atom_z, lower, lower * sixth, charge, jnp.ones((1, 128), F32)]
            )
    for cell in range(4):
        for f in range(frames):
            feat_ref[cell, f, 7:8, :] = jnp.zeros((1, 128), F32)
    facing = 1 - place_ref[1]
    for i in range(2):
        side_ref[i] = feat_ref[i * 2 + facing]


def partner_rows(base):
    first, second, third = split3(base)
    number = lax.broadcasted_iota(jnp.int32, (8, 128), 0)
    ones = jnp.where(number < 3, 1.0, 0.0).astype(F32)
    stacked = jnp.concatenate(
        [first, first, first, second, second, third, ones, jnp.zeros((8, 128), F32)], axis=0
    )
    return stacked.T.astype(BF16)


def water_partner(value, shift, absent):
    x, y, z = value[0:1] + shift[0], value[1:2] + shift[1], value[2:3]
    mx, my, mz = value[3:4], value[4:5], value[5:6]
    n = x * x + y * y + z * z + FAR * ((1.0 - value[6:7]) + absent)
    e = mx * x + my * y + mz * z
    return partner_rows(jnp.concatenate([x, y, z, mx, my, mz, n, e], axis=0))


def solute_partner(value, shift, absent):
    x, y, z, charge = value[0:1] + shift[0], value[1:2] + shift[1], value[2:3], value[5:6]
    n = x * x + y * y + z * z + FAR * ((1.0 - value[6:7]) + absent)
    base = jnp.concatenate([x, y, z, charge * x, charge * y, charge * z, n, charge], axis=0)
    lower = jnp.broadcast_to(value[3:4], (128, 128)).T
    upper = jnp.broadcast_to(value[4:5], (128, 128)).T
    return partner_rows(base), lower, upper


def own_side(value):
    x, y, z = value[0:1], value[1:2], value[2:3]
    mx, my, mz = value[3:4], value[4:5], value[5:6]
    zero = jnp.zeros((1, 128), F32)
    one = jnp.ones((1, 128), F32)
    n = x * x + y * y + z * z + P_SOFT
    c = mx * x + my * y + mz * z
    kd3 = 3.0 * KD
    sides = (
        ([-2.0 * x, -2.0 * y, -2.0 * z, zero, zero, zero, one, zero], n),
        ([zero, zero, zero, KD * mx, KD * my, KD * mz, zero, zero], None),
        ([mx, my, mz, zero, zero, zero, zero, zero], -c),
        ([zero, zero, zero, -kd3 * x, -kd3 * y, -kd3 * z, zero, kd3 * one], None),
        ([zero, zero, zero, KQ * mx, KQ * my, KQ * mz, zero, -KQ * c], None),
    )
    out = []
    for rows, term in sides:
        first, second, third = split3(jnp.concatenate(rows, axis=0))
        if term is None:
            last = jnp.zeros((16, 128), F32)
        else:
            last = jnp.concatenate(list(split3(term)) + [jnp.zeros((13, 128), F32)], axis=0)
        out.append(
            jnp.concatenate([first, second, third, first, second, first, last], axis=0).astype(BF16)
        )
    return out


def fold(acc, value):
    for k in range(value.shape[0] // 8):
        acc = acc + value[8 * k : 8 * k + 8]
    return acc


CHUNK = 16


def water_pairs(acc, p, al, ao, ab):
    for k in range(p.shape[0] // CHUNK):
        part = slice(k * CHUNK, (k + 1) * CHUNK)
        pk = p[part]
        root = lax.rsqrt(pk)
        u = root * root
        u15 = u * root
        window = jnp.maximum(P_END - pk, 0.0)
        inner = u15 * (u15 * u15 - 1.0) + (al[part] - ao[part] * ab[part] * u)
        acc = fold(acc, u15 * inner * (window * window))
    return acc


def solute_pairs(acc, p, charge, lower, upper):
    for k in range(p.shape[0] // CHUNK):
        part = slice(k * CHUNK, (k + 1) * CHUNK)
        pk = p[part]
        root = lax.rsqrt(pk)
        u15 = root * root * root
        window = jnp.maximum(P_END - pk, 0.0)
        low = jnp.concatenate([lower[part]] * 2, axis=1)
        high = jnp.concatenate([upper[part]] * 2, axis=1)
        inner = u15 * (high * (u15 * u15) - low) + charge[part]
        acc = fold(acc, u15 * inner * (window * window))
    return acc


def dot(left, right):
    return jnp.dot(left, right, preferred_element_type=F32)


def inner_kernel(feat_ref, comp_ref, acc_ref, rec_ref, left_ref, own_ref, coef_ref):
    frames = feat_ref.shape[1] - 1
    for cell in range(4):
        rows, lower, upper = solute_partner(feat_ref[cell, frames], (0.0, 0.0), 0.0)
        left_ref[frames, cell] = rows
        coef_ref[cell, 0] = lower
        coef_ref[cell, 1] = upper
        for f in range(frames):
            left_ref[f, cell] = water_partner(feat_ref[cell, f], (0.0, 0.0), 0.0)
            for q, side in enumerate(own_side(feat_ref[cell, f])):
                own_ref[f, q, cell] = side

    @pl.loop(0, frames)
    def _(f):
        for i in range(2):
            sides = [
                jnp.concatenate([own_ref[f, q, 2 * i], own_ref[f, q, 2 * i + 1]], axis=1)
                for q in range(5)
            ]
            acc_w = jnp.zeros((8, 256), F32)
            acc_s = jnp.zeros((8, 256), F32)
            for cell in range(4):
                left = left_ref[f, cell]
                acc_w = water_pairs(acc_w, *[dot(left, sides[q]) for q in range(4)])
                left = left_ref[frames, cell]
                acc_s = solute_pairs(
                    acc_s, dot(left, sides[0]), dot(left, sides[4]), coef_ref[cell, 0], coef_ref[cell, 1]
                )
            acc_ref[f, i, 0] = acc_w
            acc_ref[f, i, 1] = acc_s

    filled = comp_ref[4]
    rows = {0: filled, 13: comp_ref[5]}
    for number, (a, b) in enumerate(pair_index):
        rows[3 + number] = comp_ref[a] * comp_ref[b] * filled
    rec_ref[...] = jnp.zeros_like(rec_ref)
    for number, value in rows.items():
        rec_ref[:, number, :] = value


def outer_kernel(
    place_ref, feat_ref, side_ref, low_ref, high_ref, first_ref, rec_in_ref, send_ref,
    left_ref, own_ref, coef_ref, acc_ref, rec_ref,
):
    frames = feat_ref.shape[1] - 1
    px = place_ref[0]
    py = place_ref[1]
    last = place_ref[2]
    facing = 1 - py
    width = 2.0 * CUTOFF * UNIT
    to_side = jnp.where(py == 0, width, -width).astype(F32)
    no_low = jnp.where(px == 0, 1.0, 0.0).astype(F32)
    no_high = jnp.where(px == last, 1.0, 0.0).astype(F32)
    halo = (
        [(low_ref, k, (-width, to_side if k == 2 else 0.0), no_low) for k in range(3)]
        + [(high_ref, k, (width, to_side if k == 2 else 0.0), no_high) for k in range(3)]
        + [(side_ref, k, (0.0, to_side), 0.0) for k in range(2)]
    )
    for cell, (ref, k, shift, absent) in enumerate(halo):
        rows, lower, upper = solute_partner(ref[k, frames], shift, absent)
        left_ref[frames, cell] = rows
        coef_ref[cell, 0] = lower
        coef_ref[cell, 1] = upper
        for f in range(frames):
            left_ref[f, cell] = water_partner(ref[k, f], shift, absent)
    for cell in range(4):
        for f in range(frames):
            for q, side in enumerate(own_side(feat_ref[cell, f])):
                own_ref[f, q, cell] = side
    acc_ref[...] = first_ref[...]

    @pl.loop(0, frames)
    def _(f):
        def unit(sides, cell, acc_w, acc_s):
            left = left_ref[f, cell]
            acc_w = water_pairs(acc_w, *[dot(left, sides[q]) for q in range(4)])
            left = left_ref[frames, cell]
            acc_s = solute_pairs(
                acc_s, dot(left, sides[0]), dot(left, sides[4]), coef_ref[cell, 0], coef_ref[cell, 1]
            )
            return acc_w, acc_s

        for i in range(2):
            sides = [
                jnp.concatenate([own_ref[f, q, 2 * i], own_ref[f, q, 2 * i + 1]], axis=1)
                for q in range(5)
            ]
            acc_w = acc_ref[f, i, 0]
            acc_s = acc_ref[f, i, 1]
            for k in range(2):
                acc_w, acc_s = unit(sides, 3 * i + k, acc_w, acc_s)
            acc_ref[f, i, 0] = acc_w
            acc_ref[f, i, 1] = acc_s
        sides = [
            jnp.concatenate([own_ref[f, q, facing], own_ref[f, q, 2 + facing]], axis=1)
            for q in range(5)
        ]
        acc_w = jnp.zeros((8, 256), F32)
        acc_s = jnp.zeros((8, 256), F32)
        for k in range(2):
            acc_w, acc_s = unit(sides, 6 + k, acc_w, acc_s)

        def both(source, q):
            return jnp.concatenate(
                [
                    dot(left_ref[source, 2], own_ref[f, q, facing]),
                    dot(left_ref[source, 5], own_ref[f, q, 2 + facing]),
                ],
                axis=1,
            )

        acc_w = water_pairs(acc_w, *[both(f, q) for q in range(4)])
        p = both(frames, 0)
        charge = both(frames, 4)
        for k in range(128 // CHUNK):
            part = slice(k * CHUNK, (k + 1) * CHUNK)
            pk = p[part]
            root = lax.rsqrt(pk)
            u15 = root * root * root
            window = jnp.maximum(P_END - pk, 0.0)
            low = jnp.concatenate([coef_ref[2, 0, part], coef_ref[5, 0, part]], axis=1)
            high = jnp.concatenate([coef_ref[2, 1, part], coef_ref[5, 1, part]], axis=1)
            inner = u15 * (high * (u15 * u15) - low) + charge[part]
            acc_s = fold(acc_s, u15 * inner * (window * window))
        upper_row = (facing == 1).astype(F32)
        for i in range(2):
            for number, acc in ((0, acc_w), (1, acc_s)):
                mine = acc[:, i * 128 : (i + 1) * 128]
                acc_ref[f, i, number] += jnp.concatenate(
                    [mine * (1.0 - upper_row), mine * upper_row], axis=1
                )

    rec_ref[...] = rec_in_ref[...]
    self_root = P_SOFT**-0.5
    self_u15 = self_root**3
    for i in range(2):
        for f in range(frames):
            water = jnp.sum(acc_ref[f, i, 0], axis=0, keepdims=True)
            solute = jnp.sum(acc_ref[f, i, 1], axis=0, keepdims=True)
            for j in range(2):
                value = feat_ref[2 * i + j, f]
                filled = value[6:7]
                moment = value[3:4] * value[3:4] + value[4:5] * value[4:5] + value[5:6] * value[5:6]
                own = (self_u15 * P_CUT * P_CUT) * (
                    self_u15 * (self_u15 * self_u15 - 1.0) + KD * moment
                )
                fc = (2 * i + j) * frames + f
                part = slice(j * 128, (j + 1) * 128)
                rec_ref[fc, 1:2, :] = filled * (SCALE_SW * solute[:, part])
                rec_ref[fc, 2:3, :] = filled * (SCALE_WW * (water[:, part] - own))
    for i in range(2):
        block = rec_ref[8 * i : 8 * i + 8].reshape(128, 128).T
        send_ref[:, 4 * i : 4 * i + 4, :] = block.reshape(32, 4, 128)


def bin_kernel(frame_total, got_ref, out_ref):
    share = out_ref.shape[-1]
    number = lax.broadcasted_iota(jnp.int32, (share, 128), 0).astype(F32)
    for i in range(2):
        block = got_ref[:, 4 * i : 4 * i + 4, :].reshape(128, 128).T
        for j in range(2):
            totals = jnp.zeros((48, share), F32)
            for f in range(4):
                start = (j * 4 + f) * 16
                record = block[start : start + 16]
                chosen = jnp.where(number == record[13:14], 1.0, 0.0).astype(BF16)
                parts = jnp.concatenate(split3(record), axis=0).astype(BF16)
                totals = totals + lax.dot_general(
                    parts, chosen, (((1,), (1,)), ((), ())), preferred_element_type=F32
                )
            summed = totals[0:16] + totals[16:32] + totals[32:48]
            counted = summed[0:1]
            out_ref[0:1, i, j, :] = counted * (1.0 / (frame_total * rho_bulk * spacing**3))
            out_ref[1:13, i, j, :] = summed[1:13] / jnp.maximum(counted, 1.0)


def vmem():
    return pl.BlockSpec(memory_space=pltpu.VMEM)


def smem():
    return pl.BlockSpec(memory_space=pltpu.SMEM)


PARAMS = pltpu.CompilerParams(vmem_limit_bytes=48 * 1024 * 1024)


def shards(
    water_voxel, water_offset, water_angles, water_count,
    solute_frac, solute_type, type_sigma, type_well, type_charge,
):
    frames = water_voxel.shape[0]
    cols = lax.axis_size("px")
    ranks = lax.axis_size("fr")
    place = jnp.stack(
        [lax.axis_index("px"), lax.axis_index("py"), jnp.int32(cols - 1)]
    ).astype(jnp.int32)
    total = 4 * frames
    feat, side_out, comp = pl.pallas_call(
        prepare_kernel,
        out_shape=(
            jax.ShapeDtypeStruct((4, frames + 1, 8, 128), F32),
            jax.ShapeDtypeStruct((2, frames + 1, 8, 128), F32),
            jax.ShapeDtypeStruct((6, total, 128), F32),
        ),
        in_specs=[smem()] * 5 + [vmem()] * 5,
        out_specs=(vmem(),) * 3,
        scratch_shapes=[
            pltpu.VMEM((total, 8, 128), F32),
            pltpu.VMEM((total, 128), F32),
            pltpu.VMEM((8, total, 128), F32),
        ],
        compiler_params=PARAMS,
        name="prepare",
    )(place, water_count, type_sigma, type_well, type_charge,
      water_voxel, water_offset, water_angles, solute_frac, solute_type)

    side = lax.ppermute(side_out, "py", [(0, 1), (1, 0)])
    up = [(k, (k + 1) % cols) for k in range(cols)]
    down = [(k, (k - 1) % cols) for k in range(cols)]
    low = lax.ppermute(jnp.concatenate([feat[2:4], side[1:2]], axis=0), "px", up)
    high = lax.ppermute(jnp.concatenate([feat[0:2], side[0:1]], axis=0), "px", down)

    acc, rec = pl.pallas_call(
        inner_kernel,
        out_shape=(
            jax.ShapeDtypeStruct((frames, 2, 2, 8, 256), F32),
            jax.ShapeDtypeStruct((total, 16, 128), F32),
        ),
        in_specs=[vmem()] * 2,
        out_specs=(vmem(),) * 2,
        scratch_shapes=[
            pltpu.VMEM((frames + 1, 4, 128, ROWS), BF16),
            pltpu.VMEM((frames, 5, 4, ROWS, 128), BF16),
            pltpu.VMEM((4, 2, 128, 128), F32),
        ],
        compiler_params=PARAMS,
        cost_estimate=pl.CostEstimate(flops=10**9, bytes_accessed=10**6, transcendentals=0),
        name="inner",
    )(feat, comp)

    send = pl.pallas_call(
        outer_kernel,
        out_shape=jax.ShapeDtypeStruct((ranks, 8, 128), F32),
        in_specs=[smem()] + [vmem()] * 6,
        out_specs=vmem(),
        scratch_shapes=[
            pltpu.VMEM((frames + 1, 8, 128, ROWS), BF16),
            pltpu.VMEM((frames, 5, 4, ROWS, 128), BF16),
            pltpu.VMEM((8, 2, 128, 128), F32),
            pltpu.VMEM((frames, 2, 2, 8, 256), F32),
            pltpu.VMEM((total, 16, 128), F32),
        ],
        compiler_params=PARAMS,
        name="outer",
    )(place, feat, side, low, high, acc, rec)

    got = lax.all_to_all(send, "fr", 0, 0, tiled=True)
    share = CELL_XY * CELL_XY * SLAB // ranks
    return pl.pallas_call(
        functools.partial(bin_kernel, frames * ranks),
        out_shape=jax.ShapeDtypeStruct((13, 2, 2, share), F32),
        in_specs=[vmem()],
        out_specs=vmem(),
        compiler_params=PARAMS,
        name="bin",
    )(got)


def solution(mesh):
    placed = (
        P("fr", "px", "py", None),
        P("fr", "px", "py", None, None),
        P("fr", "px", "py", None, None),
        P("fr", "px", "py"),
        P("px", "py", None, None),
        P("px", "py", None),
        P(),
        P(),
        P(),
    )
    return jax.shard_map(
        shards, mesh=mesh, in_specs=placed, out_specs=P(None, "px", "py", "fr"), check_vma=False
    )
```

time: 480 us -> 47.5 us (0.10)
  other arithmetic: 220 us -> 0.09 us
  waiting for transfers between devices: 176 us -> 1.39 us
  starting transfers between devices: 45.6 us -> 6.58 us
  blocking collectives: 0 us -> 21.1 us
  local copies, waits for them, and re-layouts: 19.7 us -> 2.82 us
  Pallas kernels: 0 us -> 15 us
  between operations: 13.7 us -> 0.09 us
    unnamed x2 -> x0, waiting for transfers between devices: 154 us -> none
    unnamed x5 -> x0, other arithmetic: 143 us -> none
    reduce_sum x56 -> x0, other arithmetic: 57.4 us -> none  [the longest x8 34.9 us: energies(): along_other = jnp.sum(dipole_other * separation, axis=2)]
    ppermute x20 -> x3, starting transfers between devices: 45.6 us -> 6.58 us  [the longest x1 3.83 us: shards(): side = lax.ppermute(side_out, 'py', [(0, 1), (1, 0)])]
    all_to_all x0 -> x1, blocking collectives: none -> 21.1 us  [shards(): got = lax.all_to_all(send, 'fr', 0, 0, tiled=True)]
    ppermute x20 -> x3, waiting for transfers between devices: 21.9 us -> 1.39 us  [the longest x1 1.39 us: shards(): side = lax.ppermute(side_out, 'py', [(0, 1), (1, 0)])]
    pallas_call x0 -> x4, Pallas kernels: none -> 15 us  [the longest x1 6.02 us: shards(): pl.pallas_call(outer_kernel, out_shape=jax.ShapeDtypeStruct((ranks, 8, 12...]
    unnamed x13 -> x18, local copies, waits for them, and re-layouts: 17.1 us -> 2.81 us
  transfers between devices with their start and end apart: 21 -> 3, of which waited for: 10 -> 1; matrix products, arithmetic and copies ran while one was open for 2% -> 0% of each run, Pallas kernels for 0% -> 12%
where the time goes in v1:
time: 47.5 us; the launch traced here: 47.1 us
  blocking collectives  21.1 us (44%)
  Pallas kernels  15 us (32%)
  starting transfers between devices  6.58 us (14%)
  local copies, waits for them, and re-layouts  2.82 us (6%)
  waiting for transfers between devices  1.39 us (3%)
    all_to_all x1, blocking collectives, shards(): got = lax.all_to_all(send, 'fr', 0, 0, tiled=True)  21.1 us
    pallas_call x1, Pallas kernels, shards(): pl.pallas_call(outer_kernel, out_shape=jax.ShapeDtypeStruct((ranks, 8, 12...  6.02 us
    pallas_call x1, Pallas kernels, shards(): pl.pallas_call(inner_kernel, out_shape=(jax.ShapeDtypeStruct((frames, 2,...  5.64 us
    ppermute x1, starting transfers between devices, shards(): side = lax.ppermute(side_out, 'py', [(0, 1), (1, 0)])  3.83 us
    unnamed x18, local copies, waits for them, and re-layouts  2.81 us
    pallas_call x1, Pallas kernels, shards(): pl.pallas_call(functools.partial(bin_kernel, frames * ranks), out_shape=j...  1.9 us
    pallas_call x1, Pallas kernels, shards(): pl.pallas_call(prepare_kernel, out_shape=(jax.ShapeDtypeStruct((4, frames...  1.49 us
    ppermute x1, starting transfers between devices, shards(): lax.ppermute(jnp.concatenate([feat[0:2], side[0:1]], axis=0), 'px', down)  1.42 us
  transfers between devices with their start and end apart: 3, of which 1 were waited for; matrix products, arithmetic and copies ran while one was open for 0% of the time, Pallas kernels for 12%

profile of v1, /device:TPU:1, one launch (start us, length us, event | category | flops | bytes accessed | tf_op | source)
XLA Modules:
  0.0 47.1 jit_solution(2595586005286209736)
XLA Ops:
  0.0 0.0 copy-start.5
  0.0 0.8 %copy.10.count_ref = s32[4,2,2]{2,1,0:T(2,128)S(1)} copy(s32[4,2,2]{0,2,1:T(2,128)} %param.12) | data formatting | bytes 128 | tf_op args[3]
  0.8 0.7 %copy.13.frac_ref = f32[2,2,3,128]{3,2,1,0:T(4,128)S(1)} copy(f32[2,2,3,128]{3,1,2,0:T(2,128)} %param.13) | data formatting | bytes 12288 | tf_op args[4]
  1.5 0.0 copy-done.5
  1.5 0.0 copy-start.6
  1.5 0.7 %copy-done.6 = f32[4,2,2,3,128]{4,2,3,1,0:T(2,128)S(1)} copy-done((f32[4,2,2,3,128]{4,2,3,1,0:T(2,128)S(1)}, f32[4,2,2,3,128]{4,2,3,1,0:T(2,128)}, u32[]{:S(2)}) %copy-start.6) | copy-done | bytes 24600
  2.2 0.0 copy-start
  2.2 0.0 copy-start.1
  2.2 0.0 copy-start.2
  2.3 0.0 copy-start.3
  2.3 0.0 copy-start.4
  2.3 0.1 pad_add_fusion.place_ref
  2.4 0.6 %copy-done = s32[4,2,2,128]{3,2,1,0:T(2,128)S(1)} copy-done((s32[4,2,2,128]{3,2,1,0:T(2,128)S(1)}, s32[4,2,2,128]{3,2,1,0:T(2,128)}, u32[]{:S(2)}) %copy-start) | copy-done | bytes 8216
  2.9 0.0 copy-done.1
  2.9 0.0 copy-done.2
  2.9 0.0 copy-done.3
  2.9 0.0 copy-done.4
  2.9 1.5 %prepare.1 = (f32[4,5,8,128]{3,2,1,0:T(8,128)S(1)}, f32[2,5,8,128]{3,2,1,0:T(8,128)S(1)}, f32[6,16,128]{2,1,0:T(8,128)S(1)}) custom-call(s32[3]{0:T(128)S(1)} %pad_add_fusion.place_ref, s32[4,2,2]{2,1,0:T(2,128)S(1)} %copy.10.count_ref, f32[32]{0:T(128)S(1)} %copy-done.2, f32[32]{0:T(128)S(1)} %copy-done.3, f32[32]{0:T(128)S(1)} %copy-done.4, ...), custom_call_target="tpu_custom_call" | custom-call | tf_op jit(solution)/shard_map/prepare/pallas_call | solution.py:463
  4.4 3.8 %collective-permute-start = (f32[2,5,8,128]{3,2,1,0:T(8,128)S(1)}, f32[2,5,8,128]{3,2,1,0:T(8,128)S(1)}, u32[]{:S(2)}, u32[]{:S(2)}) collective-permute-start(f32[2,5,8,128]{3,2,1,0:T(8,128)S(1)} %get-tuple-element.11), channel_id=1, source_target_pairs={{0,32},{32,0},{1,33},{33,1},{2,34},{34,2},{3,35},{35,3},{4,36},{36... | collective-permute-start | bytes 122888 | tf_op jit(solution)/shard_map/ppermute | solution.py:482
  8.3 1.4 %collective-permute-done.side_ref = f32[2,5,8,128]{3,2,1,0:T(8,128)S(1)} collective-permute-done((f32[2,5,8,128]{3,2,1,0:T(8,128)S(1)}, f32[2,5,8,128]{3,2,1,0:T(8,128)S(1)}, u32[]{:S(2)}, u32[]{:S(2)}) %collective-permute-start) | collective-permute-done | bytes 40992 | tf_op jit(solution)/shard_map/ppermute | solution.py:482
  9.7 1.3 %collective-permute-start.1 = (f32[3,5,8,128]{3,2,1,0:T(8,128)S(1)}, f32[3,5,8,128]{3,2,1,0:T(8,128)S(1)}, u32[]{:S(2)}, u32[]{:S(2)}) collective-permute-start(f32[3,5,8,128]{3,2,1,0:T(8,128)S(1)} %pad_maximum_fusion), channel_id=1, source_target_pairs={{0,64},{64,128},{128,192},{192,0},{1,65},{65,129},{129,193},{193,1... | collective-permute-start | bytes 184328 | tf_op jit(solution)/shard_map/ppermute | solution.py:485
  11.0 1.4 %collective-permute-start.2 = (f32[3,5,8,128]{3,2,1,0:T(8,128)S(1)}, f32[3,5,8,128]{3,2,1,0:T(8,128)S(1)}, u32[]{:S(2)}, u32[]{:S(2)}) collective-permute-start(f32[3,5,8,128]{3,2,1,0:T(8,128)S(1)} %pad_maximum_fusion.1), channel_id=1, source_target_pairs={{0,192},{64,0},{128,64},{192,128},{1,193},{65,1},{129,65},{193,129... | collective-permute-start | bytes 184328 | tf_op jit(solution)/shard_map/ppermute | solution.py:486
  12.4 5.6 %inner.1 = (f32[4,2,2,8,256]{4,3,2,1,0:T(8,128)S(1)}, f32[16,16,128]{2,1,0:T(8,128)S(1)}) custom-call(f32[4,5,8,128]{3,2,1,0:T(8,128)S(1)} %get-tuple-element.10.feat_ref, f32[6,16,128]{2,1,0:T(8,128)S(1)} %get-tuple-element.12.comp_ref), custom_call_target="tpu_custom_call" | custom-call | flops 1000000000 | bytes 1000000 | tf_op jit(solution)/shard_map/inner/pallas_call | solution.py:488
  18.1 0.0 collective-permute-done.1.low_ref
  18.1 0.0 collective-permute-done.2.high_ref
  18.1 6.0 %outer.1 = f32[32,8,128]{2,1,0:T(8,128)S(1)} custom-call(s32[3]{0:T(128)S(1)} %pad_add_fusion.place_ref, f32[4,5,8,128]{3,2,1,0:T(8,128)S(1)} %get-tuple-element.10.feat_ref, f32[2,5,8,128]{3,2,1,0:T(8,128)S(1)} %collective-permute-done.side_ref, f32[3,5,8,128]{3,2,1,0:T(8,128)S(1)} %collective-permute-done.1.low_ref, ...), custom_call_target="tpu_custom_call" | custom-call | tf_op jit(solution)/shard_map/outer/pallas_call | solution.py:506
  24.1 21.1 %all_to_all.5.got_ref = f32[32,8,128]{2,1,0:T(8,128)S(1)} all-to-all(f32[32,8,128]{2,1,0:T(8,128)S(1)} %outer.1), channel_id=1, replica_groups=mesh['px'=4,'py'=2,'fr'=32] {'fr'}, dimensions={0} | all-to-all | bytes 262144 | tf_op jit(solution)/shard_map/all_to_all | solution.py:522
  45.3 1.9 %bin.1 = f32[13,2,2,720]{3,2,1,0:T(2,128)} custom-call(f32[32,8,128]{2,1,0:T(8,128)S(1)} %all_to_all.5.got_ref), custom_call_target="tpu_custom_call" | custom-call | tf_op jit(solution)/shard_map/bin/pallas_call | solution.py:524
  (6 shorter events, 0.0 us)
Async XLA Ops:
  0.0 1.5 %copy-start.5 = (f32[4,2,2,3,128]{4,2,3,1,0:T(2,128)S(1)}, f32[4,2,2,3,128]{4,2,3,1,0:T(2,128)}, u32[]{:S(2)}) copy-start(f32[4,2,2,3,128]{4,2,3,1,0:T(2,128)} %param.10) | copy-start | bytes 73732
  1.5 0.7 %copy-start.6 = (f32[4,2,2,3,128]{4,2,3,1,0:T(2,128)S(1)}, f32[4,2,2,3,128]{4,2,3,1,0:T(2,128)}, u32[]{:S(2)}) copy-start(f32[4,2,2,3,128]{4,2,3,1,0:T(2,128)} %param.11) | copy-start | bytes 73732
  2.2 0.7 %copy-start = (s32[4,2,2,128]{3,2,1,0:T(2,128)S(1)}, s32[4,2,2,128]{3,2,1,0:T(2,128)}, u32[]{:S(2)}) copy-start(s32[4,2,2,128]{3,2,1,0:T(2,128)} %voxel_ref.1) | copy-start | bytes 24580
  2.2 0.7 %copy-start.1 = (s32[2,2,128]{2,1,0:T(2,128)S(1)}, s32[2,2,128]{2,1,0:T(2,128)}, u32[]{:S(2)}) copy-start(s32[2,2,128]{2,1,0:T(2,128)} %type_ref.1) | copy-start | bytes 6148
  2.2 0.7 %copy-start.2 = (f32[32]{0:T(128)S(1)}, f32[32]{0:T(128)}, u32[]{:S(2)}) copy-start(f32[32]{0:T(128)} %sigma_ref.1) | copy-start | bytes 388
  2.3 0.7 %copy-start.3 = (f32[32]{0:T(128)S(1)}, f32[32]{0:T(128)}, u32[]{:S(2)}) copy-start(f32[32]{0:T(128)} %well_ref.1) | copy-start | bytes 388
  2.3 0.7 %copy-start.4 = (f32[32]{0:T(128)S(1)}, f32[32]{0:T(128)}, u32[]{:S(2)}) copy-start(f32[32]{0:T(128)} %charge_ref.1) | copy-start | bytes 388
  4.4 5.2 %collective-permute-start = (f32[2,5,8,128]{3,2,1,0:T(8,128)S(1)}, f32[2,5,8,128]{3,2,1,0:T(8,128)S(1)}, u32[]{:S(2)}, u32[]{:S(2)}) collective-permute-start(f32[2,5,8,128]{3,2,1,0:T(8,128)S(1)} %get-tuple-element.11), channel_id=1, source_target_pairs={{0,32},{32,0},{1,33},{33,1},{2,34},{34,2},{3,35},{35,3},{4,36},{36... | collective-permute-start | bytes 122888 | tf_op jit(solution)/shard_map/ppermute | solution.py:482
  9.7 8.4 %collective-permute-start.1 = (f32[3,5,8,128]{3,2,1,0:T(8,128)S(1)}, f32[3,5,8,128]{3,2,1,0:T(8,128)S(1)}, u32[]{:S(2)}, u32[]{:S(2)}) collective-permute-start(f32[3,5,8,128]{3,2,1,0:T(8,128)S(1)} %pad_maximum_fusion), channel_id=1, source_target_pairs={{0,64},{64,128},{128,192},{192,0},{1,65},{65,129},{129,193},{193,1... | collective-permute-start | bytes 184328 | tf_op jit(solution)/shard_map/ppermute | solution.py:485
  11.0 7.1 %collective-permute-start.2 = (f32[3,5,8,128]{3,2,1,0:T(8,128)S(1)}, f32[3,5,8,128]{3,2,1,0:T(8,128)S(1)}, u32[]{:S(2)}, u32[]{:S(2)}) collective-permute-start(f32[3,5,8,128]{3,2,1,0:T(8,128)S(1)} %pad_maximum_fusion.1), channel_id=1, source_target_pairs={{0,192},{64,0},{128,64},{192,128},{1,193},{65,1},{129,65},{193,129... | collective-permute-start | bytes 184328 | tf_op jit(solution)/shard_map/ppermute | solution.py:486

commit v2 on v1

--- a/solution.py
+++ b/solution.py
@@ -72,24 +72,26 @@
     return sin_out, cos_out
 
 
-def prepare_kernel(
-    place_ref, count_ref, sigma_ref, well_ref, charge_ref,
-    voxel_ref, offset_ref, angle_ref, frac_ref, type_ref,
-    feat_ref, side_ref, comp_ref,
-    raw_ref, key_ref, sorted_ref,
-):
-    frames = voxel_ref.shape[0]
-    lane = lax.broadcasted_iota(jnp.int32, (1, 128), 1)
+def prepare_kernel(packed_ref, feat_ref, side_ref, comp_ref, raw_ref, key_ref, sorted_ref):
+    frames = feat_ref.shape[1] - 1
+    pairs = 2 * frames
+    offset_at, angle_at, frac_at = pairs, 4 * pairs, 7 * pairs
+    type_at, count_at, table_at = frac_at + 6, frac_at + 8, frac_at + 10
+    lane = lax.broadcasted_iota(jnp.int32, (1, 128), 1).astype(F32)
     for i in range(2):
         for j in range(2):
+            row = slice(j, j + 1)
             for f in range(frames):
                 fc = (i * 2 + j) * frames + f
-                voxel = voxel_ref[f, i, j : j + 1, :]
-                raw_ref[fc, 0:1, :] = voxel.astype(F32)
-                raw_ref[fc, 1:4, :] = offset_ref[f, i, j]
-                raw_ref[fc, 4:7, :] = angle_ref[f, i, j]
-                raw_ref[fc, 7:8, :] = jnp.where(lane < count_ref[f, i, j], 1.0, 0.0).astype(F32)
-                key_ref[fc : fc + 1, :] = (voxel * 128 + lane).astype(F32)
+                voxel = packed_ref[f * 2 + i, row, :]
+                raw_ref[fc, 0:1, :] = voxel
+                for axis in range(3):
+                    at = (f * 2 + i) * 3 + axis
+                    raw_ref[fc, 1 + axis : 2 + axis, :] = packed_ref[offset_at + at, row, :]
+                    raw_ref[fc, 4 + axis : 5 + axis, :] = packed_ref[angle_at + at, row, :]
+                count = packed_ref[count_at + i, row, f : f + 1]
+                raw_ref[fc, 7:8, :] = jnp.where(lane < count, 1.0, 0.0).astype(F32)
+                key_ref[fc : fc + 1, :] = voxel * 128.0 + lane
     total = 4 * frames
     keys = key_ref[...]
     keys_t = keys.T
@@ -137,32 +139,34 @@
     for number, value in enumerate((quat_w, quat_x, quat_y, quat_z, sorted_ref[7], voxel - band)):
         comp_ref[number] = value
 
+    table = jnp.concatenate(
+        [packed_ref[table_at + k, 0:1, :] for k in range(3)] + [jnp.zeros((5, 128), F32)], axis=0
+    )
+    tables = jnp.concatenate(split3(table), axis=0).astype(BF16)
     for i in range(2):
         for j in range(2):
-            kind = type_ref[i, j : j + 1, :]
-            sigma = jnp.zeros((1, 128), F32)
-            well = jnp.zeros((1, 128), F32)
-            charge = jnp.zeros((1, 128), F32)
-            for t in range(sigma_ref.shape[0]):
-                same = kind == t
-                sigma = jnp.where(same, sigma_ref[t], sigma)
-                well = jnp.where(same, well_ref[t], well)
-                charge = jnp.where(same, charge_ref[t], charge)
+            kind = packed_ref[type_at + i, j : j + 1, :]
+            chosen = jnp.where(rank_iota == kind, 1.0, 0.0).astype(BF16)
+            looked = jnp.dot(tables, chosen, preferred_element_type=F32)
+            looked = looked[0:8] + looked[8:16] + looked[16:24]
+            sigma, well, charge = looked[0:1], looked[1:2], looked[2:3]
             ratio = 0.5 * (1.0 + sigma * UNIT)
             cube = ratio * ratio * ratio
             sixth = cube * cube
             lower = (4.0 * eps_water**0.5) * jnp.sqrt(well) * sixth
-            frac = frac_ref[i, j]
-            atom_x = (frac[0:1] * CUTOFF + CUTOFF * (i - 1.0)) * UNIT
-            atom_y = (frac[1:2] * CUTOFF + CUTOFF * (j - 1.0)) * UNIT
-            atom_z = (frac[2:3] * (spacing * SLAB) - 0.5 * spacing * SLAB) * UNIT
+            frac_x, frac_y, frac_z = (
+                packed_ref[frac_at + i * 3 + axis, j : j + 1, :] for axis in range(3)
+            )
+            atom_x = (frac_x * CUTOFF + CUTOFF * (i - 1.0)) * UNIT
+            atom_y = (frac_y * CUTOFF + CUTOFF * (j - 1.0)) * UNIT
+            atom_z = (frac_z * (spacing * SLAB) - 0.5 * spacing * SLAB) * UNIT
             feat_ref[i * 2 + j, frames] = rows_of(
                 [atom_x, atom_y, atom_z, lower, lower * sixth, charge, jnp.ones((1, 128), F32)]
             )
     for cell in range(4):
         for f in range(frames):
             feat_ref[cell, f, 7:8, :] = jnp.zeros((1, 128), F32)
-    facing = 1 - place_ref[1]
+    facing = 1 - lax.axis_index("py")
     for i in range(2):
         side_ref[i] = feat_ref[i * 2 + facing]
 
@@ -251,8 +255,9 @@
         root = lax.rsqrt(pk)
         u15 = root * root * root
         window = jnp.maximum(P_END - pk, 0.0)
-        low = jnp.concatenate([lower[part]] * 2, axis=1)
-        high = jnp.concatenate([upper[part]] * 2, axis=1)
+        low, high = lower[part], upper[part]
+        if low.shape[1] != pk.shape[1]:
+            low, high = jnp.concatenate([low] * 2, axis=1), jnp.concatenate([high] * 2, axis=1)
         inner = u15 * (high * (u15 * u15) - low) + charge[part]
         acc = fold(acc, u15 * inner * (window * window))
     return acc
@@ -262,7 +267,7 @@
     return jnp.dot(left, right, preferred_element_type=F32)
 
 
-def inner_kernel(feat_ref, comp_ref, acc_ref, rec_ref, left_ref, own_ref, coef_ref):
+def inner_kernel(feat_ref, comp_ref, acc_ref, rec_ref, own_ref, left_ref, coef_ref):
     frames = feat_ref.shape[1] - 1
     for cell in range(4):
         rows, lower, upper = solute_partner(feat_ref[cell, frames], (0.0, 0.0), 0.0)
@@ -302,24 +307,60 @@
         rec_ref[:, number, :] = value
 
 
+def side_kernel(side_ref, own_ref, acc_in_ref, acc_ref, left_ref, coef_ref):
+    frames = side_ref.shape[1] - 1
+    py = lax.axis_index("py")
+    facing = 1 - py
+    width = 2.0 * CUTOFF * UNIT
+    to_side = jnp.where(py == 0, width, -width).astype(F32)
+    for cell in range(2):
+        rows, lower, upper = solute_partner(side_ref[cell, frames], (0.0, to_side), 0.0)
+        left_ref[frames, cell] = rows
+        coef_ref[cell, 0] = lower
+        coef_ref[cell, 1] = upper
+        for f in range(frames):
+            left_ref[f, cell] = water_partner(side_ref[cell, f], (0.0, to_side), 0.0)
+    upper_row = (facing == 1).astype(F32)
+
+    @pl.loop(0, frames)
+    def _(f):
+        sides = [
+            jnp.concatenate([own_ref[f, q, facing], own_ref[f, q, 2 + facing]], axis=1)
+            for q in range(5)
+        ]
+        acc_w = jnp.zeros((8, 256), F32)
+        acc_s = jnp.zeros((8, 256), F32)
+        for cell in range(2):
+            left = left_ref[f, cell]
+            acc_w = water_pairs(acc_w, *[dot(left, sides[q]) for q in range(4)])
+            left = left_ref[frames, cell]
+            acc_s = solute_pairs(
+                acc_s, dot(left, sides[0]), dot(left, sides[4]), coef_ref[cell, 0], coef_ref[cell, 1]
+            )
+        for i in range(2):
+            for number, acc in ((0, acc_w), (1, acc_s)):
+                mine = acc[:, i * 128 : (i + 1) * 128]
+                acc_ref[f, i, number] = acc_in_ref[f, i, number] + jnp.concatenate(
+                    [mine * (1.0 - upper_row), mine * upper_row], axis=1
+                )
+
+
 def outer_kernel(
-    place_ref, feat_ref, side_ref, low_ref, high_ref, first_ref, rec_in_ref, send_ref,
-    left_ref, own_ref, coef_ref, acc_ref, rec_ref,
+    feat_ref, low_ref, high_ref, own_ref, acc_in_ref, rec_in_ref, send_ref,
+    left_ref, coef_ref, acc_ref, rec_ref,
 ):
     frames = feat_ref.shape[1] - 1
-    px = place_ref[0]
-    py = place_ref[1]
-    last = place_ref[2]
+    px = lax.axis_index("px")
+    py = lax.axis_index("py")
+    last = lax.axis_size("px") - 1
     facing = 1 - py
     width = 2.0 * CUTOFF * UNIT
     to_side = jnp.where(py == 0, width, -width).astype(F32)
     no_low = jnp.where(px == 0, 1.0, 0.0).astype(F32)
     no_high = jnp.where(px == last, 1.0, 0.0).astype(F32)
-    halo = (
-        [(low_ref, k, (-width, to_side if k == 2 else 0.0), no_low) for k in range(3)]
-        + [(high_ref, k, (width, to_side if k == 2 else 0.0), no_high) for k in range(3)]
-        + [(side_ref, k, (0.0, to_side), 0.0) for k in range(2)]
-    )
+    halo = [(low_ref, k, (-width, to_side if k == 2 else 0.0), no_low) for k in range(3)] + [
+        (high_ref, k, (width, to_side if k == 2 else 0.0), no_high) for k in range(3)
+    ]
     for cell, (ref, k, shift, absent) in enumerate(halo):
         rows, lower, upper = solute_partner(ref[k, frames], shift, absent)
         left_ref[frames, cell] = rows
@@ -327,43 +368,10 @@
         coef_ref[cell, 1] = upper
         for f in range(frames):
             left_ref[f, cell] = water_partner(ref[k, f], shift, absent)
-    for cell in range(4):
-        for f in range(frames):
-            for q, side in enumerate(own_side(feat_ref[cell, f])):
-                own_ref[f, q, cell] = side
-    acc_ref[...] = first_ref[...]
+    upper_row = (facing == 1).astype(F32)
 
     @pl.loop(0, frames)
     def _(f):
-        def unit(sides, cell, acc_w, acc_s):
-            left = left_ref[f, cell]
-            acc_w = water_pairs(acc_w, *[dot(left, sides[q]) for q in range(4)])
-            left = left_ref[frames, cell]
-            acc_s = solute_pairs(
-                acc_s, dot(left, sides[0]), dot(left, sides[4]), coef_ref[cell, 0], coef_ref[cell, 1]
-            )
-            return acc_w, acc_s
-
-        for i in range(2):
-            sides = [
-                jnp.concatenate([own_ref[f, q, 2 * i], own_ref[f, q, 2 * i + 1]], axis=1)
-                for q in range(5)
-            ]
-            acc_w = acc_ref[f, i, 0]
-            acc_s = acc_ref[f, i, 1]
-            for k in range(2):
-                acc_w, acc_s = unit(sides, 3 * i + k, acc_w, acc_s)
-            acc_ref[f, i, 0] = acc_w
-            acc_ref[f, i, 1] = acc_s
-        sides = [
-            jnp.concatenate([own_ref[f, q, facing], own_ref[f, q, 2 + facing]], axis=1)
-            for q in range(5)
-        ]
-        acc_w = jnp.zeros((8, 256), F32)
-        acc_s = jnp.zeros((8, 256), F32)
-        for k in range(2):
-            acc_w, acc_s = unit(sides, 6 + k, acc_w, acc_s)
-
         def both(source, q):
             return jnp.concatenate(
                 [
@@ -373,26 +381,34 @@
                 axis=1,
             )
 
-        acc_w = water_pairs(acc_w, *[both(f, q) for q in range(4)])
-        p = both(frames, 0)
-        charge = both(frames, 4)
-        for k in range(128 // CHUNK):
-            part = slice(k * CHUNK, (k + 1) * CHUNK)
-            pk = p[part]
-            root = lax.rsqrt(pk)
-            u15 = root * root * root
-            window = jnp.maximum(P_END - pk, 0.0)
-            low = jnp.concatenate([coef_ref[2, 0, part], coef_ref[5, 0, part]], axis=1)
-            high = jnp.concatenate([coef_ref[2, 1, part], coef_ref[5, 1, part]], axis=1)
-            inner = u15 * (high * (u15 * u15) - low) + charge[part]
-            acc_s = fold(acc_s, u15 * inner * (window * window))
-        upper_row = (facing == 1).astype(F32)
+        zero = jnp.zeros((8, 256), F32)
+        corner_w = water_pairs(zero, *[both(f, q) for q in range(4)])
+        lower, upper = (
+            jnp.concatenate([coef_ref[2, k], coef_ref[5, k]], axis=1) for k in range(2)
+        )
+        corner_s = solute_pairs(zero, both(frames, 0), both(frames, 4), lower, upper)
         for i in range(2):
-            for number, acc in ((0, acc_w), (1, acc_s)):
+            sides = [
+                jnp.concatenate([own_ref[f, q, 2 * i], own_ref[f, q, 2 * i + 1]], axis=1)
+                for q in range(5)
+            ]
+            start = []
+            for number, acc in ((0, corner_w), (1, corner_s)):
                 mine = acc[:, i * 128 : (i + 1) * 128]
-                acc_ref[f, i, number] += jnp.concatenate(
-                    [mine * (1.0 - upper_row), mine * upper_row], axis=1
+                start.append(
+                    acc_in_ref[f, i, number]
+                    + jnp.concatenate([mine * (1.0 - upper_row), mine * upper_row], axis=1)
                 )
+            acc_w, acc_s = start
+            for cell in (3 * i, 3 * i + 1):
+                left = left_ref[f, cell]
+                acc_w = water_pairs(acc_w, *[dot(left, sides[q]) for q in range(4)])
+                left = left_ref[frames, cell]
+                acc_s = solute_pairs(
+                    acc_s, dot(left, sides[0]), dot(left, sides[4]), coef_ref[cell, 0], coef_ref[cell, 1]
+                )
+            acc_ref[f, i, 0] = acc_w
+            acc_ref[f, i, 1] = acc_s
 
     rec_ref[...] = rec_in_ref[...]
     self_root = P_SOFT**-0.5
@@ -442,11 +458,7 @@
     return pl.BlockSpec(memory_space=pltpu.VMEM)
 
 
-def smem():
-    return pl.BlockSpec(memory_space=pltpu.SMEM)
-
-
-PARAMS = pltpu.CompilerParams(vmem_limit_bytes=48 * 1024 * 1024)
+PARAMS = pltpu.CompilerParams(vmem_limit_bytes=24 * 1024 * 1024)
 
 
 def shards(
@@ -456,10 +468,29 @@
     frames = water_voxel.shape[0]
     cols = lax.axis_size("px")
     ranks = lax.axis_size("fr")
-    place = jnp.stack(
-        [lax.axis_index("px"), lax.axis_index("py"), jnp.int32(cols - 1)]
-    ).astype(jnp.int32)
     total = 4 * frames
+    rows = (-1, 2, 128)
+    pieces = (
+        water_voxel.reshape(rows),
+        jnp.transpose(water_offset, (0, 1, 3, 2, 4)).reshape(rows),
+        jnp.transpose(water_angles, (0, 1, 3, 2, 4)).reshape(rows),
+        jnp.transpose(solute_frac, (0, 2, 1, 3)).reshape(rows),
+        solute_type.reshape(rows),
+        jnp.transpose(water_count, (1, 2, 0)),
+        type_sigma.reshape(1, 1, -1), type_well.reshape(1, 1, -1), type_charge.reshape(1, 1, -1),
+    )
+    deep = sum(piece.shape[0] for piece in pieces)
+    sums = {F32: jnp.zeros((deep, 2, 128), F32), jnp.int32: jnp.zeros((deep, 2, 128), jnp.int32)}
+    start = 0
+    for piece in pieces:
+        size = piece.shape
+        kind = F32 if piece.dtype == F32 else jnp.int32
+        sums[kind] = sums[kind] + lax.pad(
+            piece, jnp.zeros((), kind),
+            ((start, deep - start - size[0], 0), (0, 2 - size[1], 0), (0, 128 - size[2], 0)),
+        )
+        start += size[0]
+    packed = sums[F32] + sums[jnp.int32].astype(F32)
     feat, side_out, comp = pl.pallas_call(
         prepare_kernel,
         out_shape=(
@@ -467,7 +498,7 @@
             jax.ShapeDtypeStruct((2, frames + 1, 8, 128), F32),
             jax.ShapeDtypeStruct((6, total, 128), F32),
         ),
-        in_specs=[smem()] * 5 + [vmem()] * 5,
+        in_specs=[vmem()],
         out_specs=(vmem(),) * 3,
         scratch_shapes=[
             pltpu.VMEM((total, 8, 128), F32),
@@ -476,26 +507,22 @@
         ],
         compiler_params=PARAMS,
         name="prepare",
-    )(place, water_count, type_sigma, type_well, type_charge,
-      water_voxel, water_offset, water_angles, solute_frac, solute_type)
+    )(packed)
 
     side = lax.ppermute(side_out, "py", [(0, 1), (1, 0)])
-    up = [(k, (k + 1) % cols) for k in range(cols)]
-    down = [(k, (k - 1) % cols) for k in range(cols)]
-    low = lax.ppermute(jnp.concatenate([feat[2:4], side[1:2]], axis=0), "px", up)
-    high = lax.ppermute(jnp.concatenate([feat[0:2], side[0:1]], axis=0), "px", down)
-
-    acc, rec = pl.pallas_call(
+
+    acc_shape = jax.ShapeDtypeStruct((frames, 2, 2, 8, 256), F32)
+    acc, rec, own = pl.pallas_call(
         inner_kernel,
         out_shape=(
-            jax.ShapeDtypeStruct((frames, 2, 2, 8, 256), F32),
+            acc_shape,
             jax.ShapeDtypeStruct((total, 16, 128), F32),
+            jax.ShapeDtypeStruct((frames, 5, 4, ROWS, 128), BF16),
         ),
         in_specs=[vmem()] * 2,
-        out_specs=(vmem(),) * 2,
+        out_specs=(vmem(),) * 3,
         scratch_shapes=[
             pltpu.VMEM((frames + 1, 4, 128, ROWS), BF16),
-            pltpu.VMEM((frames, 5, 4, ROWS, 128), BF16),
             pltpu.VMEM((4, 2, 128, 128), F32),
         ],
         compiler_params=PARAMS,
@@ -503,21 +530,39 @@
         name="inner",
     )(feat, comp)
 
+    side, acc = lax.optimization_barrier((side, acc))
+    up = [(k, (k + 1) % cols) for k in range(cols)]
+    down = [(k, (k - 1) % cols) for k in range(cols)]
+    low = lax.ppermute(jnp.concatenate([feat[2:4], side[1:2]], axis=0), "px", up)
+    high = lax.ppermute(jnp.concatenate([feat[0:2], side[0:1]], axis=0), "px", down)
+    acc = pl.pallas_call(
+        side_kernel,
+        out_shape=acc_shape,
+        in_specs=[vmem()] * 3,
+        out_specs=vmem(),
+        scratch_shapes=[
+            pltpu.VMEM((frames + 1, 2, 128, ROWS), BF16),
+            pltpu.VMEM((2, 2, 128, 128), F32),
+        ],
+        compiler_params=PARAMS,
+        cost_estimate=pl.CostEstimate(flops=10**9, bytes_accessed=10**6, transcendentals=0),
+        name="side",
+    )(side, own, acc)
+
     send = pl.pallas_call(
         outer_kernel,
         out_shape=jax.ShapeDtypeStruct((ranks, 8, 128), F32),
-        in_specs=[smem()] + [vmem()] * 6,
+        in_specs=[vmem()] * 6,
         out_specs=vmem(),
         scratch_shapes=[
-            pltpu.VMEM((frames + 1, 8, 128, ROWS), BF16),
-            pltpu.VMEM((frames, 5, 4, ROWS, 128), BF16),
-            pltpu.VMEM((8, 2, 128, 128), F32),
+            pltpu.VMEM((frames + 1, 6, 128, ROWS), BF16),
+            pltpu.VMEM((6, 2, 128, 128), F32),
             pltpu.VMEM((frames, 2, 2, 8, 256), F32),
             pltpu.VMEM((total, 16, 128), F32),
         ],
         compiler_params=PARAMS,
         name="outer",
-    )(place, feat, side, low, high, acc, rec)
+    )(feat, low, high, own, acc, rec)
 
     got = lax.all_to_all(send, "fr", 0, 0, tiled=True)
     share = CELL_XY * CELL_XY * SLAB // ranks

time: 47.5 us -> 42 us (0.88)
  local copies, waits for them, and re-layouts: 2.82 us -> 0.01 us
  waiting for transfers between devices: 1.39 us -> 0.01 us
  blocking collectives: 21.1 us -> 19.9 us
  other arithmetic: 0.09 us -> 0.89 us
  Pallas kernels: 15 us -> 14.4 us
    unnamed x18 -> x0, local copies, waits for them, and re-layouts: 2.81 us -> none
    pallas_call x1 -> x2, Pallas kernels: 5.64 us -> 7.59 us  [the longest x1 5.69 us: shards(): pl.pallas_call(inner_kernel, out_shape=(acc_shape, jax.ShapeDtypeStruct((...]
    pallas_call x1, Pallas kernels: 6.02 us -> 4.14 us  [shards(): pl.pallas_call(outer_kernel, out_shape=jax.ShapeDtypeStruct((ranks, 8, 12...]
    ppermute x1, waiting for transfers between devices: 1.39 us -> 0.01 us  [shards(): side = lax.ppermute(side_out, 'py', [(0, 1), (1, 0)])]
    all_to_all x1, blocking collectives: 21.1 us -> 19.9 us  [shards(): got = lax.all_to_all(send, 'fr', 0, 0, tiled=True)]
    add x0 -> x1, other arithmetic: none -> 0.88 us  [shards(): packed = sums[F32] + sums[jnp.int32].astype(F32)]
    pallas_call x1, Pallas kernels: 1.49 us -> 0.79 us  [shards(): pl.pallas_call(prepare_kernel, out_shape=(jax.ShapeDtypeStruct((4, frames...]
  transfers between devices with their start and end apart: 3 -> 3, of which waited for: 1 -> 0; matrix products, arithmetic and copies ran while one was open for 0% -> 0% of each run, Pallas kernels for 12% -> 18%
where the time goes in v2:
time: 42 us; the launch traced here: 41.8 us
  blocking collectives  19.9 us (47%)
  Pallas kernels  14.4 us (34%)
  starting transfers between devices  6.58 us (16%)
  other arithmetic  0.89 us (2%)
    all_to_all x1, blocking collectives, shards(): got = lax.all_to_all(send, 'fr', 0, 0, tiled=True)  19.9 us
    pallas_call x1, Pallas kernels, shards(): pl.pallas_call(inner_kernel, out_shape=(acc_shape, jax.ShapeDtypeStruct((...  5.69 us
    pallas_call x1, Pallas kernels, shards(): pl.pallas_call(outer_kernel, out_shape=jax.ShapeDtypeStruct((ranks, 8, 12...  4.14 us
    ppermute x1, starting transfers between devices, shards(): side = lax.ppermute(side_out, 'py', [(0, 1), (1, 0)])  3.83 us
    pallas_call x1, Pallas kernels, shards(): pl.pallas_call(side_kernel, out_shape=acc_shape, in_specs=[vmem()] * 3, o...  1.91 us
    pallas_call x1, Pallas kernels, shards(): pl.pallas_call(functools.partial(bin_kernel, frames * ranks), out_shape=j...  1.9 us
    ppermute x1, starting transfers between devices, shards(): lax.ppermute(jnp.concatenate([feat[0:2], side[0:1]], axis=0), 'px', down)  1.46 us
    ppermute x1, starting transfers between devices, shards(): lax.ppermute(jnp.concatenate([feat[2:4], side[1:2]], axis=0), 'px', up)  1.29 us
  transfers between devices with their start and end apart: 3, of which 0 were waited for; matrix products, arithmetic and copies ran while one was open for 0% of the time, Pallas kernels for 18%

profile of v2, /device:TPU:1, one launch (start us, length us, event | category | flops | bytes accessed | tf_op | source)
XLA Modules:
  0.0 41.8 jit_solution(4164664226363995238)
XLA Ops:
  0.0 0.9 %convert_add_fusion.packed_ref = f32[69,2,128]{2,1,0:T(2,128)S(1)} fusion(s32[2,2,4]{2,1,0:T(2,128)} %bitcast.18, s32[2,2,128]{2,1,0:T(2,128)} %param.14, s32[8,2,128]{2,1,0:T(2,128)} %bitcast.16, f32[1,1,32]{2,1,0:T(1,128)} %bitcast.19, f32[1,1,32]{2,1,0:T(1,128)} %bitcast.20, f32[1,1,32]{2,1,0:T(1,128)} %bitcast.21, f32[6,2,128]{2,1,0:T(2,128)} %bitcast.17, ...), kind=kLoop, calls=%fused_computation | loop fusion | flops 158976 | bytes 136640 | tf_op jit(solution)/shard_map/add | solution.py:493
  0.9 0.8 %prepare.1 = (f32[4,5,8,128]{3,2,1,0:T(8,128)S(1)}, f32[2,5,8,128]{3,2,1,0:T(8,128)S(1)}, f32[6,16,128]{2,1,0:T(8,128)S(1)}) custom-call(f32[69,2,128]{2,1,0:T(2,128)S(1)} %convert_add_fusion.packed_ref), custom_call_target="tpu_custom_call" | custom-call | tf_op jit(solution)/shard_map/prepare/pallas_call | solution.py:494
  1.7 3.8 %collective-permute-start = (f32[2,5,8,128]{3,2,1,0:T(8,128)S(1)}, f32[2,5,8,128]{3,2,1,0:T(8,128)S(1)}, u32[]{:S(2)}, u32[]{:S(2)}) collective-permute-start(f32[2,5,8,128]{3,2,1,0:T(8,128)S(1)} %get-tuple-element.14), channel_id=1, source_target_pairs={{0,32},{32,0},{1,33},{33,1},{2,34},{34,2},{3,35},{35,3},{4,36},{36... | collective-permute-start | bytes 122888 | tf_op jit(solution)/shard_map/ppermute | solution.py:512
  5.5 5.7 %inner.1 = (f32[4,2,2,8,256]{4,3,2,1,0:T(8,128)S(1)}, f32[16,16,128]{2,1,0:T(8,128)S(1)}, bf16[4,5,4,64,128]{4,3,2,1,0:T(8,128)(2,1)S(1)}) custom-call(f32[4,5,8,128]{3,2,1,0:T(8,128)S(1)} %get-tuple-element.13.feat_ref, f32[6,16,128]{2,1,0:T(8,128)S(1)} %get-tuple-element.15.comp_ref), custom_call_target="tpu_custom_call" | custom-call | flops 1000000000 | bytes 1000000 | tf_op jit(solution)/shard_map/inner/pallas_call | solution.py:515
  11.2 0.0 collective-permute-done.side_ref
  11.2 1.3 %collective-permute-start.1 = (f32[3,5,8,128]{3,2,1,0:T(8,128)S(1)}, f32[3,5,8,128]{3,2,1,0:T(8,128)S(1)}, u32[]{:S(2)}, u32[]{:S(2)}) collective-permute-start(f32[3,5,8,128]{3,2,1,0:T(8,128)S(1)} %pad_maximum_fusion), channel_id=1, source_target_pairs={{0,64},{64,128},{128,192},{192,0},{1,65},{65,129},{129,193},{193,1... | collective-permute-start | bytes 184328 | tf_op jit(solution)/shard_map/ppermute | solution.py:536
  12.5 1.5 %collective-permute-start.2 = (f32[3,5,8,128]{3,2,1,0:T(8,128)S(1)}, f32[3,5,8,128]{3,2,1,0:T(8,128)S(1)}, u32[]{:S(2)}, u32[]{:S(2)}) collective-permute-start(f32[3,5,8,128]{3,2,1,0:T(8,128)S(1)} %pad_maximum_fusion.1), channel_id=1, source_target_pairs={{0,192},{64,0},{128,64},{192,128},{1,193},{65,1},{129,65},{193,129... | collective-permute-start | bytes 184328 | tf_op jit(solution)/shard_map/ppermute | solution.py:537
  14.0 1.9 %side.1.acc_in_ref = f32[4,2,2,8,256]{4,3,2,1,0:T(8,128)S(1)} custom-call(f32[2,5,8,128]{3,2,1,0:T(8,128)S(1)} %collective-permute-done.side_ref, bf16[4,5,4,64,128]{4,3,2,1,0:T(8,128)(2,1)S(1)} %get-tuple-element.18.own_ref, f32[4,2,2,8,256]{4,3,2,1,0:T(8,128)S(1)} %get-tuple-element.19.acc_in_ref), custom_call_target="tpu_custom_call" | custom-call | flops 1000000000 | bytes 1000000 | tf_op jit(solution)/shard_map/side/pallas_call | solution.py:538
  15.9 0.0 collective-permute-done.1.low_ref
  15.9 0.0 collective-permute-done.2.high_ref
  15.9 4.1 %outer.1 = f32[32,8,128]{2,1,0:T(8,128)S(1)} custom-call(f32[4,5,8,128]{3,2,1,0:T(8,128)S(1)} %get-tuple-element.13.feat_ref, f32[3,5,8,128]{3,2,1,0:T(8,128)S(1)} %collective-permute-done.1.low_ref, f32[3,5,8,128]{3,2,1,0:T(8,128)S(1)} %collective-permute-done.2.high_ref, bf16[4,5,4,64,128]{4,3,2,1,0:T(8,128)(2,1)S(1)} %get-tuple-element.18.own_ref, ...), custom_call_target="tpu_custom_call" | custom-call | tf_op jit(solution)/shard_map/outer/pallas_call | solution.py:552
  20.1 19.9 %all_to_all.5.got_ref = f32[32,8,128]{2,1,0:T(8,128)S(1)} all-to-all(f32[32,8,128]{2,1,0:T(8,128)S(1)} %outer.1), channel_id=1, replica_groups=mesh['px'=4,'py'=2,'fr'=32] {'fr'}, dimensions={0} | all-to-all | bytes 262144 | tf_op jit(solution)/shard_map/all_to_all | solution.py:567
  39.9 1.9 %bin.1 = f32[13,2,2,720]{3,2,1,0:T(2,128)} custom-call(f32[32,8,128]{2,1,0:T(8,128)S(1)} %all_to_all.5.got_ref), custom_call_target="tpu_custom_call" | custom-call | tf_op jit(solution)/shard_map/bin/pallas_call | solution.py:569
  (4 shorter events, 0.0 us)
Async XLA Ops:
  1.7 9.5 %collective-permute-start = (f32[2,5,8,128]{3,2,1,0:T(8,128)S(1)}, f32[2,5,8,128]{3,2,1,0:T(8,128)S(1)}, u32[]{:S(2)}, u32[]{:S(2)}) collective-permute-start(f32[2,5,8,128]{3,2,1,0:T(8,128)S(1)} %get-tuple-element.14), channel_id=1, source_target_pairs={{0,32},{32,0},{1,33},{33,1},{2,34},{34,2},{3,35},{35,3},{4,36},{36... | collective-permute-start | bytes 122888 | tf_op jit(solution)/shard_map/ppermute | solution.py:512
  11.2 4.7 %collective-permute-start.1 = (f32[3,5,8,128]{3,2,1,0:T(8,128)S(1)}, f32[3,5,8,128]{3,2,1,0:T(8,128)S(1)}, u32[]{:S(2)}, u32[]{:S(2)}) collective-permute-start(f32[3,5,8,128]{3,2,1,0:T(8,128)S(1)} %pad_maximum_fusion), channel_id=1, source_target_pairs={{0,64},{64,128},{128,192},{192,0},{1,65},{65,129},{129,193},{193,1... | collective-permute-start | bytes 184328 | tf_op jit(solution)/shard_map/ppermute | solution.py:536
  12.5 3.4 %collective-permute-start.2 = (f32[3,5,8,128]{3,2,1,0:T(8,128)S(1)}, f32[3,5,8,128]{3,2,1,0:T(8,128)S(1)}, u32[]{:S(2)}, u32[]{:S(2)}) collective-permute-start(f32[3,5,8,128]{3,2,1,0:T(8,128)S(1)} %pad_maximum_fusion.1), channel_id=1, source_target_pairs={{0,192},{64,0},{128,64},{192,128},{1,193},{65,1},{129,65},{193,129... | collective-permute-start | bytes 184328 | tf_op jit(solution)/shard_map/ppermute | solution.py:537

commit v3 on v2

--- a/solution.py
+++ b/solution.py
@@ -137,7 +137,9 @@
     share = CELL_XY * CELL_XY * SLAB // 32
     band = (lax.broadcasted_iota(jnp.int32, (total, 128), 1) // 4 * share).astype(F32)
     for number, value in enumerate((quat_w, quat_x, quat_y, quat_z, sorted_ref[7], voxel - band)):
-        comp_ref[number] = value
+        comp_ref[:, number, :] = value
+    comp_ref[:, 6, :] = jnp.zeros((total, 128), F32)
+    comp_ref[:, 7, :] = jnp.zeros((total, 128), F32)
 
     table = jnp.concatenate(
         [packed_ref[table_at + k, 0:1, :] for k in range(3)] + [jnp.zeros((5, 128), F32)], axis=0
@@ -175,10 +177,13 @@
     first, second, third = split3(base)
     number = lax.broadcasted_iota(jnp.int32, (8, 128), 0)
     ones = jnp.where(number < 3, 1.0, 0.0).astype(F32)
-    stacked = jnp.concatenate(
+    return jnp.concatenate(
         [first, first, first, second, second, third, ones, jnp.zeros((8, 128), F32)], axis=0
     )
-    return stacked.T.astype(BF16)
+
+
+def pair_rows(base, other):
+    return jnp.concatenate([partner_rows(base), partner_rows(other)], axis=0).T.astype(BF16)
 
 
 def water_partner(value, shift, absent):
@@ -186,16 +191,17 @@
     mx, my, mz = value[3:4], value[4:5], value[5:6]
     n = x * x + y * y + z * z + FAR * ((1.0 - value[6:7]) + absent)
     e = mx * x + my * y + mz * z
-    return partner_rows(jnp.concatenate([x, y, z, mx, my, mz, n, e], axis=0))
+    return jnp.concatenate([x, y, z, mx, my, mz, n, e], axis=0)
 
 
 def solute_partner(value, shift, absent):
     x, y, z, charge = value[0:1] + shift[0], value[1:2] + shift[1], value[2:3], value[5:6]
     n = x * x + y * y + z * z + FAR * ((1.0 - value[6:7]) + absent)
-    base = jnp.concatenate([x, y, z, charge * x, charge * y, charge * z, n, charge], axis=0)
-    lower = jnp.broadcast_to(value[3:4], (128, 128)).T
-    upper = jnp.broadcast_to(value[4:5], (128, 128)).T
-    return partner_rows(base), lower, upper
+    return jnp.concatenate([x, y, z, charge * x, charge * y, charge * z, n, charge], axis=0)
+
+
+def solute_levels(value):
+    return (jnp.broadcast_to(value[k : k + 1], (128, 128)).T for k in (3, 4))
 
 
 def own_side(value):
@@ -203,7 +209,7 @@
     mx, my, mz = value[3:4], value[4:5], value[5:6]
     zero = jnp.zeros((1, 128), F32)
     one = jnp.ones((1, 128), F32)
-    n = x * x + y * y + z * z + P_SOFT
+    n = x * x + y * y + z * z + P_SOFT + FAR * (1.0 - value[6:7])
     c = mx * x + my * y + mz * z
     kd3 = 3.0 * KD
     sides = (
@@ -235,31 +241,39 @@
 CHUNK = 16
 
 
-def water_pairs(acc, p, al, ao, ab):
-    for k in range(p.shape[0] // CHUNK):
-        part = slice(k * CHUNK, (k + 1) * CHUNK)
-        pk = p[part]
-        root = lax.rsqrt(pk)
-        u = root * root
-        u15 = u * root
-        window = jnp.maximum(P_END - pk, 0.0)
-        inner = u15 * (u15 * u15 - 1.0) + (al[part] - ao[part] * ab[part] * u)
-        acc = fold(acc, u15 * inner * (window * window))
+def water_energy(p, al, ao, ab):
+    root = lax.rsqrt(p)
+    u = root * root
+    u15 = u * root
+    window = jnp.maximum(P_END - p, 0.0)
+    inner = u15 * (u15 * u15 - 1.0) + (al - ao * ab * u)
+    return u15 * inner * (window * window)
+
+
+def solute_energy(p, charge, lower, upper):
+    root = lax.rsqrt(p)
+    u15 = root * root * root
+    window = jnp.maximum(P_END - p, 0.0)
+    inner = u15 * (upper * (u15 * u15) - lower) + charge
+    return u15 * inner * (window * window)
+
+
+def chunks(rows):
+    return [slice(k * CHUNK, (k + 1) * CHUNK) for k in range(rows // CHUNK)]
+
+
+def water_pairs(acc, values):
+    for part in chunks(values[0].shape[0]):
+        acc = fold(acc, water_energy(*[value[part] for value in values]))
     return acc
 
 
 def solute_pairs(acc, p, charge, lower, upper):
-    for k in range(p.shape[0] // CHUNK):
-        part = slice(k * CHUNK, (k + 1) * CHUNK)
-        pk = p[part]
-        root = lax.rsqrt(pk)
-        u15 = root * root * root
-        window = jnp.maximum(P_END - pk, 0.0)
+    for part in chunks(p.shape[0]):
         low, high = lower[part], upper[part]
-        if low.shape[1] != pk.shape[1]:
+        if low.shape[1] != p.shape[1]:
             low, high = jnp.concatenate([low] * 2, axis=1), jnp.concatenate([high] * 2, axis=1)
-        inner = u15 * (high * (u15 * u15) - low) + charge[part]
-        acc = fold(acc, u15 * inner * (window * window))
+        acc = fold(acc, solute_energy(p[part], charge[part], low, high))
     return acc
 
 
@@ -267,157 +281,212 @@
     return jnp.dot(left, right, preferred_element_type=F32)
 
 
-def inner_kernel(feat_ref, comp_ref, acc_ref, rec_ref, own_ref, left_ref, coef_ref):
+def only(side, number):
+    parts = [side, jnp.zeros_like(side)]
+    return jnp.concatenate(parts if number == 0 else parts[::-1], axis=0)
+
+
+def each(left, right):
+    top = jnp.concatenate([left, jnp.zeros_like(right)], axis=1)
+    bottom = jnp.concatenate([jnp.zeros_like(left), right], axis=1)
+    return jnp.concatenate([top, bottom], axis=0)
+
+
+def crossed(left, right):
+    top = jnp.concatenate([jnp.zeros_like(left), right], axis=1)
+    bottom = jnp.concatenate([left, jnp.zeros_like(right)], axis=1)
+    return jnp.concatenate([top, bottom], axis=0)
+
+
+def halves_of(column, f, feat_ref):
+    first, second = feat_ref[2 * column, f], feat_ref[2 * column + 1, f]
+    return (
+        jnp.concatenate([first[:, :64], second[:, :64]], axis=1),
+        jnp.concatenate([first[:, 64:], second[:, 64:]], axis=1),
+    )
+
+
+def inner_kernel(feat_ref, acc_ref, other_ref, own_ref, left_ref, sum_ref):
     frames = feat_ref.shape[1] - 1
-    for cell in range(4):
-        rows, lower, upper = solute_partner(feat_ref[cell, frames], (0.0, 0.0), 0.0)
-        left_ref[frames, cell] = rows
-        coef_ref[cell, 0] = lower
-        coef_ref[cell, 1] = upper
+    for i in range(2):
         for f in range(frames):
-            left_ref[f, cell] = water_partner(feat_ref[cell, f], (0.0, 0.0), 0.0)
-            for q, side in enumerate(own_side(feat_ref[cell, f])):
-                own_ref[f, q, cell] = side
+            left_ref[f, i] = pair_rows(
+                water_partner(feat_ref[2 * i, f], (0.0, 0.0), 0.0),
+                water_partner(feat_ref[2 * i + 1, f], (0.0, 0.0), 0.0),
+            )
+            lower, upper = (own_side(half) for half in halves_of(i, f, feat_ref))
+            for q in range(5):
+                own_ref[f, q, i] = jnp.concatenate([lower[q], upper[q]], axis=1)
 
     @pl.loop(0, frames)
     def _(f):
         for i in range(2):
-            sides = [
-                jnp.concatenate([own_ref[f, q, 2 * i], own_ref[f, q, 2 * i + 1]], axis=1)
-                for q in range(5)
-            ]
-            acc_w = jnp.zeros((8, 256), F32)
-            acc_s = jnp.zeros((8, 256), F32)
-            for cell in range(4):
-                left = left_ref[f, cell]
-                acc_w = water_pairs(acc_w, *[dot(left, sides[q]) for q in range(4)])
-                left = left_ref[frames, cell]
-                acc_s = solute_pairs(
-                    acc_s, dot(left, sides[0]), dot(left, sides[4]), coef_ref[cell, 0], coef_ref[cell, 1]
+            sides = [own_ref[f, q, i] for q in range(4)]
+            acc = jnp.zeros((8, 256), F32)
+            left = left_ref[f, i]
+            for j in range(2):
+                acc = water_pairs(acc, [dot(left, only(side, j)) for side in sides])
+            if i == 0:
+                near = left_ref[f, 1, 0:64]
+                for j in range(2):
+                    values = [dot(near, only(side, j)) for side in sides]
+                    for part in chunks(64):
+                        energy = water_energy(*[value[part] for value in values])
+                        acc = fold(acc, energy)
+                        sum_ref[f, j, part] = energy[:, :128] + energy[:, 128:]
+                far = left_ref[f, 1, 64:128]
+                values = [dot(far, each(side[:, 128:], side[:, 128:])) for side in sides]
+                late = jnp.zeros((8, 256), F32)
+                for part in chunks(64):
+                    energy = water_energy(*[value[part] for value in values])
+                    late = fold(late, energy)
+                    rows = slice(64 + part.start, 64 + part.stop)
+                    sum_ref[f, 0, rows] = energy[:, :128]
+                    sum_ref[f, 1, rows] = energy[:, 128:]
+                acc = acc + jnp.concatenate(
+                    [jnp.zeros((8, 128), F32), late[:, :128] + late[:, 128:]], axis=1
                 )
-            acc_ref[f, i, 0] = acc_w
-            acc_ref[f, i, 1] = acc_s
-
-    filled = comp_ref[4]
-    rows = {0: filled, 13: comp_ref[5]}
-    for number, (a, b) in enumerate(pair_index):
-        rows[3 + number] = comp_ref[a] * comp_ref[b] * filled
-    rec_ref[...] = jnp.zeros_like(rec_ref)
-    for number, value in rows.items():
-        rec_ref[:, number, :] = value
-
-
-def side_kernel(side_ref, own_ref, acc_in_ref, acc_ref, left_ref, coef_ref):
+            acc_ref[f, i] = acc
+        for j in range(2):
+            other_ref[f, j] = fold(jnp.zeros((8, 128), F32), sum_ref[f, j].T)
+
+
+def to_facing():
+    return jnp.where(lax.axis_index("py") == 0, 1.0, -1.0).astype(F32) * (2.0 * CUTOFF * UNIT)
+
+
+def side_kernel(
+    feat_ref, side_ref, own_ref, acc_ref, wall_ref, face_ref,
+    solute_ref, left_ref, coef_ref,
+):
     frames = side_ref.shape[1] - 1
-    py = lax.axis_index("py")
-    facing = 1 - py
-    width = 2.0 * CUTOFF * UNIT
-    to_side = jnp.where(py == 0, width, -width).astype(F32)
-    for cell in range(2):
-        rows, lower, upper = solute_partner(side_ref[cell, frames], (0.0, to_side), 0.0)
-        left_ref[frames, cell] = rows
-        coef_ref[cell, 0] = lower
-        coef_ref[cell, 1] = upper
-        for f in range(frames):
-            left_ref[f, cell] = water_partner(side_ref[cell, f], (0.0, to_side), 0.0)
-    upper_row = (facing == 1).astype(F32)
+    facing = 1 - lax.axis_index("py")
+    shift = (0.0, to_facing())
+    for i in range(2):
+        atoms = [feat_ref[2 * i + j, frames] for j in range(2)]
+        solute_ref[i] = pair_rows(*[solute_partner(value, (0.0, 0.0), 0.0) for value in atoms])
+        for j in range(2):
+            coef_ref[2 * i + j, 0], coef_ref[2 * i + j, 1] = solute_levels(atoms[j])
+    solute_ref[2] = pair_rows(*[solute_partner(side_ref[k, frames], shift, 0.0) for k in range(2)])
+    for k in range(2):
+        coef_ref[4 + k, 0], coef_ref[4 + k, 1] = solute_levels(side_ref[k, frames])
+    for f in range(frames):
+        left_ref[f] = pair_rows(*[water_partner(side_ref[k, f], shift, 0.0) for k in range(2)])
+        first, second = own_side(feat_ref[facing, f]), own_side(feat_ref[2 + facing, f])
+        for q in range(5):
+            face_ref[f, q] = jnp.concatenate([first[q], second[q]], axis=1)
 
     @pl.loop(0, frames)
     def _(f):
-        sides = [
-            jnp.concatenate([own_ref[f, q, facing], own_ref[f, q, 2 + facing]], axis=1)
-            for q in range(5)
-        ]
-        acc_w = jnp.zeros((8, 256), F32)
-        acc_s = jnp.zeros((8, 256), F32)
-        for cell in range(2):
-            left = left_ref[f, cell]
-            acc_w = water_pairs(acc_w, *[dot(left, sides[q]) for q in range(4)])
-            left = left_ref[frames, cell]
-            acc_s = solute_pairs(
-                acc_s, dot(left, sides[0]), dot(left, sides[4]), coef_ref[cell, 0], coef_ref[cell, 1]
+        for i in range(2):
+            sides = [own_ref[f, q, i] for q in (0, 4)]
+            acc = jnp.zeros((8, 256), F32)
+            for column in range(2):
+                left = solute_ref[column]
+                for j in range(2):
+                    cell = 2 * column + j
+                    acc = solute_pairs(
+                        acc, *[dot(left, only(side, j)) for side in sides],
+                        coef_ref[cell, 0], coef_ref[cell, 1],
+                    )
+            acc_ref[f, i] = acc
+        faces = [face_ref[f, q] for q in range(5)]
+        water = jnp.zeros((8, 256), F32)
+        solute = jnp.zeros((8, 256), F32)
+        for meet, order in ((each, (4, 5)), (crossed, (5, 4))):
+            sides = [meet(face[:, :128], face[:, 128:]) for face in faces]
+            water = water_pairs(water, [dot(left_ref[f], side) for side in sides[:4]])
+            levels = [
+                jnp.concatenate([coef_ref[order[0], k], coef_ref[order[1], k]], axis=1) for k in range(2)
+            ]
+            solute = solute_pairs(
+                solute, *[dot(solute_ref[2], sides[q]) for q in (0, 4)], *levels
             )
-        for i in range(2):
-            for number, acc in ((0, acc_w), (1, acc_s)):
-                mine = acc[:, i * 128 : (i + 1) * 128]
-                acc_ref[f, i, number] = acc_in_ref[f, i, number] + jnp.concatenate(
-                    [mine * (1.0 - upper_row), mine * upper_row], axis=1
-                )
+        wall_ref[f, 0] = water
+        wall_ref[f, 1] = solute
 
 
 def outer_kernel(
-    feat_ref, low_ref, high_ref, own_ref, acc_in_ref, rec_in_ref, send_ref,
-    left_ref, coef_ref, acc_ref, rec_ref,
+    feat_ref, low_ref, high_ref, own_ref, face_ref, water_ref, other_ref, solute_in_ref, wall_in_ref,
+    comp_ref, send_ref, left_ref, solute_ref, coef_ref, acc_ref, wall_ref, rec_ref,
 ):
     frames = feat_ref.shape[1] - 1
     px = lax.axis_index("px")
-    py = lax.axis_index("py")
-    last = lax.axis_size("px") - 1
-    facing = 1 - py
     width = 2.0 * CUTOFF * UNIT
-    to_side = jnp.where(py == 0, width, -width).astype(F32)
+    across = to_facing()
     no_low = jnp.where(px == 0, 1.0, 0.0).astype(F32)
-    no_high = jnp.where(px == last, 1.0, 0.0).astype(F32)
-    halo = [(low_ref, k, (-width, to_side if k == 2 else 0.0), no_low) for k in range(3)] + [
-        (high_ref, k, (width, to_side if k == 2 else 0.0), no_high) for k in range(3)
-    ]
-    for cell, (ref, k, shift, absent) in enumerate(halo):
-        rows, lower, upper = solute_partner(ref[k, frames], shift, absent)
-        left_ref[frames, cell] = rows
-        coef_ref[cell, 0] = lower
-        coef_ref[cell, 1] = upper
+    no_high = jnp.where(px == lax.axis_size("px") - 1, 1.0, 0.0).astype(F32)
+    low = ((-width, 0.0), no_low)
+    high = ((width, 0.0), no_high)
+    pairs = (
+        ((low_ref, 0, *low), (low_ref, 1, *low)),
+        ((high_ref, 0, *high), (high_ref, 1, *high)),
+        ((low_ref, 2, (-width, across), no_low), (high_ref, 2, (width, across), no_high)),
+    )
+    for number, pair in enumerate(pairs):
+        solute_ref[number] = pair_rows(
+            *[solute_partner(ref[k, frames], shift, absent) for ref, k, shift, absent in pair]
+        )
+        for place, (ref, k, _, _) in enumerate(pair):
+            cell = 2 * number + place
+            coef_ref[cell, 0], coef_ref[cell, 1] = solute_levels(ref[k, frames])
         for f in range(frames):
-            left_ref[f, cell] = water_partner(ref[k, f], shift, absent)
-    upper_row = (facing == 1).astype(F32)
+            left_ref[f, number] = pair_rows(
+                *[water_partner(ref[k, f], shift, absent) for ref, k, shift, absent in pair]
+            )
 
     @pl.loop(0, frames)
     def _(f):
-        def both(source, q):
-            return jnp.concatenate(
-                [
-                    dot(left_ref[source, 2], own_ref[f, q, facing]),
-                    dot(left_ref[source, 5], own_ref[f, q, 2 + facing]),
-                ],
-                axis=1,
+        faces = [face_ref[f, q] for q in range(5)]
+        sides = [each(face[:, :128], face[:, 128:]) for face in faces]
+        wall_ref[f, 0] = water_pairs(
+            wall_in_ref[f, 0], [dot(left_ref[f, 2], side) for side in sides[:4]]
+        )
+        levels = [jnp.concatenate([coef_ref[4, k], coef_ref[5, k]], axis=1) for k in range(2)]
+        wall_ref[f, 1] = solute_pairs(
+            wall_in_ref[f, 1], *[dot(solute_ref[2], sides[q]) for q in (0, 4)], *levels
+        )
+        for i in range(2):
+            sides = [own_ref[f, q, i] for q in range(5)]
+            full, part = (slice(64, 128), slice(0, 64)) if i == 0 else (slice(0, 64), slice(64, 128))
+            lanes = slice(0, 128) if i == 0 else slice(128, 256)
+            water = water_ref[f, i]
+            for j in range(2):
+                water = water_pairs(
+                    water, [dot(left_ref[f, i, full], only(side, j)) for side in sides[:4]]
+                )
+            late = water_pairs(
+                jnp.zeros((8, 256), F32),
+                [dot(left_ref[f, i, part], each(side[:, lanes], side[:, lanes])) for side in sides[:4]],
             )
-
-        zero = jnp.zeros((8, 256), F32)
-        corner_w = water_pairs(zero, *[both(f, q) for q in range(4)])
-        lower, upper = (
-            jnp.concatenate([coef_ref[2, k], coef_ref[5, k]], axis=1) for k in range(2)
-        )
-        corner_s = solute_pairs(zero, both(frames, 0), both(frames, 4), lower, upper)
-        for i in range(2):
-            sides = [
-                jnp.concatenate([own_ref[f, q, 2 * i], own_ref[f, q, 2 * i + 1]], axis=1)
-                for q in range(5)
-            ]
-            start = []
-            for number, acc in ((0, corner_w), (1, corner_s)):
-                mine = acc[:, i * 128 : (i + 1) * 128]
-                start.append(
-                    acc_in_ref[f, i, number]
-                    + jnp.concatenate([mine * (1.0 - upper_row), mine * upper_row], axis=1)
+            late = [late[:, :128] + late[:, 128:], jnp.zeros((8, 128), F32)]
+            acc_ref[f, i, 0] = water + jnp.concatenate(late if i == 0 else late[::-1], axis=1)
+            solute = solute_in_ref[f, i]
+            for j in range(2):
+                cell = 2 * i + j
+                solute = solute_pairs(
+                    solute, *[dot(solute_ref[i], only(sides[q], j)) for q in (0, 4)],
+                    coef_ref[cell, 0], coef_ref[cell, 1],
                 )
-            acc_w, acc_s = start
-            for cell in (3 * i, 3 * i + 1):
-                left = left_ref[f, cell]
-                acc_w = water_pairs(acc_w, *[dot(left, sides[q]) for q in range(4)])
-                left = left_ref[frames, cell]
-                acc_s = solute_pairs(
-                    acc_s, dot(left, sides[0]), dot(left, sides[4]), coef_ref[cell, 0], coef_ref[cell, 1]
-                )
-            acc_ref[f, i, 0] = acc_w
-            acc_ref[f, i, 1] = acc_s
-
-    rec_ref[...] = rec_in_ref[...]
+            acc_ref[f, i, 1] = solute
+
+    rec_ref[...] = comp_ref[...]
     self_root = P_SOFT**-0.5
     self_u15 = self_root**3
-    for i in range(2):
-        for f in range(frames):
-            water = jnp.sum(acc_ref[f, i, 0], axis=0, keepdims=True)
-            solute = jnp.sum(acc_ref[f, i, 1], axis=0, keepdims=True)
+    facing = 1 - lax.axis_index("py")
+    for f in range(frames):
+        walls = [jnp.sum(wall_ref[f, k], axis=0, keepdims=True) for k in range(2)]
+        for i in range(2):
+            sums = [jnp.sum(acc_ref[f, i, k], axis=0, keepdims=True) for k in range(2)]
             for j in range(2):
+                near = (facing == j).astype(F32)
+                water, solute = (
+                    jnp.concatenate([value[:, 64 * j : 64 * j + 64], value[:, 128 + 64 * j : 192 + 64 * j]], axis=1)
+                    + near * wall[:, 128 * i : 128 * i + 128]
+                    for value, wall in zip(sums, walls)
+                )
+                if i == 1:
+                    water = water + jnp.sum(other_ref[f, j], axis=0, keepdims=True)
                 value = feat_ref[2 * i + j, f]
                 filled = value[6:7]
                 moment = value[3:4] * value[3:4] + value[4:5] * value[4:5] + value[5:6] * value[5:6]
@@ -425,26 +494,31 @@
                     self_u15 * (self_u15 * self_u15 - 1.0) + KD * moment
                 )
                 fc = (2 * i + j) * frames + f
-                part = slice(j * 128, (j + 1) * 128)
-                rec_ref[fc, 1:2, :] = filled * (SCALE_SW * solute[:, part])
-                rec_ref[fc, 2:3, :] = filled * (SCALE_WW * (water[:, part] - own))
-    for i in range(2):
-        block = rec_ref[8 * i : 8 * i + 8].reshape(128, 128).T
-        send_ref[:, 4 * i : 4 * i + 4, :] = block.reshape(32, 4, 128)
-
-
-def bin_kernel(frame_total, got_ref, out_ref):
+                rec_ref[fc, 6:7, :] = filled * (SCALE_SW * solute)
+                rec_ref[fc, 7:8, :] = filled * (SCALE_WW * (water - own))
+    send_ref[...] = rec_ref[...].reshape(128, 128).T.reshape(send_ref.shape)
+
+
+def bin_kernel(frame_total, got_ref, out_ref, field_ref, rec_ref):
     share = out_ref.shape[-1]
     number = lax.broadcasted_iota(jnp.int32, (share, 128), 0).astype(F32)
+    field_ref[...] = got_ref[...].reshape(128, 128).T.reshape(field_ref.shape)
+    filled = field_ref[:, 4, :]
+    quaternion = [field_ref[:, k, :] for k in range(4)]
+    rec_ref[:, 0, :] = filled
+    rec_ref[:, 1, :] = field_ref[:, 6, :]
+    rec_ref[:, 2, :] = field_ref[:, 7, :]
+    for k, (a, b) in enumerate(pair_index):
+        rec_ref[:, 3 + k, :] = quaternion[a] * quaternion[b] * filled
+    for k in range(13, 16):
+        rec_ref[:, k, :] = jnp.zeros_like(filled)
     for i in range(2):
-        block = got_ref[:, 4 * i : 4 * i + 4, :].reshape(128, 128).T
         for j in range(2):
             totals = jnp.zeros((48, share), F32)
             for f in range(4):
-                start = (j * 4 + f) * 16
-                record = block[start : start + 16]
-                chosen = jnp.where(number == record[13:14], 1.0, 0.0).astype(BF16)
-                parts = jnp.concatenate(split3(record), axis=0).astype(BF16)
+                fc = (2 * i + j) * 4 + f
+                chosen = jnp.where(number == field_ref[fc, 5:6, :], 1.0, 0.0).astype(BF16)
+                parts = jnp.concatenate(split3(rec_ref[fc]), axis=0).astype(BF16)
                 totals = totals + lax.dot_general(
                     parts, chosen, (((1,), (1,)), ((), ())), preferred_element_type=F32
                 )
@@ -496,7 +570,7 @@
         out_shape=(
             jax.ShapeDtypeStruct((4, frames + 1, 8, 128), F32),
             jax.ShapeDtypeStruct((2, frames + 1, 8, 128), F32),
-            jax.ShapeDtypeStruct((6, total, 128), F32),
+            jax.ShapeDtypeStruct((total, 8, 128), F32),
         ),
         in_specs=[vmem()],
         out_specs=(vmem(),) * 3,
@@ -511,58 +585,66 @@
 
     side = lax.ppermute(side_out, "py", [(0, 1), (1, 0)])
 
-    acc_shape = jax.ShapeDtypeStruct((frames, 2, 2, 8, 256), F32)
-    acc, rec, own = pl.pallas_call(
+    work = pl.CostEstimate(flops=10**9, bytes_accessed=10**6, transcendentals=0)
+    column_shape = jax.ShapeDtypeStruct((frames, 2, 8, 256), F32)
+    water, other, own = pl.pallas_call(
         inner_kernel,
         out_shape=(
-            acc_shape,
-            jax.ShapeDtypeStruct((total, 16, 128), F32),
-            jax.ShapeDtypeStruct((frames, 5, 4, ROWS, 128), BF16),
+            column_shape,
+            jax.ShapeDtypeStruct((frames, 2, 8, 128), F32),
+            jax.ShapeDtypeStruct((frames, 5, 2, ROWS, 256), BF16),
         ),
-        in_specs=[vmem()] * 2,
+        in_specs=[vmem()],
         out_specs=(vmem(),) * 3,
         scratch_shapes=[
-            pltpu.VMEM((frames + 1, 4, 128, ROWS), BF16),
-            pltpu.VMEM((4, 2, 128, 128), F32),
+            pltpu.VMEM((frames, 2, 128, 2 * ROWS), BF16),
+            pltpu.VMEM((frames, 2, 128, 128), F32),
         ],
         compiler_params=PARAMS,
-        cost_estimate=pl.CostEstimate(flops=10**9, bytes_accessed=10**6, transcendentals=0),
+        cost_estimate=work,
         name="inner",
-    )(feat, comp)
-
-    side, acc = lax.optimization_barrier((side, acc))
+    )(feat)
+
+    side, water = lax.optimization_barrier((side, water))
     up = [(k, (k + 1) % cols) for k in range(cols)]
     down = [(k, (k - 1) % cols) for k in range(cols)]
     low = lax.ppermute(jnp.concatenate([feat[2:4], side[1:2]], axis=0), "px", up)
     high = lax.ppermute(jnp.concatenate([feat[0:2], side[0:1]], axis=0), "px", down)
-    acc = pl.pallas_call(
+    solute, wall, face = pl.pallas_call(
         side_kernel,
-        out_shape=acc_shape,
+        out_shape=(
+            column_shape,
+            column_shape,
+            jax.ShapeDtypeStruct((frames, 5, ROWS, 256), BF16),
+        ),
         in_specs=[vmem()] * 3,
+        out_specs=(vmem(),) * 3,
+        scratch_shapes=[
+            pltpu.VMEM((3, 128, 2 * ROWS), BF16),
+            pltpu.VMEM((frames, 128, 2 * ROWS), BF16),
+            pltpu.VMEM((6, 2, 128, 128), F32),
+        ],
+        compiler_params=PARAMS,
+        cost_estimate=work,
+        name="side",
+    )(feat, side, own)
+
+    send = pl.pallas_call(
+        outer_kernel,
+        out_shape=jax.ShapeDtypeStruct((ranks, 4, 128), F32),
+        in_specs=[vmem()] * 10,
         out_specs=vmem(),
         scratch_shapes=[
-            pltpu.VMEM((frames + 1, 2, 128, ROWS), BF16),
-            pltpu.VMEM((2, 2, 128, 128), F32),
-        ],
-        compiler_params=PARAMS,
-        cost_estimate=pl.CostEstimate(flops=10**9, bytes_accessed=10**6, transcendentals=0),
-        name="side",
-    )(side, own, acc)
-
-    send = pl.pallas_call(
-        outer_kernel,
-        out_shape=jax.ShapeDtypeStruct((ranks, 8, 128), F32),
-        in_specs=[vmem()] * 6,
-        out_specs=vmem(),
-        scratch_shapes=[
-            pltpu.VMEM((frames + 1, 6, 128, ROWS), BF16),
+            pltpu.VMEM((frames, 3, 128, 2 * ROWS), BF16),
+            pltpu.VMEM((3, 128, 2 * ROWS), BF16),
             pltpu.VMEM((6, 2, 128, 128), F32),
             pltpu.VMEM((frames, 2, 2, 8, 256), F32),
-            pltpu.VMEM((total, 16, 128), F32),
+            pltpu.VMEM((frames, 2, 8, 256), F32),
+            pltpu.VMEM((total, 8, 128), F32),
         ],
         compiler_params=PARAMS,
         name="outer",
-    )(feat, low, high, own, acc, rec)
+    )(feat, low, high, own, face, water, other, solute, wall, comp)
 
     got = lax.all_to_all(send, "fr", 0, 0, tiled=True)
     share = CELL_XY * CELL_XY * SLAB // ranks
@@ -571,6 +653,7 @@
         out_shape=jax.ShapeDtypeStruct((13, 2, 2, share), F32),
         in_specs=[vmem()],
         out_specs=vmem(),
+        scratch_shapes=[pltpu.VMEM((total, 8, 128), F32), pltpu.VMEM((total, 16, 128), F32)],
         compiler_params=PARAMS,
         name="bin",
     )(got)

time: 42 us -> 39.9 us (0.950)
  Pallas kernels: 14.4 us -> 13.2 us
  blocking collectives: 19.9 us -> 18.9 us
    pallas_call x3, Pallas kernels: 11.7 us -> 10.5 us  [the longest x1 4.13 us: shards(): pl.pallas_call(side_kernel, out_shape=(column_shape, column_shape, jax.Sh...]
    all_to_all x1, blocking collectives: 19.9 us -> 18.9 us  [shards(): got = lax.all_to_all(send, 'fr', 0, 0, tiled=True)]
  transfers between devices with their start and end apart: 3 -> 3, of which waited for: 0 -> 0; matrix products, arithmetic and copies ran while one was open for 0% -> 0% of each run, Pallas kernels for 18% -> 17%
where the time goes in v3:
time: 39.9 us; the launch traced here: 39.7 us
  blocking collectives  18.9 us (47%)
  Pallas kernels  13.2 us (33%)
  starting transfers between devices  6.58 us (16%)
  other arithmetic  0.9 us (2%)
    all_to_all x1, blocking collectives, shards(): got = lax.all_to_all(send, 'fr', 0, 0, tiled=True)  18.9 us
    pallas_call x1, Pallas kernels, shards(): pl.pallas_call(side_kernel, out_shape=(column_shape, column_shape, jax.Sh...  4.13 us
    ppermute x1, starting transfers between devices, shards(): side = lax.ppermute(side_out, 'py', [(0, 1), (1, 0)])  3.83 us
    pallas_call x1, Pallas kernels, shards(): pl.pallas_call(outer_kernel, out_shape=jax.ShapeDtypeStruct((ranks, 4, 12...  3.72 us
    pallas_call x1, Pallas kernels, shards(): pl.pallas_call(inner_kernel, out_shape=(column_shape, jax.ShapeDtypeStruc...  2.63 us
    pallas_call x1, Pallas kernels, shards(): pl.pallas_call(functools.partial(bin_kernel, frames * ranks), out_shape=j...  1.93 us
    ppermute x1, starting transfers between devices, shards(): lax.ppermute(jnp.concatenate([feat[0:2], side[0:1]], axis=0), 'px', down)  1.47 us
    ppermute x1, starting transfers between devices, shards(): lax.ppermute(jnp.concatenate([feat[2:4], side[1:2]], axis=0), 'px', up)  1.29 us
  transfers between devices with their start and end apart: 3, of which 0 were waited for; matrix products, arithmetic and copies ran while one was open for 0% of the time, Pallas kernels for 17%

profile of v3, /device:TPU:1, one launch (start us, length us, event | category | flops | bytes accessed | tf_op | source)
XLA Modules:
  0.0 39.7 jit_solution(16438569272249428540)
XLA Ops:
  0.0 0.9 %convert_add_fusion.packed_ref = f32[69,2,128]{2,1,0:T(2,128)S(1)} fusion(s32[2,2,4]{2,1,0:T(2,128)} %bitcast.18, s32[2,2,128]{2,1,0:T(2,128)} %param.14, s32[8,2,128]{2,1,0:T(2,128)} %bitcast.16, f32[1,1,32]{2,1,0:T(1,128)} %bitcast.19, f32[1,1,32]{2,1,0:T(1,128)} %bitcast.20, f32[1,1,32]{2,1,0:T(1,128)} %bitcast.21, f32[6,2,128]{2,1,0:T(2,128)} %bitcast.17, ...), kind=kLoop, calls=%fused_computation | loop fusion | flops 158976 | bytes 136640 | tf_op jit(solution)/shard_map/add | solution.py:567
  0.9 0.8 %prepare.1 = (f32[4,5,8,128]{3,2,1,0:T(8,128)S(1)}, f32[2,5,8,128]{3,2,1,0:T(8,128)S(1)}, f32[16,8,128]{2,1,0:T(8,128)S(1)}) custom-call(f32[69,2,128]{2,1,0:T(2,128)S(1)} %convert_add_fusion.packed_ref), custom_call_target="tpu_custom_call" | custom-call | tf_op jit(solution)/shard_map/prepare/pallas_call | solution.py:568
  1.7 3.8 %collective-permute-start = (f32[2,5,8,128]{3,2,1,0:T(8,128)S(1)}, f32[2,5,8,128]{3,2,1,0:T(8,128)S(1)}, u32[]{:S(2)}, u32[]{:S(2)}) collective-permute-start(f32[2,5,8,128]{3,2,1,0:T(8,128)S(1)} %get-tuple-element.17), channel_id=1, source_target_pairs={{0,32},{32,0},{1,33},{33,1},{2,34},{34,2},{3,35},{35,3},{4,36},{36... | collective-permute-start | bytes 122888 | tf_op jit(solution)/shard_map/ppermute | solution.py:586
  5.5 2.6 %inner.1 = (f32[4,2,8,256]{3,2,1,0:T(8,128)S(1)}, f32[4,2,8,128]{3,2,1,0:T(8,128)S(1)}, bf16[4,5,2,64,256]{4,3,2,1,0:T(8,128)(2,1)S(1)}) custom-call(f32[4,5,8,128]{3,2,1,0:T(8,128)S(1)} %get-tuple-element.16.feat_ref), custom_call_target="tpu_custom_call" | custom-call | flops 1000000000 | bytes 1000000 | tf_op jit(solution)/shard_map/inner/pallas_call | solution.py:590
  8.2 0.0 collective-permute-done.side_ref
  8.2 1.3 %collective-permute-start.1 = (f32[3,5,8,128]{3,2,1,0:T(8,128)S(1)}, f32[3,5,8,128]{3,2,1,0:T(8,128)S(1)}, u32[]{:S(2)}, u32[]{:S(2)}) collective-permute-start(f32[3,5,8,128]{3,2,1,0:T(8,128)S(1)} %pad_maximum_fusion), channel_id=1, source_target_pairs={{0,64},{64,128},{128,192},{192,0},{1,65},{65,129},{129,193},{193,1... | collective-permute-start | bytes 184328 | tf_op jit(solution)/shard_map/ppermute | solution.py:611
  9.5 1.5 %collective-permute-start.2 = (f32[3,5,8,128]{3,2,1,0:T(8,128)S(1)}, f32[3,5,8,128]{3,2,1,0:T(8,128)S(1)}, u32[]{:S(2)}, u32[]{:S(2)}) collective-permute-start(f32[3,5,8,128]{3,2,1,0:T(8,128)S(1)} %pad_maximum_fusion.1), channel_id=1, source_target_pairs={{0,192},{64,0},{128,64},{192,128},{1,193},{65,1},{129,65},{193,129... | collective-permute-start | bytes 184328 | tf_op jit(solution)/shard_map/ppermute | solution.py:612
  11.0 4.1 %side.1 = (f32[4,2,8,256]{3,2,1,0:T(8,128)S(1)}, f32[4,2,8,256]{3,2,1,0:T(8,128)S(1)}, bf16[4,5,64,256]{3,2,1,0:T(8,128)(2,1)S(1)}) custom-call(f32[4,5,8,128]{3,2,1,0:T(8,128)S(1)} %get-tuple-element.16.feat_ref, f32[2,5,8,128]{3,2,1,0:T(8,128)S(1)} %collective-permute-done.side_ref, bf16[4,5,2,64,256]{4,3,2,1,0:T(8,128)(2,1)S(1)} %get-tuple-element.20.own_ref), custom_call_target="tpu_custom_call" | custom-call | flops 1000000000 | bytes 1000000 | tf_op jit(solution)/shard_map/side/pallas_call | solution.py:613
  15.1 0.0 collective-permute-done.1.low_ref
  15.1 0.0 collective-permute-done.2.high_ref
  15.1 3.7 %outer.1 = f32[32,4,128]{2,1,0:T(4,128)S(1)} custom-call(f32[4,5,8,128]{3,2,1,0:T(8,128)S(1)} %get-tuple-element.16.feat_ref, f32[3,5,8,128]{3,2,1,0:T(8,128)S(1)} %collective-permute-done.1.low_ref, f32[3,5,8,128]{3,2,1,0:T(8,128)S(1)} %collective-permute-done.2.high_ref, bf16[4,5,2,64,256]{4,3,2,1,0:T(8,128)(2,1)S(1)} %get-tuple-element.20.own_ref, ...), custom_call_target="tpu_custom_call" | custom-call | tf_op jit(solution)/shard_map/outer/pallas_call | solution.py:632
  18.8 18.9 %all_to_all.5.got_ref = f32[32,4,128]{2,1,0:T(4,128)S(1)} all-to-all(f32[32,4,128]{2,1,0:T(4,128)S(1)} %outer.1), channel_id=1, replica_groups=mesh['px'=4,'py'=2,'fr'=32] {'fr'}, dimensions={0} | all-to-all | bytes 131072 | tf_op jit(solution)/shard_map/all_to_all | solution.py:649
  37.8 1.9 %bin.1 = f32[13,2,2,720]{3,2,1,0:T(2,128)} custom-call(f32[32,4,128]{2,1,0:T(4,128)S(1)} %all_to_all.5.got_ref), custom_call_target="tpu_custom_call" | custom-call | tf_op jit(solution)/shard_map/bin/pallas_call | solution.py:651
  (4 shorter events, 0.0 us)
Async XLA Ops:
  1.7 6.5 %collective-permute-start = (f32[2,5,8,128]{3,2,1,0:T(8,128)S(1)}, f32[2,5,8,128]{3,2,1,0:T(8,128)S(1)}, u32[]{:S(2)}, u32[]{:S(2)}) collective-permute-start(f32[2,5,8,128]{3,2,1,0:T(8,128)S(1)} %get-tuple-element.17), channel_id=1, source_target_pairs={{0,32},{32,0},{1,33},{33,1},{2,34},{34,2},{3,35},{35,3},{4,36},{36... | collective-permute-start | bytes 122888 | tf_op jit(solution)/shard_map/ppermute | solution.py:586
  8.2 6.9 %collective-permute-start.1 = (f32[3,5,8,128]{3,2,1,0:T(8,128)S(1)}, f32[3,5,8,128]{3,2,1,0:T(8,128)S(1)}, u32[]{:S(2)}, u32[]{:S(2)}) collective-permute-start(f32[3,5,8,128]{3,2,1,0:T(8,128)S(1)} %pad_maximum_fusion), channel_id=1, source_target_pairs={{0,64},{64,128},{128,192},{192,0},{1,65},{65,129},{129,193},{193,1... | collective-permute-start | bytes 184328 | tf_op jit(solution)/shard_map/ppermute | solution.py:611
  9.5 5.6 %collective-permute-start.2 = (f32[3,5,8,128]{3,2,1,0:T(8,128)S(1)}, f32[3,5,8,128]{3,2,1,0:T(8,128)S(1)}, u32[]{:S(2)}, u32[]{:S(2)}) collective-permute-start(f32[3,5,8,128]{3,2,1,0:T(8,128)S(1)} %pad_maximum_fusion.1), channel_id=1, source_target_pairs={{0,192},{64,0},{128,64},{192,128},{1,193},{65,1},{129,65},{193,129... | collective-permute-start | bytes 184328 | tf_op jit(solution)/shard_map/ppermute | solution.py:612

commit v4 on v3

--- a/solution.py
+++ b/solution.py
@@ -501,7 +501,8 @@
 
 def bin_kernel(frame_total, got_ref, out_ref, field_ref, rec_ref):
     share = out_ref.shape[-1]
-    number = lax.broadcasted_iota(jnp.int32, (share, 128), 0).astype(F32)
+    groups = -(-share // 128)
+    number = lax.broadcasted_iota(jnp.int32, (128, 128), 0).astype(F32)
     field_ref[...] = got_ref[...].reshape(128, 128).T.reshape(field_ref.shape)
     filled = field_ref[:, 4, :]
     quaternion = [field_ref[:, k, :] for k in range(4)]
@@ -514,18 +515,27 @@
         rec_ref[:, k, :] = jnp.zeros_like(filled)
     for i in range(2):
         for j in range(2):
-            totals = jnp.zeros((48, share), F32)
+            totals = jnp.zeros((48 * groups, 128), F32)
             for f in range(4):
                 fc = (2 * i + j) * 4 + f
-                chosen = jnp.where(number == field_ref[fc, 5:6, :], 1.0, 0.0).astype(BF16)
-                parts = jnp.concatenate(split3(rec_ref[fc]), axis=0).astype(BF16)
+                voxel = field_ref[fc, 5:6, :]
+                group = jnp.floor((voxel + 0.5) * (1.0 / 128.0))
+                chosen = jnp.where(number == voxel - 128.0 * group, 1.0, 0.0).astype(BF16)
+                parts = jnp.concatenate(split3(rec_ref[fc]), axis=0)
+                parts = jnp.concatenate(
+                    [jnp.where(group == k, parts, 0.0) for k in range(groups)], axis=0
+                ).astype(BF16)
                 totals = totals + lax.dot_general(
                     parts, chosen, (((1,), (1,)), ((), ())), preferred_element_type=F32
                 )
-            summed = totals[0:16] + totals[16:32] + totals[32:48]
-            counted = summed[0:1]
-            out_ref[0:1, i, j, :] = counted * (1.0 / (frame_total * rho_bulk * spacing**3))
-            out_ref[1:13, i, j, :] = summed[1:13] / jnp.maximum(counted, 1.0)
+            for k in range(groups):
+                lanes = min(128, share - 128 * k)
+                part = totals[48 * k : 48 * k + 48]
+                summed = (part[0:16] + part[16:32] + part[32:48])[:, :lanes]
+                counted = summed[0:1]
+                span = slice(128 * k, 128 * k + lanes)
+                out_ref[0:1, i, j, span] = counted * (1.0 / (frame_total * rho_bulk * spacing**3))
+                out_ref[1:13, i, j, span] = summed[1:13] / jnp.maximum(counted, 1.0)
 
 
 def vmem():

time: 39.9 us -> 39.2 us (0.982)
  Pallas kernels: 13.2 us -> 12.6 us
    pallas_call x1, Pallas kernels: 1.93 us -> 1.3 us  [shards(): pl.pallas_call(functools.partial(bin_kernel, frames * ranks), out_shape=j...]
where the time goes in v4:
time: 39.2 us; the launch traced here: 39.1 us
  blocking collectives  18.9 us (48%)
  Pallas kernels  12.6 us (32%)
  starting transfers between devices  6.58 us (17%)
  other arithmetic  0.9 us (2%)
    all_to_all x1, blocking collectives, shards(): got = lax.all_to_all(send, 'fr', 0, 0, tiled=True)  18.9 us
    pallas_call x1, Pallas kernels, shards(): pl.pallas_call(side_kernel, out_shape=(column_shape, column_shape, jax.Sh...  4.13 us
    ppermute x1, starting transfers between devices, shards(): side = lax.ppermute(side_out, 'py', [(0, 1), (1, 0)])  3.83 us
    pallas_call x1, Pallas kernels, shards(): pl.pallas_call(outer_kernel, out_shape=jax.ShapeDtypeStruct((ranks, 4, 12...  3.72 us
    pallas_call x1, Pallas kernels, shards(): pl.pallas_call(inner_kernel, out_shape=(column_shape, jax.ShapeDtypeStruc...  2.63 us
    ppermute x1, starting transfers between devices, shards(): lax.ppermute(jnp.concatenate([feat[0:2], side[0:1]], axis=0), 'px', down)  1.47 us
    pallas_call x1, Pallas kernels, shards(): pl.pallas_call(functools.partial(bin_kernel, frames * ranks), out_shape=j...  1.3 us
    ppermute x1, starting transfers between devices, shards(): lax.ppermute(jnp.concatenate([feat[2:4], side[1:2]], axis=0), 'px', up)  1.29 us
  transfers between devices with their start and end apart: 3, of which 0 were waited for; matrix products, arithmetic and copies ran while one was open for 0% of the time, Pallas kernels for 17%

profile of v4, /device:TPU:1, one launch (start us, length us, event | category | flops | bytes accessed | tf_op | source)
XLA Modules:
  0.0 39.1 jit_solution(15950810260092446848)
XLA Ops:
  0.0 0.9 %convert_add_fusion.packed_ref = f32[69,2,128]{2,1,0:T(2,128)S(1)} fusion(s32[2,2,4]{2,1,0:T(2,128)} %bitcast.18, s32[2,2,128]{2,1,0:T(2,128)} %param.14, s32[8,2,128]{2,1,0:T(2,128)} %bitcast.16, f32[1,1,32]{2,1,0:T(1,128)} %bitcast.19, f32[1,1,32]{2,1,0:T(1,128)} %bitcast.20, f32[1,1,32]{2,1,0:T(1,128)} %bitcast.21, f32[6,2,128]{2,1,0:T(2,128)} %bitcast.17, ...), kind=kLoop, calls=%fused_computation | loop fusion | flops 158976 | bytes 136640 | tf_op jit(solution)/shard_map/add | solution.py:577
  0.9 0.8 %prepare.1 = (f32[4,5,8,128]{3,2,1,0:T(8,128)S(1)}, f32[2,5,8,128]{3,2,1,0:T(8,128)S(1)}, f32[16,8,128]{2,1,0:T(8,128)S(1)}) custom-call(f32[69,2,128]{2,1,0:T(2,128)S(1)} %convert_add_fusion.packed_ref), custom_call_target="tpu_custom_call" | custom-call | tf_op jit(solution)/shard_map/prepare/pallas_call | solution.py:578
  1.7 3.8 %collective-permute-start = (f32[2,5,8,128]{3,2,1,0:T(8,128)S(1)}, f32[2,5,8,128]{3,2,1,0:T(8,128)S(1)}, u32[]{:S(2)}, u32[]{:S(2)}) collective-permute-start(f32[2,5,8,128]{3,2,1,0:T(8,128)S(1)} %get-tuple-element.17), channel_id=1, source_target_pairs={{0,32},{32,0},{1,33},{33,1},{2,34},{34,2},{3,35},{35,3},{4,36},{36... | collective-permute-start | bytes 122888 | tf_op jit(solution)/shard_map/ppermute | solution.py:596
  5.5 2.6 %inner.1 = (f32[4,2,8,256]{3,2,1,0:T(8,128)S(1)}, f32[4,2,8,128]{3,2,1,0:T(8,128)S(1)}, bf16[4,5,2,64,256]{4,3,2,1,0:T(8,128)(2,1)S(1)}) custom-call(f32[4,5,8,128]{3,2,1,0:T(8,128)S(1)} %get-tuple-element.16.feat_ref), custom_call_target="tpu_custom_call" | custom-call | flops 1000000000 | bytes 1000000 | tf_op jit(solution)/shard_map/inner/pallas_call | solution.py:600
  8.2 0.0 collective-permute-done.side_ref
  8.2 1.3 %collective-permute-start.1 = (f32[3,5,8,128]{3,2,1,0:T(8,128)S(1)}, f32[3,5,8,128]{3,2,1,0:T(8,128)S(1)}, u32[]{:S(2)}, u32[]{:S(2)}) collective-permute-start(f32[3,5,8,128]{3,2,1,0:T(8,128)S(1)} %pad_maximum_fusion), channel_id=1, source_target_pairs={{0,64},{64,128},{128,192},{192,0},{1,65},{65,129},{129,193},{193,1... | collective-permute-start | bytes 184328 | tf_op jit(solution)/shard_map/ppermute | solution.py:621
  9.5 1.5 %collective-permute-start.2 = (f32[3,5,8,128]{3,2,1,0:T(8,128)S(1)}, f32[3,5,8,128]{3,2,1,0:T(8,128)S(1)}, u32[]{:S(2)}, u32[]{:S(2)}) collective-permute-start(f32[3,5,8,128]{3,2,1,0:T(8,128)S(1)} %pad_maximum_fusion.1), channel_id=1, source_target_pairs={{0,192},{64,0},{128,64},{192,128},{1,193},{65,1},{129,65},{193,129... | collective-permute-start | bytes 184328 | tf_op jit(solution)/shard_map/ppermute | solution.py:622
  11.0 4.1 %side.1 = (f32[4,2,8,256]{3,2,1,0:T(8,128)S(1)}, f32[4,2,8,256]{3,2,1,0:T(8,128)S(1)}, bf16[4,5,64,256]{3,2,1,0:T(8,128)(2,1)S(1)}) custom-call(f32[4,5,8,128]{3,2,1,0:T(8,128)S(1)} %get-tuple-element.16.feat_ref, f32[2,5,8,128]{3,2,1,0:T(8,128)S(1)} %collective-permute-done.side_ref, bf16[4,5,2,64,256]{4,3,2,1,0:T(8,128)(2,1)S(1)} %get-tuple-element.20.own_ref), custom_call_target="tpu_custom_call" | custom-call | flops 1000000000 | bytes 1000000 | tf_op jit(solution)/shard_map/side/pallas_call | solution.py:623
  15.1 0.0 collective-permute-done.1.low_ref
  15.1 0.0 collective-permute-done.2.high_ref
  15.1 3.7 %outer.1 = f32[32,4,128]{2,1,0:T(4,128)S(1)} custom-call(f32[4,5,8,128]{3,2,1,0:T(8,128)S(1)} %get-tuple-element.16.feat_ref, f32[3,5,8,128]{3,2,1,0:T(8,128)S(1)} %collective-permute-done.1.low_ref, f32[3,5,8,128]{3,2,1,0:T(8,128)S(1)} %collective-permute-done.2.high_ref, bf16[4,5,2,64,256]{4,3,2,1,0:T(8,128)(2,1)S(1)} %get-tuple-element.20.own_ref, ...), custom_call_target="tpu_custom_call" | custom-call | tf_op jit(solution)/shard_map/outer/pallas_call | solution.py:642
  18.8 18.9 %all_to_all.5.got_ref = f32[32,4,128]{2,1,0:T(4,128)S(1)} all-to-all(f32[32,4,128]{2,1,0:T(4,128)S(1)} %outer.1), channel_id=1, replica_groups=mesh['px'=4,'py'=2,'fr'=32] {'fr'}, dimensions={0} | all-to-all | bytes 131072 | tf_op jit(solution)/shard_map/all_to_all | solution.py:659
  37.8 1.3 %bin.1 = f32[13,2,2,720]{3,2,1,0:T(2,128)} custom-call(f32[32,4,128]{2,1,0:T(4,128)S(1)} %all_to_all.5.got_ref), custom_call_target="tpu_custom_call" | custom-call | tf_op jit(solution)/shard_map/bin/pallas_call | solution.py:661
  (4 shorter events, 0.0 us)
Async XLA Ops:
  1.7 6.5 %collective-permute-start = (f32[2,5,8,128]{3,2,1,0:T(8,128)S(1)}, f32[2,5,8,128]{3,2,1,0:T(8,128)S(1)}, u32[]{:S(2)}, u32[]{:S(2)}) collective-permute-start(f32[2,5,8,128]{3,2,1,0:T(8,128)S(1)} %get-tuple-element.17), channel_id=1, source_target_pairs={{0,32},{32,0},{1,33},{33,1},{2,34},{34,2},{3,35},{35,3},{4,36},{36... | collective-permute-start | bytes 122888 | tf_op jit(solution)/shard_map/ppermute | solution.py:596
  8.2 6.9 %collective-permute-start.1 = (f32[3,5,8,128]{3,2,1,0:T(8,128)S(1)}, f32[3,5,8,128]{3,2,1,0:T(8,128)S(1)}, u32[]{:S(2)}, u32[]{:S(2)}) collective-permute-start(f32[3,5,8,128]{3,2,1,0:T(8,128)S(1)} %pad_maximum_fusion), channel_id=1, source_target_pairs={{0,64},{64,128},{128,192},{192,0},{1,65},{65,129},{129,193},{193,1... | collective-permute-start | bytes 184328 | tf_op jit(solution)/shard_map/ppermute | solution.py:621
  9.5 5.6 %collective-permute-start.2 = (f32[3,5,8,128]{3,2,1,0:T(8,128)S(1)}, f32[3,5,8,128]{3,2,1,0:T(8,128)S(1)}, u32[]{:S(2)}, u32[]{:S(2)}) collective-permute-start(f32[3,5,8,128]{3,2,1,0:T(8,128)S(1)} %pad_maximum_fusion.1), channel_id=1, source_target_pairs={{0,192},{64,0},{128,64},{192,128},{1,193},{65,1},{129,65},{193,129... | collective-permute-start | bytes 184328 | tf_op jit(solution)/shard_map/ppermute | solution.py:622

commit v5 on v4

--- a/solution.py
+++ b/solution.py
@@ -31,6 +31,9 @@
 SCALE_WW = 0.5 * 4.0 * eps_water / (P_CUT * P_CUT)
 SCALE_SW = 1.0 / (P_CUT * P_CUT)
 FAR = 1.0e4
+MONO = 96
+P_ROWS, Q_ROWS, M_ROWS = slice(0, 64), slice(64, 128), slice(128, 224)
+OWN_ROWS, HELD_ROWS = 224, 320
 ROWS = 64
 
 
@@ -183,15 +186,47 @@
 
 
 def pair_rows(base, other):
-    return jnp.concatenate([partner_rows(base), partner_rows(other)], axis=0).T.astype(BF16)
+    return jnp.concatenate([partner_rows(base), partner_rows(other)], axis=0).astype(BF16).T
+
+
+def moment_rows(base, other):
+    parts = []
+    for value in (base, other):
+        first, second, third = split3(value)
+        parts += [first, first, first, second, second, third]
+    return jnp.concatenate(parts, axis=0).astype(BF16).T
+
+
+def moved_water(value, shift):
+    x, y, z = value[0:1] + shift[0], value[1:2] + shift[1], value[2:3]
+    return (x, y, z), (value[3:4], value[4:5], value[5:6])
 
 
 def water_partner(value, shift, absent):
-    x, y, z = value[0:1] + shift[0], value[1:2] + shift[1], value[2:3]
-    mx, my, mz = value[3:4], value[4:5], value[5:6]
+    (x, y, z), _ = moved_water(value, shift)
     n = x * x + y * y + z * z + FAR * ((1.0 - value[6:7]) + absent)
-    e = mx * x + my * y + mz * z
-    return jnp.concatenate([x, y, z, mx, my, mz, n, e], axis=0)
+    zero = jnp.zeros((3, 128), F32)
+    return jnp.concatenate([x, y, z, zero, n, zero[0:1]], axis=0)
+
+
+def moment_partner(value, shift):
+    place, moment = moved_water(value, shift)
+    n = place[0] * place[0] + place[1] * place[1] + place[2] * place[2]
+    e = moment[0] * place[0] + moment[1] * place[1] + moment[2] * place[2]
+    rows = [moment[a] * n - 3.0 * place[a] * e for a in range(3)] + list(moment)
+    rows += [3.0 * place[a] * moment[b] - 2.0 * moment[a] * place[b] for a in range(3) for b in range(3)]
+    return jnp.concatenate(rows + [3.0 * e], axis=0)
+
+
+def own_moments(value):
+    place = (value[0:1], value[1:2], value[2:3])
+    moment = (value[3:4], value[4:5], value[5:6])
+    n = place[0] * place[0] + place[1] * place[1] + place[2] * place[2] + P_SOFT
+    c = moment[0] * place[0] + moment[1] * place[1] + moment[2] * place[2]
+    rows = list(moment) + [moment[a] * n - 3.0 * c * place[a] for a in range(3)]
+    rows += [moment[a] * place[b] for a in range(3) for b in range(3)]
+    first, second, third = split3(KD * jnp.concatenate(rows + [c], axis=0))
+    return jnp.concatenate([first, second, third, first, second, first], axis=0).astype(BF16)
 
 
 def solute_partner(value, shift, absent):
@@ -211,12 +246,8 @@
     one = jnp.ones((1, 128), F32)
     n = x * x + y * y + z * z + P_SOFT + FAR * (1.0 - value[6:7])
     c = mx * x + my * y + mz * z
-    kd3 = 3.0 * KD
     sides = (
         ([-2.0 * x, -2.0 * y, -2.0 * z, zero, zero, zero, one, zero], n),
-        ([zero, zero, zero, KD * mx, KD * my, KD * mz, zero, zero], None),
-        ([mx, my, mz, zero, zero, zero, zero, zero], -c),
-        ([zero, zero, zero, -kd3 * x, -kd3 * y, -kd3 * z, zero, kd3 * one], None),
         ([zero, zero, zero, KQ * mx, KQ * my, KQ * mz, zero, -KQ * c], None),
     )
     out = []
@@ -226,10 +257,16 @@
             last = jnp.zeros((16, 128), F32)
         else:
             last = jnp.concatenate(list(split3(term)) + [jnp.zeros((13, 128), F32)], axis=0)
-        out.append(
-            jnp.concatenate([first, second, third, first, second, first, last], axis=0).astype(BF16)
-        )
-    return out
+        out += [first, second, third, first, second, first, last]
+    return jnp.concatenate([jnp.concatenate(out, axis=0).astype(BF16), own_moments(value)], axis=0)
+
+
+def run_frames(frames, set_up, frame):
+    set_up(0)
+    for f in range(frames):
+        if f + 1 < frames:
+            set_up(f + 1)
+        frame(f)
 
 
 def fold(acc, value):
@@ -241,12 +278,12 @@
 CHUNK = 16
 
 
-def water_energy(p, al, ao, ab):
+def water_energy(p, moments):
     root = lax.rsqrt(p)
     u = root * root
     u15 = u * root
     window = jnp.maximum(P_END - p, 0.0)
-    inner = u15 * (u15 * u15 - 1.0) + (al - ao * ab * u)
+    inner = u15 * (u15 * u15 - 1.0) + moments * u
     return u15 * inner * (window * window)
 
 
@@ -306,36 +343,39 @@
     )
 
 
-def inner_kernel(feat_ref, acc_ref, other_ref, own_ref, left_ref, sum_ref):
+def inner_kernel(feat_ref, acc_ref, other_ref, own_ref, left_ref, mono_ref, sum_ref):
     frames = feat_ref.shape[1] - 1
-    for i in range(2):
-        for f in range(frames):
+    def set_up(f):
+        for i in range(2):
             left_ref[f, i] = pair_rows(
-                water_partner(feat_ref[2 * i, f], (0.0, 0.0), 0.0),
-                water_partner(feat_ref[2 * i + 1, f], (0.0, 0.0), 0.0),
-            )
-            lower, upper = (own_side(half) for half in halves_of(i, f, feat_ref))
-            for q in range(5):
-                own_ref[f, q, i] = jnp.concatenate([lower[q], upper[q]], axis=1)
-
-    @pl.loop(0, frames)
-    def _(f):
+                *[water_partner(feat_ref[2 * i + j, f], (0.0, 0.0), 0.0) for j in range(2)]
+            )
+            mono_ref[f, i] = moment_rows(
+                *[moment_partner(feat_ref[2 * i + j, f], (0.0, 0.0)) for j in range(2)]
+            )
+            own_ref[f, i, 0:OWN_ROWS] = jnp.concatenate(
+                [own_side(half) for half in halves_of(i, f, feat_ref)], axis=1
+            )
+
+    def frame(f):
         for i in range(2):
-            sides = [own_ref[f, q, i] for q in range(4)]
+            sides = (own_ref[f, i, P_ROWS], own_ref[f, i, M_ROWS])
             acc = jnp.zeros((8, 256), F32)
-            left = left_ref[f, i]
+            lefts = (left_ref[f, i], mono_ref[f, i])
             for j in range(2):
-                acc = water_pairs(acc, [dot(left, only(side, j)) for side in sides])
+                acc = water_pairs(acc, [dot(left, only(side, j)) for left, side in zip(lefts, sides)])
             if i == 0:
-                near = left_ref[f, 1, 0:64]
+                near = (left_ref[f, 1, 0:64], mono_ref[f, 1, 0:64])
                 for j in range(2):
-                    values = [dot(near, only(side, j)) for side in sides]
+                    values = [dot(left, only(side, j)) for left, side in zip(near, sides)]
                     for part in chunks(64):
                         energy = water_energy(*[value[part] for value in values])
                         acc = fold(acc, energy)
                         sum_ref[f, j, part] = energy[:, :128] + energy[:, 128:]
-                far = left_ref[f, 1, 64:128]
-                values = [dot(far, each(side[:, 128:], side[:, 128:])) for side in sides]
+                far = (left_ref[f, 1, 64:128], mono_ref[f, 1, 64:128])
+                values = [
+                    dot(left, each(side[:, 128:], side[:, 128:])) for left, side in zip(far, sides)
+                ]
                 late = jnp.zeros((8, 256), F32)
                 for part in chunks(64):
                     energy = water_energy(*[value[part] for value in values])
@@ -350,6 +390,8 @@
         for j in range(2):
             other_ref[f, j] = fold(jnp.zeros((8, 128), F32), sum_ref[f, j].T)
 
+    run_frames(frames, set_up, frame)
+
 
 def to_facing():
     return jnp.where(lax.axis_index("py") == 0, 1.0, -1.0).astype(F32) * (2.0 * CUTOFF * UNIT)
@@ -357,7 +399,7 @@
 
 def side_kernel(
     feat_ref, side_ref, own_ref, acc_ref, wall_ref, face_ref,
-    solute_ref, left_ref, coef_ref,
+    solute_ref, left_ref, mono_ref, coef_ref,
 ):
     frames = side_ref.shape[1] - 1
     facing = 1 - lax.axis_index("py")
@@ -370,16 +412,16 @@
     solute_ref[2] = pair_rows(*[solute_partner(side_ref[k, frames], shift, 0.0) for k in range(2)])
     for k in range(2):
         coef_ref[4 + k, 0], coef_ref[4 + k, 1] = solute_levels(side_ref[k, frames])
-    for f in range(frames):
+    def set_up(f):
         left_ref[f] = pair_rows(*[water_partner(side_ref[k, f], shift, 0.0) for k in range(2)])
-        first, second = own_side(feat_ref[facing, f]), own_side(feat_ref[2 + facing, f])
-        for q in range(5):
-            face_ref[f, q] = jnp.concatenate([first[q], second[q]], axis=1)
-
-    @pl.loop(0, frames)
-    def _(f):
+        mono_ref[f] = moment_rows(*[moment_partner(side_ref[k, f], shift) for k in range(2)])
+        face_ref[f, 0:OWN_ROWS] = jnp.concatenate(
+            [own_side(feat_ref[facing, f]), own_side(feat_ref[2 + facing, f])], axis=1
+        )
+
+    def frame(f):
         for i in range(2):
-            sides = [own_ref[f, q, i] for q in (0, 4)]
+            sides = [own_ref[f, i, P_ROWS], own_ref[f, i, Q_ROWS]]
             acc = jnp.zeros((8, 256), F32)
             for column in range(2):
                 left = solute_ref[column]
@@ -390,25 +432,27 @@
                         coef_ref[cell, 0], coef_ref[cell, 1],
                     )
             acc_ref[f, i] = acc
-        faces = [face_ref[f, q] for q in range(5)]
+        faces = [face_ref[f, rows] for rows in (P_ROWS, Q_ROWS, M_ROWS)]
         water = jnp.zeros((8, 256), F32)
         solute = jnp.zeros((8, 256), F32)
         for meet, order in ((each, (4, 5)), (crossed, (5, 4))):
             sides = [meet(face[:, :128], face[:, 128:]) for face in faces]
-            water = water_pairs(water, [dot(left_ref[f], side) for side in sides[:4]])
+            water = water_pairs(water, [dot(left_ref[f], sides[0]), dot(mono_ref[f], sides[2])])
             levels = [
                 jnp.concatenate([coef_ref[order[0], k], coef_ref[order[1], k]], axis=1) for k in range(2)
             ]
             solute = solute_pairs(
-                solute, *[dot(solute_ref[2], sides[q]) for q in (0, 4)], *levels
+                solute, *[dot(solute_ref[2], sides[q]) for q in range(2)], *levels
             )
         wall_ref[f, 0] = water
         wall_ref[f, 1] = solute
 
+    run_frames(frames, set_up, frame)
+
 
 def outer_kernel(
     feat_ref, low_ref, high_ref, own_ref, face_ref, water_ref, other_ref, solute_in_ref, wall_in_ref,
-    comp_ref, send_ref, left_ref, solute_ref, coef_ref, acc_ref, wall_ref, rec_ref,
+    comp_ref, send_ref, left_ref, mono_ref, solute_ref, coef_ref, acc_ref, wall_ref, rec_ref,
 ):
     frames = feat_ref.shape[1] - 1
     px = lax.axis_index("px")
@@ -430,34 +474,45 @@
         for place, (ref, k, _, _) in enumerate(pair):
             cell = 2 * number + place
             coef_ref[cell, 0], coef_ref[cell, 1] = solute_levels(ref[k, frames])
-        for f in range(frames):
+
+    def set_up(f):
+        for number, pair in enumerate(pairs):
             left_ref[f, number] = pair_rows(
                 *[water_partner(ref[k, f], shift, absent) for ref, k, shift, absent in pair]
             )
-
-    @pl.loop(0, frames)
-    def _(f):
-        faces = [face_ref[f, q] for q in range(5)]
+            mono_ref[f, number] = moment_rows(
+                *[moment_partner(ref[k, f], shift) for ref, k, shift, _ in pair]
+            )
+
+    def frame(f):
+        faces = [face_ref[f, rows] for rows in (P_ROWS, Q_ROWS, M_ROWS)]
         sides = [each(face[:, :128], face[:, 128:]) for face in faces]
         wall_ref[f, 0] = water_pairs(
-            wall_in_ref[f, 0], [dot(left_ref[f, 2], side) for side in sides[:4]]
+            wall_in_ref[f, 0], [dot(left_ref[f, 2], sides[0]), dot(mono_ref[f, 2], sides[2])]
         )
         levels = [jnp.concatenate([coef_ref[4, k], coef_ref[5, k]], axis=1) for k in range(2)]
         wall_ref[f, 1] = solute_pairs(
-            wall_in_ref[f, 1], *[dot(solute_ref[2], sides[q]) for q in (0, 4)], *levels
+            wall_in_ref[f, 1], *[dot(solute_ref[2], sides[q]) for q in range(2)], *levels
         )
         for i in range(2):
-            sides = [own_ref[f, q, i] for q in range(5)]
+            sides = [own_ref[f, i, rows] for rows in (P_ROWS, Q_ROWS, M_ROWS)]
             full, part = (slice(64, 128), slice(0, 64)) if i == 0 else (slice(0, 64), slice(64, 128))
             lanes = slice(0, 128) if i == 0 else slice(128, 256)
             water = water_ref[f, i]
             for j in range(2):
                 water = water_pairs(
-                    water, [dot(left_ref[f, i, full], only(side, j)) for side in sides[:4]]
+                    water,
+                    [
+                        dot(left_ref[f, i, full], only(sides[0], j)),
+                        dot(mono_ref[f, i, full], only(sides[2], j)),
+                    ],
                 )
             late = water_pairs(
                 jnp.zeros((8, 256), F32),
-                [dot(left_ref[f, i, part], each(side[:, lanes], side[:, lanes])) for side in sides[:4]],
+                [
+                    dot(left_ref[f, i, part], each(sides[0][:, lanes], sides[0][:, lanes])),
+                    dot(mono_ref[f, i, part], each(sides[2][:, lanes], sides[2][:, lanes])),
+                ],
             )
             late = [late[:, :128] + late[:, 128:], jnp.zeros((8, 128), F32)]
             acc_ref[f, i, 0] = water + jnp.concatenate(late if i == 0 else late[::-1], axis=1)
@@ -465,11 +520,12 @@
             for j in range(2):
                 cell = 2 * i + j
                 solute = solute_pairs(
-                    solute, *[dot(solute_ref[i], only(sides[q], j)) for q in (0, 4)],
+                    solute, *[dot(solute_ref[i], only(sides[q], j)) for q in range(2)],
                     coef_ref[cell, 0], coef_ref[cell, 1],
                 )
             acc_ref[f, i, 1] = solute
 
+    run_frames(frames, set_up, frame)
     rec_ref[...] = comp_ref[...]
     self_root = P_SOFT**-0.5
     self_u15 = self_root**3
@@ -602,12 +658,13 @@
         out_shape=(
             column_shape,
             jax.ShapeDtypeStruct((frames, 2, 8, 128), F32),
-            jax.ShapeDtypeStruct((frames, 5, 2, ROWS, 256), BF16),
+            jax.ShapeDtypeStruct((frames, 2, HELD_ROWS, 256), BF16),
         ),
         in_specs=[vmem()],
         out_specs=(vmem(),) * 3,
         scratch_shapes=[
             pltpu.VMEM((frames, 2, 128, 2 * ROWS), BF16),
+            pltpu.VMEM((frames, 2, 128, 2 * MONO), BF16),
             pltpu.VMEM((frames, 2, 128, 128), F32),
         ],
         compiler_params=PARAMS,
@@ -625,13 +682,14 @@
         out_shape=(
             column_shape,
             column_shape,
-            jax.ShapeDtypeStruct((frames, 5, ROWS, 256), BF16),
+            jax.ShapeDtypeStruct((frames, HELD_ROWS, 256), BF16),
         ),
         in_specs=[vmem()] * 3,
         out_specs=(vmem(),) * 3,
         scratch_shapes=[
             pltpu.VMEM((3, 128, 2 * ROWS), BF16),
             pltpu.VMEM((frames, 128, 2 * ROWS), BF16),
+            pltpu.VMEM((frames, 128, 2 * MONO), BF16),
             pltpu.VMEM((6, 2, 128, 128), F32),
         ],
         compiler_params=PARAMS,
@@ -646,6 +704,7 @@
         out_specs=vmem(),
         scratch_shapes=[
             pltpu.VMEM((frames, 3, 128, 2 * ROWS), BF16),
+            pltpu.VMEM((frames, 3, 128, 2 * MONO), BF16),
             pltpu.VMEM((3, 128, 2 * ROWS), BF16),
             pltpu.VMEM((6, 2, 128, 128), F32),
             pltpu.VMEM((frames, 2, 2, 8, 256), F32),

time: 39.2 us -> 38 us (0.969)
  Pallas kernels: 12.6 us -> 10.7 us
  blocking collectives: 18.9 us -> 19.5 us
    pallas_call x1, Pallas kernels: 4.13 us -> 3.49 us  [shards(): pl.pallas_call(side_kernel, out_shape=(column_shape, column_shape, jax.Sh...]
    pallas_call x1, Pallas kernels: 3.72 us -> 3.11 us  [shards(): pl.pallas_call(outer_kernel, out_shape=jax.ShapeDtypeStruct((ranks, 4, 12...]
    pallas_call x1, Pallas kernels: 2.63 us -> 2.03 us  [shards(): pl.pallas_call(inner_kernel, out_shape=(column_shape, jax.ShapeDtypeStruc...]
    all_to_all x1, blocking collectives: 18.9 us -> 19.5 us  [shards(): got = lax.all_to_all(send, 'fr', 0, 0, tiled=True)]
  transfers between devices with their start and end apart: 3 -> 3, of which waited for: 0 -> 0; matrix products, arithmetic and copies ran while one was open for 0% -> 0% of each run, Pallas kernels for 17% -> 15%
where the time goes in v5:
time: 38 us; the launch traced here: 37.8 us
  blocking collectives  19.5 us (51%)
  Pallas kernels  10.7 us (28%)
  starting transfers between devices  6.58 us (17%)
  other arithmetic  0.9 us (2%)
    all_to_all x1, blocking collectives, shards(): got = lax.all_to_all(send, 'fr', 0, 0, tiled=True)  19.5 us
    ppermute x1, starting transfers between devices, shards(): side = lax.ppermute(side_out, 'py', [(0, 1), (1, 0)])  3.83 us
    pallas_call x1, Pallas kernels, shards(): pl.pallas_call(side_kernel, out_shape=(column_shape, column_shape, jax.Sh...  3.49 us
    pallas_call x1, Pallas kernels, shards(): pl.pallas_call(outer_kernel, out_shape=jax.ShapeDtypeStruct((ranks, 4, 12...  3.11 us
    pallas_call x1, Pallas kernels, shards(): pl.pallas_call(inner_kernel, out_shape=(column_shape, jax.ShapeDtypeStruc...  2.03 us
    ppermute x1, starting transfers between devices, shards(): lax.ppermute(jnp.concatenate([feat[0:2], side[0:1]], axis=0), 'px', down)  1.47 us
    pallas_call x1, Pallas kernels, shards(): pl.pallas_call(functools.partial(bin_kernel, frames * ranks), out_shape=j...  1.3 us
    ppermute x1, starting transfers between devices, shards(): lax.ppermute(jnp.concatenate([feat[2:4], side[1:2]], axis=0), 'px', up)  1.29 us
  transfers between devices with their start and end apart: 3, of which 0 were waited for; matrix products, arithmetic and copies ran while one was open for 0% of the time, Pallas kernels for 15%

profile of v5, /device:TPU:1, one launch (start us, length us, event | category | flops | bytes accessed | tf_op | source)
XLA Modules:
  0.0 37.8 jit_solution(14165162900655382203)
XLA Ops:
  0.0 0.9 %convert_add_fusion.packed_ref = f32[69,2,128]{2,1,0:T(2,128)S(1)} fusion(s32[2,2,4]{2,1,0:T(2,128)} %bitcast.18, s32[2,2,128]{2,1,0:T(2,128)} %param.14, s32[8,2,128]{2,1,0:T(2,128)} %bitcast.16, f32[1,1,32]{2,1,0:T(1,128)} %bitcast.19, f32[1,1,32]{2,1,0:T(1,128)} %bitcast.20, f32[1,1,32]{2,1,0:T(1,128)} %bitcast.21, f32[6,2,128]{2,1,0:T(2,128)} %bitcast.17, ...), kind=kLoop, calls=%fused_computation | loop fusion | flops 158976 | bytes 136640 | tf_op jit(solution)/shard_map/add | solution.py:633
  0.9 0.8 %prepare.1 = (f32[4,5,8,128]{3,2,1,0:T(8,128)S(1)}, f32[2,5,8,128]{3,2,1,0:T(8,128)S(1)}, f32[16,8,128]{2,1,0:T(8,128)S(1)}) custom-call(f32[69,2,128]{2,1,0:T(2,128)S(1)} %convert_add_fusion.packed_ref), custom_call_target="tpu_custom_call" | custom-call | tf_op jit(solution)/shard_map/prepare/pallas_call | solution.py:634
  1.7 3.8 %collective-permute-start = (f32[2,5,8,128]{3,2,1,0:T(8,128)S(1)}, f32[2,5,8,128]{3,2,1,0:T(8,128)S(1)}, u32[]{:S(2)}, u32[]{:S(2)}) collective-permute-start(f32[2,5,8,128]{3,2,1,0:T(8,128)S(1)} %get-tuple-element.17), channel_id=1, source_target_pairs={{0,32},{32,0},{1,33},{33,1},{2,34},{34,2},{3,35},{35,3},{4,36},{36... | collective-permute-start | bytes 122888 | tf_op jit(solution)/shard_map/ppermute | solution.py:652
  5.5 2.0 %inner.1 = (f32[4,2,8,256]{3,2,1,0:T(8,128)S(1)}, f32[4,2,8,128]{3,2,1,0:T(8,128)S(1)}, bf16[4,2,320,256]{3,2,1,0:T(8,128)(2,1)S(1)}) custom-call(f32[4,5,8,128]{3,2,1,0:T(8,128)S(1)} %get-tuple-element.16.feat_ref), custom_call_target="tpu_custom_call" | custom-call | flops 1000000000 | bytes 1000000 | tf_op jit(solution)/shard_map/inner/pallas_call | solution.py:656
  7.6 0.0 collective-permute-done.side_ref
  7.6 1.3 %collective-permute-start.1 = (f32[3,5,8,128]{3,2,1,0:T(8,128)S(1)}, f32[3,5,8,128]{3,2,1,0:T(8,128)S(1)}, u32[]{:S(2)}, u32[]{:S(2)}) collective-permute-start(f32[3,5,8,128]{3,2,1,0:T(8,128)S(1)} %pad_maximum_fusion), channel_id=1, source_target_pairs={{0,64},{64,128},{128,192},{192,0},{1,65},{65,129},{129,193},{193,1... | collective-permute-start | bytes 184328 | tf_op jit(solution)/shard_map/ppermute | solution.py:678
  8.9 1.5 %collective-permute-start.2 = (f32[3,5,8,128]{3,2,1,0:T(8,128)S(1)}, f32[3,5,8,128]{3,2,1,0:T(8,128)S(1)}, u32[]{:S(2)}, u32[]{:S(2)}) collective-permute-start(f32[3,5,8,128]{3,2,1,0:T(8,128)S(1)} %pad_maximum_fusion.1), channel_id=1, source_target_pairs={{0,192},{64,0},{128,64},{192,128},{1,193},{65,1},{129,65},{193,129... | collective-permute-start | bytes 184328 | tf_op jit(solution)/shard_map/ppermute | solution.py:679
  10.4 3.5 %side.1 = (f32[4,2,8,256]{3,2,1,0:T(8,128)S(1)}, f32[4,2,8,256]{3,2,1,0:T(8,128)S(1)}, bf16[4,320,256]{2,1,0:T(8,128)(2,1)S(1)}) custom-call(f32[4,5,8,128]{3,2,1,0:T(8,128)S(1)} %get-tuple-element.16.feat_ref, f32[2,5,8,128]{3,2,1,0:T(8,128)S(1)} %collective-permute-done.side_ref, bf16[4,2,320,256]{3,2,1,0:T(8,128)(2,1)S(1)} %get-tuple-element.20.own_ref), custom_call_target="tpu_custom_call" | custom-call | flops 1000000000 | bytes 1000000 | tf_op jit(solution)/shard_map/side/pallas_call | solution.py:680
  13.9 0.0 collective-permute-done.1.low_ref
  13.9 0.0 collective-permute-done.2.high_ref
  13.9 3.1 %outer.1 = f32[32,4,128]{2,1,0:T(4,128)S(1)} custom-call(f32[4,5,8,128]{3,2,1,0:T(8,128)S(1)} %get-tuple-element.16.feat_ref, f32[3,5,8,128]{3,2,1,0:T(8,128)S(1)} %collective-permute-done.1.low_ref, f32[3,5,8,128]{3,2,1,0:T(8,128)S(1)} %collective-permute-done.2.high_ref, bf16[4,2,320,256]{3,2,1,0:T(8,128)(2,1)S(1)} %get-tuple-element.20.own_ref, ...), custom_call_target="tpu_custom_call" | custom-call | tf_op jit(solution)/shard_map/outer/pallas_call | solution.py:700
  17.0 19.5 %all_to_all.5.got_ref = f32[32,4,128]{2,1,0:T(4,128)S(1)} all-to-all(f32[32,4,128]{2,1,0:T(4,128)S(1)} %outer.1), channel_id=1, replica_groups=mesh['px'=4,'py'=2,'fr'=32] {'fr'}, dimensions={0} | all-to-all | bytes 131072 | tf_op jit(solution)/shard_map/all_to_all | solution.py:718
  36.5 1.3 %bin.1 = f32[13,2,2,720]{3,2,1,0:T(2,128)} custom-call(f32[32,4,128]{2,1,0:T(4,128)S(1)} %all_to_all.5.got_ref), custom_call_target="tpu_custom_call" | custom-call | tf_op jit(solution)/shard_map/bin/pallas_call | solution.py:720
  (4 shorter events, 0.0 us)
Async XLA Ops:
  1.7 5.9 %collective-permute-start = (f32[2,5,8,128]{3,2,1,0:T(8,128)S(1)}, f32[2,5,8,128]{3,2,1,0:T(8,128)S(1)}, u32[]{:S(2)}, u32[]{:S(2)}) collective-permute-start(f32[2,5,8,128]{3,2,1,0:T(8,128)S(1)} %get-tuple-element.17), channel_id=1, source_target_pairs={{0,32},{32,0},{1,33},{33,1},{2,34},{34,2},{3,35},{35,3},{4,36},{36... | collective-permute-start | bytes 122888 | tf_op jit(solution)/shard_map/ppermute | solution.py:652
  7.6 6.3 %collective-permute-start.1 = (f32[3,5,8,128]{3,2,1,0:T(8,128)S(1)}, f32[3,5,8,128]{3,2,1,0:T(8,128)S(1)}, u32[]{:S(2)}, u32[]{:S(2)}) collective-permute-start(f32[3,5,8,128]{3,2,1,0:T(8,128)S(1)} %pad_maximum_fusion), channel_id=1, source_target_pairs={{0,64},{64,128},{128,192},{192,0},{1,65},{65,129},{129,193},{193,1... | collective-permute-start | bytes 184328 | tf_op jit(solution)/shard_map/ppermute | solution.py:678
  8.9 5.0 %collective-permute-start.2 = (f32[3,5,8,128]{3,2,1,0:T(8,128)S(1)}, f32[3,5,8,128]{3,2,1,0:T(8,128)S(1)}, u32[]{:S(2)}, u32[]{:S(2)}) collective-permute-start(f32[3,5,8,128]{3,2,1,0:T(8,128)S(1)} %pad_maximum_fusion.1), channel_id=1, source_target_pairs={{0,192},{64,0},{128,64},{192,128},{1,193},{65,1},{129,65},{193,129... | collective-permute-start | bytes 184328 | tf_op jit(solution)/shard_map/ppermute | solution.py:679

commit v6 on v5

--- a/solution.py
+++ b/solution.py
@@ -397,77 +397,8 @@
     return jnp.where(lax.axis_index("py") == 0, 1.0, -1.0).astype(F32) * (2.0 * CUTOFF * UNIT)
 
 
-def side_kernel(
-    feat_ref, side_ref, own_ref, acc_ref, wall_ref, face_ref,
-    solute_ref, left_ref, mono_ref, coef_ref,
-):
-    frames = side_ref.shape[1] - 1
-    facing = 1 - lax.axis_index("py")
-    shift = (0.0, to_facing())
-    for i in range(2):
-        atoms = [feat_ref[2 * i + j, frames] for j in range(2)]
-        solute_ref[i] = pair_rows(*[solute_partner(value, (0.0, 0.0), 0.0) for value in atoms])
-        for j in range(2):
-            coef_ref[2 * i + j, 0], coef_ref[2 * i + j, 1] = solute_levels(atoms[j])
-    solute_ref[2] = pair_rows(*[solute_partner(side_ref[k, frames], shift, 0.0) for k in range(2)])
-    for k in range(2):
-        coef_ref[4 + k, 0], coef_ref[4 + k, 1] = solute_levels(side_ref[k, frames])
-    def set_up(f):
-        left_ref[f] = pair_rows(*[water_partner(side_ref[k, f], shift, 0.0) for k in range(2)])
-        mono_ref[f] = moment_rows(*[moment_partner(side_ref[k, f], shift) for k in range(2)])
-        face_ref[f, 0:OWN_ROWS] = jnp.concatenate(
-            [own_side(feat_ref[facing, f]), own_side(feat_ref[2 + facing, f])], axis=1
-        )
-
-    def frame(f):
-        for i in range(2):
-            sides = [own_ref[f, i, P_ROWS], own_ref[f, i, Q_ROWS]]
-            acc = jnp.zeros((8, 256), F32)
-            for column in range(2):
-                left = solute_ref[column]
-                for j in range(2):
-                    cell = 2 * column + j
-                    acc = solute_pairs(
-                        acc, *[dot(left, only(side, j)) for side in sides],
-                        coef_ref[cell, 0], coef_ref[cell, 1],
-                    )
-            acc_ref[f, i] = acc
-        faces = [face_ref[f, rows] for rows in (P_ROWS, Q_ROWS, M_ROWS)]
-        water = jnp.zeros((8, 256), F32)
-        solute = jnp.zeros((8, 256), F32)
-        for meet, order in ((each, (4, 5)), (crossed, (5, 4))):
-            sides = [meet(face[:, :128], face[:, 128:]) for face in faces]
-            water = water_pairs(water, [dot(left_ref[f], sides[0]), dot(mono_ref[f], sides[2])])
-            levels = [
-                jnp.concatenate([coef_ref[order[0], k], coef_ref[order[1], k]], axis=1) for k in range(2)
-            ]
-            solute = solute_pairs(
-                solute, *[dot(solute_ref[2], sides[q]) for q in range(2)], *levels
-            )
-        wall_ref[f, 0] = water
-        wall_ref[f, 1] = solute
-
-    run_frames(frames, set_up, frame)
-
-
-def outer_kernel(
-    feat_ref, low_ref, high_ref, own_ref, face_ref, water_ref, other_ref, solute_in_ref, wall_in_ref,
-    comp_ref, send_ref, left_ref, mono_ref, solute_ref, coef_ref, acc_ref, wall_ref, rec_ref,
-):
-    frames = feat_ref.shape[1] - 1
-    px = lax.axis_index("px")
-    width = 2.0 * CUTOFF * UNIT
-    across = to_facing()
-    no_low = jnp.where(px == 0, 1.0, 0.0).astype(F32)
-    no_high = jnp.where(px == lax.axis_size("px") - 1, 1.0, 0.0).astype(F32)
-    low = ((-width, 0.0), no_low)
-    high = ((width, 0.0), no_high)
-    pairs = (
-        ((low_ref, 0, *low), (low_ref, 1, *low)),
-        ((high_ref, 0, *high), (high_ref, 1, *high)),
-        ((low_ref, 2, (-width, across), no_low), (high_ref, 2, (width, across), no_high)),
-    )
-    for number, pair in enumerate(pairs):
+def set_solutes(pairs, frames, solute_ref, coef_ref, start):
+    for number, pair in enumerate(pairs, start):
         solute_ref[number] = pair_rows(
             *[solute_partner(ref[k, frames], shift, absent) for ref, k, shift, absent in pair]
         )
@@ -475,27 +406,54 @@
             cell = 2 * number + place
             coef_ref[cell, 0], coef_ref[cell, 1] = solute_levels(ref[k, frames])
 
+
+def set_waters(pairs, f, left_ref, mono_ref):
+    for number, pair in enumerate(pairs):
+        left_ref[f, number] = pair_rows(
+            *[water_partner(ref[k, f], shift, absent) for ref, k, shift, absent in pair]
+        )
+        mono_ref[f, number] = moment_rows(
+            *[moment_partner(ref[k, f], shift) for ref, k, shift, _ in pair]
+        )
+
+
+def ends():
+    px = lax.axis_index("px")
+    no_low = jnp.where(px == 0, 1.0, 0.0).astype(F32)
+    no_high = jnp.where(px == lax.axis_size("px") - 1, 1.0, 0.0).astype(F32)
+    width = 2.0 * CUTOFF * UNIT
+    return (-width, no_low), (width, no_high)
+
+
+def column_kernel(
+    feat_ref, low_ref, high_ref, own_ref, water_ref, acc_ref, left_ref, mono_ref, solute_ref, coef_ref,
+):
+    frames = feat_ref.shape[1] - 1
+    (low_x, no_low), (high_x, no_high) = ends()
+    pairs = (
+        tuple((low_ref, j, (low_x, 0.0), no_low) for j in range(2)),
+        tuple((high_ref, j, (high_x, 0.0), no_high) for j in range(2)),
+    )
+    own_pairs = [[(feat_ref, 2 * i + j, (0.0, 0.0), 0.0) for j in range(2)] for i in range(2)]
+    set_solutes(own_pairs, frames, solute_ref, coef_ref, 0)
+    set_solutes(pairs, frames, solute_ref, coef_ref, 2)
+
     def set_up(f):
-        for number, pair in enumerate(pairs):
-            left_ref[f, number] = pair_rows(
-                *[water_partner(ref[k, f], shift, absent) for ref, k, shift, absent in pair]
-            )
-            mono_ref[f, number] = moment_rows(
-                *[moment_partner(ref[k, f], shift) for ref, k, shift, _ in pair]
-            )
+        set_waters(pairs, f, left_ref, mono_ref)
 
     def frame(f):
-        faces = [face_ref[f, rows] for rows in (P_ROWS, Q_ROWS, M_ROWS)]
-        sides = [each(face[:, :128], face[:, 128:]) for face in faces]
-        wall_ref[f, 0] = water_pairs(
-            wall_in_ref[f, 0], [dot(left_ref[f, 2], sides[0]), dot(mono_ref[f, 2], sides[2])]
-        )
-        levels = [jnp.concatenate([coef_ref[4, k], coef_ref[5, k]], axis=1) for k in range(2)]
-        wall_ref[f, 1] = solute_pairs(
-            wall_in_ref[f, 1], *[dot(solute_ref[2], sides[q]) for q in range(2)], *levels
-        )
         for i in range(2):
             sides = [own_ref[f, i, rows] for rows in (P_ROWS, Q_ROWS, M_ROWS)]
+            solute = jnp.zeros((8, 256), F32)
+            for column in (0, 1, 2 + i):
+                left = solute_ref[column]
+                for j in range(2):
+                    cell = 2 * column + j
+                    solute = solute_pairs(
+                        solute, *[dot(left, only(sides[q], j)) for q in range(2)],
+                        coef_ref[cell, 0], coef_ref[cell, 1],
+                    )
+            acc_ref[f, i, 1] = solute
             full, part = (slice(64, 128), slice(0, 64)) if i == 0 else (slice(0, 64), slice(64, 128))
             lanes = slice(0, 128) if i == 0 else slice(128, 256)
             water = water_ref[f, i]
@@ -516,20 +474,52 @@
             )
             late = [late[:, :128] + late[:, 128:], jnp.zeros((8, 128), F32)]
             acc_ref[f, i, 0] = water + jnp.concatenate(late if i == 0 else late[::-1], axis=1)
-            solute = solute_in_ref[f, i]
-            for j in range(2):
-                cell = 2 * i + j
-                solute = solute_pairs(
-                    solute, *[dot(solute_ref[i], only(sides[q], j)) for q in range(2)],
-                    coef_ref[cell, 0], coef_ref[cell, 1],
-                )
-            acc_ref[f, i, 1] = solute
+
+    run_frames(frames, set_up, frame)
+
+
+def facing_kernel(
+    feat_ref, side_ref, acc_ref, other_ref, comp_ref, send_ref,
+    left_ref, mono_ref, solute_ref, coef_ref, face_ref, wall_ref, rec_ref,
+):
+    frames = feat_ref.shape[1] - 1
+    facing = 1 - lax.axis_index("py")
+    across = to_facing()
+    (low_x, no_low), (high_x, no_high) = ends()
+    pairs = (
+        tuple((side_ref, k, (0.0, across), 0.0) for k in range(2)),
+        ((side_ref, 2, (low_x, across), no_low), (side_ref, 3, (high_x, across), no_high)),
+    )
+    set_solutes(pairs, frames, solute_ref, coef_ref, 0)
+
+    def set_up(f):
+        set_waters(pairs, f, left_ref, mono_ref)
+        face_ref[f] = jnp.concatenate(
+            [own_side(feat_ref[facing, f]), own_side(feat_ref[2 + facing, f])], axis=1
+        )
+
+    def frame(f):
+        faces = [face_ref[f, rows] for rows in (P_ROWS, Q_ROWS, M_ROWS)]
+        water = jnp.zeros((8, 256), F32)
+        solute = jnp.zeros((8, 256), F32)
+        for meet, number, order in ((each, 0, (0, 1)), (crossed, 0, (1, 0)), (each, 1, (2, 3))):
+            sides = [meet(face[:, :128], face[:, 128:]) for face in faces]
+            water = water_pairs(
+                water, [dot(left_ref[f, number], sides[0]), dot(mono_ref[f, number], sides[2])]
+            )
+            levels = [
+                jnp.concatenate([coef_ref[order[0], k], coef_ref[order[1], k]], axis=1) for k in range(2)
+            ]
+            solute = solute_pairs(
+                solute, *[dot(solute_ref[number], sides[q]) for q in range(2)], *levels
+            )
+        wall_ref[f, 0] = water
+        wall_ref[f, 1] = solute
 
     run_frames(frames, set_up, frame)
     rec_ref[...] = comp_ref[...]
     self_root = P_SOFT**-0.5
     self_u15 = self_root**3
-    facing = 1 - lax.axis_index("py")
     for f in range(frames):
         walls = [jnp.sum(wall_ref[f, k], axis=0, keepdims=True) for k in range(2)]
         for i in range(2):
@@ -649,7 +639,10 @@
         name="prepare",
     )(packed)
 
-    side = lax.ppermute(side_out, "py", [(0, 1), (1, 0)])
+    up = [(k, (k + 1) % cols) for k in range(cols)]
+    down = [(k, (k - 1) % cols) for k in range(cols)]
+    low = lax.ppermute(feat[2:4], "px", up)
+    high = lax.ppermute(feat[0:2], "px", down)
 
     work = pl.CostEstimate(flops=10**9, bytes_accessed=10**6, transcendentals=0)
     column_shape = jax.ShapeDtypeStruct((frames, 2, 8, 256), F32)
@@ -672,48 +665,43 @@
         name="inner",
     )(feat)
 
-    side, water = lax.optimization_barrier((side, water))
-    up = [(k, (k + 1) % cols) for k in range(cols)]
-    down = [(k, (k - 1) % cols) for k in range(cols)]
-    low = lax.ppermute(jnp.concatenate([feat[2:4], side[1:2]], axis=0), "px", up)
-    high = lax.ppermute(jnp.concatenate([feat[0:2], side[0:1]], axis=0), "px", down)
-    solute, wall, face = pl.pallas_call(
-        side_kernel,
-        out_shape=(
-            column_shape,
-            column_shape,
-            jax.ShapeDtypeStruct((frames, HELD_ROWS, 256), BF16),
-        ),
-        in_specs=[vmem()] * 3,
-        out_specs=(vmem(),) * 3,
+    low, high, water = lax.optimization_barrier((low, high, water))
+    facing = 1 - lax.axis_index("py")
+    beyond = [lax.dynamic_slice_in_dim(column, facing, 1, axis=0) for column in (low, high)]
+    side = lax.ppermute(jnp.concatenate([side_out, *beyond], axis=0), "py", [(0, 1), (1, 0)])
+    acc = pl.pallas_call(
+        column_kernel,
+        out_shape=jax.ShapeDtypeStruct((frames, 2, 2, 8, 256), F32),
+        in_specs=[vmem()] * 5,
+        out_specs=vmem(),
         scratch_shapes=[
-            pltpu.VMEM((3, 128, 2 * ROWS), BF16),
-            pltpu.VMEM((frames, 128, 2 * ROWS), BF16),
-            pltpu.VMEM((frames, 128, 2 * MONO), BF16),
-            pltpu.VMEM((6, 2, 128, 128), F32),
+            pltpu.VMEM((frames, 2, 128, 2 * ROWS), BF16),
+            pltpu.VMEM((frames, 2, 128, 2 * MONO), BF16),
+            pltpu.VMEM((4, 128, 2 * ROWS), BF16),
+            pltpu.VMEM((8, 2, 128, 128), F32),
         ],
         compiler_params=PARAMS,
         cost_estimate=work,
-        name="side",
-    )(feat, side, own)
+        name="columns",
+    )(feat, low, high, own, water)
 
     send = pl.pallas_call(
-        outer_kernel,
+        facing_kernel,
         out_shape=jax.ShapeDtypeStruct((ranks, 4, 128), F32),
-        in_specs=[vmem()] * 10,
+        in_specs=[vmem()] * 5,
         out_specs=vmem(),
         scratch_shapes=[
-            pltpu.VMEM((frames, 3, 128, 2 * ROWS), BF16),
-            pltpu.VMEM((frames, 3, 128, 2 * MONO), BF16),
-            pltpu.VMEM((3, 128, 2 * ROWS), BF16),
-            pltpu.VMEM((6, 2, 128, 128), F32),
-            pltpu.VMEM((frames, 2, 2, 8, 256), F32),
+            pltpu.VMEM((frames, 2, 128, 2 * ROWS), BF16),
+            pltpu.VMEM((frames, 2, 128, 2 * MONO), BF16),
+            pltpu.VMEM((2, 128, 2 * ROWS), BF16),
+            pltpu.VMEM((4, 2, 128, 128), F32),
+            pltpu.VMEM((frames, OWN_ROWS, 256), BF16),
             pltpu.VMEM((frames, 2, 8, 256), F32),
             pltpu.VMEM((total, 8, 128), F32),
         ],
         compiler_params=PARAMS,
-        name="outer",
-    )(feat, low, high, own, face, water, other, solute, wall, comp)
+        name="facing",
+    )(feat, side, acc, other, comp)
 
     got = lax.all_to_all(send, "fr", 0, 0, tiled=True)
     share = CELL_XY * CELL_XY * SLAB // ranks

time: 38 us -> 37.1 us (0.976)
  blocking collectives: 19.5 us -> 18.6 us
    all_to_all x1, blocking collectives: 19.5 us -> 18.6 us  [shards(): got = lax.all_to_all(send, 'fr', 0, 0, tiled=True)]
  transfers between devices with their start and end apart: 3 -> 3, of which waited for: 0 -> 0; matrix products, arithmetic and copies ran while one was open for 0% -> 0% of each run, Pallas kernels for 15% -> 18%
where the time goes in v6:
time: 37.1 us; the launch traced here: 36.9 us
  blocking collectives  18.6 us (50%)
  Pallas kernels  10.8 us (29%)
  starting transfers between devices  6.58 us (18%)
  other arithmetic  0.89 us (2%)
    all_to_all x1, blocking collectives, shards(): got = lax.all_to_all(send, 'fr', 0, 0, tiled=True)  18.6 us
    pallas_call x1, Pallas kernels, shards(): pl.pallas_call(column_kernel, out_shape=jax.ShapeDtypeStruct((frames, 2,...  4.48 us
    ppermute x1, starting transfers between devices, shards(): lax.ppermute(jnp.concatenate([side_out, *beyond], axis=0), 'py', [(0, 1),...  3.1 us
    pallas_call x1, Pallas kernels, shards(): pl.pallas_call(facing_kernel, out_shape=jax.ShapeDtypeStruct((ranks, 4, 1...  2.19 us
    ppermute x1, starting transfers between devices, shards(): low = lax.ppermute(feat[2:4], 'px', up)  2.12 us
    pallas_call x1, Pallas kernels, shards(): pl.pallas_call(inner_kernel, out_shape=(column_shape, jax.ShapeDtypeStruc...  2.03 us
    ppermute x1, starting transfers between devices, shards(): high = lax.ppermute(feat[0:2], 'px', down)  1.36 us
    pallas_call x1, Pallas kernels, shards(): pl.pallas_call(functools.partial(bin_kernel, frames * ranks), out_shape=j...  1.3 us
  transfers between devices with their start and end apart: 3, of which 0 were waited for; matrix products, arithmetic and copies ran while one was open for 0% of the time, Pallas kernels for 18%

profile of v6, /device:TPU:1, one launch (start us, length us, event | category | flops | bytes accessed | tf_op | source)
XLA Modules:
  0.0 36.9 jit_solution(14234630235609547048)
XLA Ops:
  0.0 0.9 %convert_add_fusion.packed_ref = f32[69,2,128]{2,1,0:T(2,128)S(1)} fusion(s32[2,2,4]{2,1,0:T(2,128)} %bitcast.18, s32[2,2,128]{2,1,0:T(2,128)} %param.14, s32[8,2,128]{2,1,0:T(2,128)} %bitcast.16, f32[1,1,32]{2,1,0:T(1,128)} %bitcast.19, f32[1,1,32]{2,1,0:T(1,128)} %bitcast.20, f32[1,1,32]{2,1,0:T(1,128)} %bitcast.21, f32[6,2,128]{2,1,0:T(2,128)} %bitcast.17, ...), kind=kLoop, calls=%fused_computation.1 | loop fusion | flops 158976 | bytes 136640 | tf_op jit(solution)/shard_map/add | solution.py:623
  0.9 0.8 %prepare.1 = (f32[4,5,8,128]{3,2,1,0:T(8,128)S(1)}, f32[2,5,8,128]{3,2,1,0:T(8,128)S(1)}, f32[16,8,128]{2,1,0:T(8,128)S(1)}) custom-call(f32[69,2,128]{2,1,0:T(2,128)S(1)} %convert_add_fusion.packed_ref), custom_call_target="tpu_custom_call" | custom-call | tf_op jit(solution)/shard_map/prepare/pallas_call | solution.py:624
  1.7 2.1 %collective-permute-start = (f32[2,5,8,128]{3,2,1,0:T(8,128)S(1)}, f32[2,5,8,128]{3,2,1,0:T(8,128)S(1)}, u32[]{:S(2)}, u32[]{:S(2)}) collective-permute-start(f32[2,5,8,128]{3,2,1,0:T(8,128)S(1)} %get-tuple-element.24), channel_id=1, source_target_pairs={{0,64},{64,128},{128,192},{192,0},{1,65},{65,129},{129,193},{193,1... | collective-permute-start | bytes 122888 | tf_op jit(solution)/shard_map/ppermute | solution.py:644
  3.8 1.4 %collective-permute-start.1 = (f32[2,5,8,128]{3,2,1,0:T(8,128)S(1)}, f32[2,5,8,128]{3,2,1,0:T(8,128)S(1)}, u32[]{:S(2)}, u32[]{:S(2)}) collective-permute-start(f32[2,5,8,128]{3,2,1,0:T(8,128)S(1)} %get-tuple-element.23), channel_id=1, source_target_pairs={{0,192},{64,0},{128,64},{192,128},{1,193},{65,1},{129,65},{193,129... | collective-permute-start | bytes 122888 | tf_op jit(solution)/shard_map/ppermute | solution.py:645
  5.2 2.0 %inner.1 = (f32[4,2,8,256]{3,2,1,0:T(8,128)S(1)}, f32[4,2,8,128]{3,2,1,0:T(8,128)S(1)}, bf16[4,2,320,256]{3,2,1,0:T(8,128)(2,1)S(1)}) custom-call(f32[4,5,8,128]{3,2,1,0:T(8,128)S(1)} %get-tuple-element.14.feat_ref), custom_call_target="tpu_custom_call" | custom-call | flops 1000000000 | bytes 1000000 | tf_op jit(solution)/shard_map/inner/pallas_call | solution.py:649
  7.2 0.0 collective-permute-done.low_ref
  7.2 0.0 collective-permute-done.1.high_ref
  7.3 3.1 %collective-permute-start.2 = (f32[4,5,8,128]{3,2,1,0:T(8,128)S(1)}, f32[4,5,8,128]{3,2,1,0:T(8,128)S(1)}, u32[]{:S(2)}, u32[]{:S(2)}) collective-permute-start(f32[4,5,8,128]{3,2,1,0:T(8,128)S(1)} %pad_maximum_fusion), channel_id=1, source_target_pairs={{0,32},{32,0},{1,33},{33,1},{2,34},{34,2},{3,35},{35,3},{4,36},{36... | collective-permute-start | bytes 245768 | tf_op jit(solution)/shard_map/ppermute | solution.py:671
  10.4 4.5 %columns.1.acc_ref = f32[4,2,2,8,256]{4,3,2,1,0:T(8,128)S(1)} custom-call(f32[4,5,8,128]{3,2,1,0:T(8,128)S(1)} %get-tuple-element.14.feat_ref, f32[2,5,8,128]{3,2,1,0:T(8,128)S(1)} %collective-permute-done.low_ref, f32[2,5,8,128]{3,2,1,0:T(8,128)S(1)} %collective-permute-done.1.high_ref, bf16[4,2,320,256]{3,2,1,0:T(8,128)(2,1)S(1)} %get-tuple-element.19.own_ref, ...), custom_call_target="tpu_custom_call" | custom-call | flops 1000000000 | bytes 1000000 | tf_op jit(solution)/shard_map/columns/pallas_call | solution.py:672
  14.9 0.0 collective-permute-done.2.side_ref
  14.9 2.2 %facing.1 = f32[32,4,128]{2,1,0:T(4,128)S(1)} custom-call(f32[4,5,8,128]{3,2,1,0:T(8,128)S(1)} %get-tuple-element.14.feat_ref, f32[4,5,8,128]{3,2,1,0:T(8,128)S(1)} %collective-permute-done.2.side_ref, f32[4,2,2,8,256]{4,3,2,1,0:T(8,128)S(1)} %columns.1.acc_ref, f32[4,2,8,128]{3,2,1,0:T(8,128)S(1)} %get-tuple-element.21.other_ref, ...), custom_call_target="tpu_custom_call" | custom-call | tf_op jit(solution)/shard_map/facing/pallas_call | solution.py:688
  17.1 18.6 %all_to_all.5.got_ref = f32[32,4,128]{2,1,0:T(4,128)S(1)} all-to-all(f32[32,4,128]{2,1,0:T(4,128)S(1)} %facing.1), channel_id=1, replica_groups=mesh['px'=4,'py'=2,'fr'=32] {'fr'}, dimensions={0} | all-to-all | bytes 131072 | tf_op jit(solution)/shard_map/all_to_all | solution.py:706
  35.6 1.3 %bin.1 = f32[13,2,2,720]{3,2,1,0:T(2,128)} custom-call(f32[32,4,128]{2,1,0:T(4,128)S(1)} %all_to_all.5.got_ref), custom_call_target="tpu_custom_call" | custom-call | tf_op jit(solution)/shard_map/bin/pallas_call | solution.py:708
  (3 shorter events, 0.0 us)
Async XLA Ops:
  1.7 5.5 %collective-permute-start = (f32[2,5,8,128]{3,2,1,0:T(8,128)S(1)}, f32[2,5,8,128]{3,2,1,0:T(8,128)S(1)}, u32[]{:S(2)}, u32[]{:S(2)}) collective-permute-start(f32[2,5,8,128]{3,2,1,0:T(8,128)S(1)} %get-tuple-element.24), channel_id=1, source_target_pairs={{0,64},{64,128},{128,192},{192,0},{1,65},{65,129},{129,193},{193,1... | collective-permute-start | bytes 122888 | tf_op jit(solution)/shard_map/ppermute | solution.py:644
  3.8 3.4 %collective-permute-start.1 = (f32[2,5,8,128]{3,2,1,0:T(8,128)S(1)}, f32[2,5,8,128]{3,2,1,0:T(8,128)S(1)}, u32[]{:S(2)}, u32[]{:S(2)}) collective-permute-start(f32[2,5,8,128]{3,2,1,0:T(8,128)S(1)} %get-tuple-element.23), channel_id=1, source_target_pairs={{0,192},{64,0},{128,64},{192,128},{1,193},{65,1},{129,65},{193,129... | collective-permute-start | bytes 122888 | tf_op jit(solution)/shard_map/ppermute | solution.py:645
  7.3 7.6 %collective-permute-start.2 = (f32[4,5,8,128]{3,2,1,0:T(8,128)S(1)}, f32[4,5,8,128]{3,2,1,0:T(8,128)S(1)}, u32[]{:S(2)}, u32[]{:S(2)}) collective-permute-start(f32[4,5,8,128]{3,2,1,0:T(8,128)S(1)} %pad_maximum_fusion), channel_id=1, source_target_pairs={{0,32},{32,0},{1,33},{33,1},{2,34},{34,2},{3,35},{35,3},{4,36},{36... | collective-permute-start | bytes 245768 | tf_op jit(solution)/shard_map/ppermute | solution.py:671

commit v7 on v6

--- a/solution.py
+++ b/solution.py
@@ -343,8 +343,25 @@
     )
 
 
-def inner_kernel(feat_ref, acc_ref, other_ref, own_ref, left_ref, mono_ref, sum_ref):
+def atom_pairs(acc, columns, own_ref, f, i, solute_ref, coef_ref):
+    for column in columns:
+        left = solute_ref[column]
+        for j in range(2):
+            cell = 2 * column + j
+            acc = solute_pairs(
+                acc, *[dot(left, only(own_ref[f, i, rows], j)) for rows in (P_ROWS, Q_ROWS)],
+                coef_ref[cell, 0], coef_ref[cell, 1],
+            )
+    return acc
+
+
+def inner_kernel(
+    feat_ref, acc_ref, other_ref, own_ref, atoms_ref, left_ref, mono_ref, sum_ref, solute_ref, coef_ref,
+):
     frames = feat_ref.shape[1] - 1
+    own_pairs = [[(feat_ref, 2 * i + j, (0.0, 0.0), 0.0) for j in range(2)] for i in range(2)]
+    set_solutes(own_pairs, frames, solute_ref, coef_ref, 0)
+
     def set_up(f):
         for i in range(2):
             left_ref[f, i] = pair_rows(
@@ -358,6 +375,7 @@
             )
 
     def frame(f):
+        atoms_ref[f] = atom_pairs(jnp.zeros((8, 256), F32), (0, 1), own_ref, f, 0, solute_ref, coef_ref)
         for i in range(2):
             sides = (own_ref[f, i, P_ROWS], own_ref[f, i, M_ROWS])
             acc = jnp.zeros((8, 256), F32)
@@ -426,7 +444,8 @@
 
 
 def column_kernel(
-    feat_ref, low_ref, high_ref, own_ref, water_ref, acc_ref, left_ref, mono_ref, solute_ref, coef_ref,
+    feat_ref, low_ref, high_ref, own_ref, water_ref, atoms_ref, acc_ref,
+    left_ref, mono_ref, solute_ref, coef_ref,
 ):
     frames = feat_ref.shape[1] - 1
     (low_x, no_low), (high_x, no_high) = ends()
@@ -444,15 +463,9 @@
     def frame(f):
         for i in range(2):
             sides = [own_ref[f, i, rows] for rows in (P_ROWS, Q_ROWS, M_ROWS)]
-            solute = jnp.zeros((8, 256), F32)
-            for column in (0, 1, 2 + i):
-                left = solute_ref[column]
-                for j in range(2):
-                    cell = 2 * column + j
-                    solute = solute_pairs(
-                        solute, *[dot(left, only(sides[q], j)) for q in range(2)],
-                        coef_ref[cell, 0], coef_ref[cell, 1],
-                    )
+            solute = atoms_ref[f] if i == 0 else jnp.zeros((8, 256), F32)
+            columns = (2,) if i == 0 else (0, 1, 3)
+            solute = atom_pairs(solute, columns, own_ref, f, i, solute_ref, coef_ref)
             acc_ref[f, i, 1] = solute
             full, part = (slice(64, 128), slice(0, 64)) if i == 0 else (slice(0, 64), slice(64, 128))
             lanes = slice(0, 128) if i == 0 else slice(128, 256)
@@ -646,19 +659,22 @@
 
     work = pl.CostEstimate(flops=10**9, bytes_accessed=10**6, transcendentals=0)
     column_shape = jax.ShapeDtypeStruct((frames, 2, 8, 256), F32)
-    water, other, own = pl.pallas_call(
+    water, other, own, atoms = pl.pallas_call(
         inner_kernel,
         out_shape=(
             column_shape,
             jax.ShapeDtypeStruct((frames, 2, 8, 128), F32),
             jax.ShapeDtypeStruct((frames, 2, HELD_ROWS, 256), BF16),
+            jax.ShapeDtypeStruct((frames, 8, 256), F32),
         ),
         in_specs=[vmem()],
-        out_specs=(vmem(),) * 3,
+        out_specs=(vmem(),) * 4,
         scratch_shapes=[
             pltpu.VMEM((frames, 2, 128, 2 * ROWS), BF16),
             pltpu.VMEM((frames, 2, 128, 2 * MONO), BF16),
             pltpu.VMEM((frames, 2, 128, 128), F32),
+            pltpu.VMEM((2, 128, 2 * ROWS), BF16),
+            pltpu.VMEM((4, 2, 128, 128), F32),
         ],
         compiler_params=PARAMS,
         cost_estimate=work,
@@ -672,7 +688,7 @@
     acc = pl.pallas_call(
         column_kernel,
         out_shape=jax.ShapeDtypeStruct((frames, 2, 2, 8, 256), F32),
-        in_specs=[vmem()] * 5,
+        in_specs=[vmem()] * 6,
         out_specs=vmem(),
         scratch_shapes=[
             pltpu.VMEM((frames, 2, 128, 2 * ROWS), BF16),
@@ -683,7 +699,7 @@
         compiler_params=PARAMS,
         cost_estimate=work,
         name="columns",
-    )(feat, low, high, own, water)
+    )(feat, low, high, own, water, atoms)
 
     send = pl.pallas_call(
         facing_kernel,

time: 37.1 us -> 37.3 us (level)
    pallas_call x1, Pallas kernels: 2.03 us -> 3.2 us  [shards(): pl.pallas_call(inner_kernel, out_shape=(column_shape, jax.ShapeDtypeStruc...]
    pallas_call x1, Pallas kernels: 4.48 us -> 3.38 us  [shards(): pl.pallas_call(column_kernel, out_shape=jax.ShapeDtypeStruct((frames, 2,...]
where the time goes in v7:
time: 37.3 us; the launch traced here: 37.1 us
  blocking collectives  18.6 us (50%)
  Pallas kernels  10.9 us (29%)
  starting transfers between devices  6.58 us (18%)
  other arithmetic  0.89 us (2%)
    all_to_all x1, blocking collectives, shards(): got = lax.all_to_all(send, 'fr', 0, 0, tiled=True)  18.6 us
    pallas_call x1, Pallas kernels, shards(): pl.pallas_call(column_kernel, out_shape=jax.ShapeDtypeStruct((frames, 2,...  3.38 us
    pallas_call x1, Pallas kernels, shards(): pl.pallas_call(inner_kernel, out_shape=(column_shape, jax.ShapeDtypeStruc...  3.2 us
    ppermute x1, starting transfers between devices, shards(): lax.ppermute(jnp.concatenate([side_out, *beyond], axis=0), 'py', [(0, 1),...  3.1 us
    pallas_call x1, Pallas kernels, shards(): pl.pallas_call(facing_kernel, out_shape=jax.ShapeDtypeStruct((ranks, 4, 1...  2.19 us
    ppermute x1, starting transfers between devices, shards(): low = lax.ppermute(feat[2:4], 'px', up)  2.12 us
    ppermute x1, starting transfers between devices, shards(): high = lax.ppermute(feat[0:2], 'px', down)  1.36 us
    pallas_call x1, Pallas kernels, shards(): pl.pallas_call(functools.partial(bin_kernel, frames * ranks), out_shape=j...  1.3 us
  transfers between devices with their start and end apart: 3, of which 0 were waited for; matrix products, arithmetic and copies ran while one was open for 0% of the time, Pallas kernels for 18%

profile of v7, /device:TPU:1, one launch (start us, length us, event | category | flops | bytes accessed | tf_op | source)
XLA Modules:
  0.0 37.1 jit_solution(18287730399073155553)
XLA Ops:
  0.0 0.9 %convert_add_fusion.packed_ref = f32[69,2,128]{2,1,0:T(2,128)S(1)} fusion(s32[2,2,4]{2,1,0:T(2,128)} %bitcast.18, s32[2,2,128]{2,1,0:T(2,128)} %param.14, s32[8,2,128]{2,1,0:T(2,128)} %bitcast.16, f32[1,1,32]{2,1,0:T(1,128)} %bitcast.19, f32[1,1,32]{2,1,0:T(1,128)} %bitcast.20, f32[1,1,32]{2,1,0:T(1,128)} %bitcast.21, f32[6,2,128]{2,1,0:T(2,128)} %bitcast.17, ...), kind=kLoop, calls=%fused_computation.1 | loop fusion | flops 158976 | bytes 136640 | tf_op jit(solution)/shard_map/add | solution.py:636
  0.9 0.8 %prepare.1 = (f32[4,5,8,128]{3,2,1,0:T(8,128)S(1)}, f32[2,5,8,128]{3,2,1,0:T(8,128)S(1)}, f32[16,8,128]{2,1,0:T(8,128)S(1)}) custom-call(f32[69,2,128]{2,1,0:T(2,128)S(1)} %convert_add_fusion.packed_ref), custom_call_target="tpu_custom_call" | custom-call | tf_op jit(solution)/shard_map/prepare/pallas_call | solution.py:637
  1.7 2.1 %collective-permute-start = (f32[2,5,8,128]{3,2,1,0:T(8,128)S(1)}, f32[2,5,8,128]{3,2,1,0:T(8,128)S(1)}, u32[]{:S(2)}, u32[]{:S(2)}) collective-permute-start(f32[2,5,8,128]{3,2,1,0:T(8,128)S(1)} %get-tuple-element.26), channel_id=1, source_target_pairs={{0,64},{64,128},{128,192},{192,0},{1,65},{65,129},{129,193},{193,1... | collective-permute-start | bytes 122888 | tf_op jit(solution)/shard_map/ppermute | solution.py:657
  3.8 1.4 %collective-permute-start.1 = (f32[2,5,8,128]{3,2,1,0:T(8,128)S(1)}, f32[2,5,8,128]{3,2,1,0:T(8,128)S(1)}, u32[]{:S(2)}, u32[]{:S(2)}) collective-permute-start(f32[2,5,8,128]{3,2,1,0:T(8,128)S(1)} %get-tuple-element.25), channel_id=1, source_target_pairs={{0,192},{64,0},{128,64},{192,128},{1,193},{65,1},{129,65},{193,129... | collective-permute-start | bytes 122888 | tf_op jit(solution)/shard_map/ppermute | solution.py:658
  5.2 3.2 %inner.1 = (f32[4,2,8,256]{3,2,1,0:T(8,128)S(1)}, f32[4,2,8,128]{3,2,1,0:T(8,128)S(1)}, bf16[4,2,320,256]{3,2,1,0:T(8,128)(2,1)S(1)}, f32[4,8,256]{2,1,0:T(8,128)S(1)}) custom-call(f32[4,5,8,128]{3,2,1,0:T(8,128)S(1)} %get-tuple-element.15.feat_ref), custom_call_target="tpu_custom_call" | custom-call | flops 1000000000 | bytes 1000000 | tf_op jit(solution)/shard_map/inner/pallas_call | solution.py:662
  8.4 0.0 collective-permute-done.low_ref
  8.4 0.0 collective-permute-done.1.high_ref
  8.5 3.1 %collective-permute-start.2 = (f32[4,5,8,128]{3,2,1,0:T(8,128)S(1)}, f32[4,5,8,128]{3,2,1,0:T(8,128)S(1)}, u32[]{:S(2)}, u32[]{:S(2)}) collective-permute-start(f32[4,5,8,128]{3,2,1,0:T(8,128)S(1)} %pad_maximum_fusion), channel_id=1, source_target_pairs={{0,32},{32,0},{1,33},{33,1},{2,34},{34,2},{3,35},{35,3},{4,36},{36... | collective-permute-start | bytes 245768 | tf_op jit(solution)/shard_map/ppermute | solution.py:687
  11.6 3.4 %columns.1.acc_ref = f32[4,2,2,8,256]{4,3,2,1,0:T(8,128)S(1)} custom-call(f32[4,5,8,128]{3,2,1,0:T(8,128)S(1)} %get-tuple-element.15.feat_ref, f32[2,5,8,128]{3,2,1,0:T(8,128)S(1)} %collective-permute-done.low_ref, f32[2,5,8,128]{3,2,1,0:T(8,128)S(1)} %collective-permute-done.1.high_ref, bf16[4,2,320,256]{3,2,1,0:T(8,128)(2,1)S(1)} %get-tuple-element.20.own_ref, ...), custom_call_target="tpu_custom_call" | custom-call | flops 1000000000 | bytes 1000000 | tf_op jit(solution)/shard_map/columns/pallas_call | solution.py:688
  14.9 0.0 collective-permute-done.2.side_ref
  15.0 2.2 %facing.1 = f32[32,4,128]{2,1,0:T(4,128)S(1)} custom-call(f32[4,5,8,128]{3,2,1,0:T(8,128)S(1)} %get-tuple-element.15.feat_ref, f32[4,5,8,128]{3,2,1,0:T(8,128)S(1)} %collective-permute-done.2.side_ref, f32[4,2,2,8,256]{4,3,2,1,0:T(8,128)S(1)} %columns.1.acc_ref, f32[4,2,8,128]{3,2,1,0:T(8,128)S(1)} %get-tuple-element.23.other_ref, ...), custom_call_target="tpu_custom_call" | custom-call | tf_op jit(solution)/shard_map/facing/pallas_call | solution.py:704
  17.2 18.6 %all_to_all.5.got_ref = f32[32,4,128]{2,1,0:T(4,128)S(1)} all-to-all(f32[32,4,128]{2,1,0:T(4,128)S(1)} %facing.1), channel_id=1, replica_groups=mesh['px'=4,'py'=2,'fr'=32] {'fr'}, dimensions={0} | all-to-all | bytes 131072 | tf_op jit(solution)/shard_map/all_to_all | solution.py:722
  35.8 1.3 %bin.1 = f32[13,2,2,720]{3,2,1,0:T(2,128)} custom-call(f32[32,4,128]{2,1,0:T(4,128)S(1)} %all_to_all.5.got_ref), custom_call_target="tpu_custom_call" | custom-call | tf_op jit(solution)/shard_map/bin/pallas_call | solution.py:724
  (3 shorter events, 0.0 us)
Async XLA Ops:
  1.7 6.7 %collective-permute-start = (f32[2,5,8,128]{3,2,1,0:T(8,128)S(1)}, f32[2,5,8,128]{3,2,1,0:T(8,128)S(1)}, u32[]{:S(2)}, u32[]{:S(2)}) collective-permute-start(f32[2,5,8,128]{3,2,1,0:T(8,128)S(1)} %get-tuple-element.26), channel_id=1, source_target_pairs={{0,64},{64,128},{128,192},{192,0},{1,65},{65,129},{129,193},{193,1... | collective-permute-start | bytes 122888 | tf_op jit(solution)/shard_map/ppermute | solution.py:657
  3.8 4.6 %collective-permute-start.1 = (f32[2,5,8,128]{3,2,1,0:T(8,128)S(1)}, f32[2,5,8,128]{3,2,1,0:T(8,128)S(1)}, u32[]{:S(2)}, u32[]{:S(2)}) collective-permute-start(f32[2,5,8,128]{3,2,1,0:T(8,128)S(1)} %get-tuple-element.25), channel_id=1, source_target_pairs={{0,192},{64,0},{128,64},{192,128},{1,193},{65,1},{129,65},{193,129... | collective-permute-start | bytes 122888 | tf_op jit(solution)/shard_map/ppermute | solution.py:658
  8.5 6.5 %collective-permute-start.2 = (f32[4,5,8,128]{3,2,1,0:T(8,128)S(1)}, f32[4,5,8,128]{3,2,1,0:T(8,128)S(1)}, u32[]{:S(2)}, u32[]{:S(2)}) collective-permute-start(f32[4,5,8,128]{3,2,1,0:T(8,128)S(1)} %pad_maximum_fusion), channel_id=1, source_target_pairs={{0,32},{32,0},{1,33},{33,1},{2,34},{34,2},{3,35},{35,3},{4,36},{36... | collective-permute-start | bytes 245768 | tf_op jit(solution)/shard_map/ppermute | solution.py:687
